TPU v7x, 32 devices: a whole 2x2x4 slice. The times are simulated.
32 devices in a mesh: dp: 8 (over z, y), tensor: 4 (over x, core).
Axes of the slice: x: 2, y: 2, z: 4, core: 2. Of those that a mesh axis runs over, the one named last changes fastest.
Arguments:
- clean_latents: bfloat16 [64, 256, 16], P('dp'), may hold values from -6 to 6
- noise_draw: bfloat16 [64, 256, 16], P('dp'), may hold values from -6 to 6
- timesteps: float32 [64], P('dp'), may hold values from 0 to 1, as said below
- labels: int32 [64], P('dp'), may hold values from 0 to 31
- col_weights: float32 [768, 4, 2880], P('dp', 'tensor'), may hold values from -0.21875 to 0.21875
- col_moments: float32 [768, 4, 2880], P('dp', 'tensor'), may hold values from -0.015625 to 0.015625
- col_errors: float32 [8, 4, 768, 2880], P('dp', 'tensor'), may hold values from -0.00030517578 to 0.00030517578
- row_weights: float32 [4, 960, 768], P('tensor', None, 'dp'), may hold values from -0.21875 to 0.21875
- row_moments: float32 [4, 960, 768], P('tensor', None, 'dp'), may hold values from -0.015625 to 0.015625
- row_errors: float32 [8, 4, 960, 768], P('dp', 'tensor'), may hold values from -0.00030517578 to 0.00030517578
- bias_weights: float32 [4, 2880], P('tensor'), may hold values from -4 to 4
- bias_moments: float32 [4, 2880], P('tensor'), may hold values from -0.046875 to 0.046875
- small_weights: float32 [1093, 768], P(None, 'dp'), may hold values from -4 to 4
- small_moments: float32 [1093, 768], P(None, 'dp'), may hold values from -0.046875 to 0.046875
- head_bias: float32 [16], replicated, may hold values from -6 to 6
- head_moments: float32 [16], replicated, may hold values from -0.00030517578 to 0.00030517578
- right_factors: float32 [4, 8, 4416], P('tensor'), may hold values from -6 to 6
Outputs:
- loss_value: float32 [], replicated
- col_new: float32 [768, 4, 2880], P('dp', 'tensor')
- col_momentum: float32 [768, 4, 2880], P('dp', 'tensor')
- col_residue: float32 [8, 4, 768, 2880], P('dp', 'tensor')
- row_new: float32 [4, 960, 768], P('tensor', None, 'dp')
- row_momentum: float32 [4, 960, 768], P('tensor', None, 'dp')
- row_residue: float32 [8, 4, 960, 768], P('dp', 'tensor')
- bias_new: float32 [4, 2880], P('tensor')
- bias_momentum: float32 [4, 2880], P('tensor')
- small_new: float32 [1093, 768], P(None, 'dp')
- small_momentum: float32 [1093, 768], P(None, 'dp')
- head_new: float32 [16], replicated
- head_momentum: float32 [16], replicated
- left_factors: float32 [4, 8, 3264], P('tensor')
- right_new: float32 [4, 8, 4416], P('tensor')
Inputs may be any that keep to these rules, and one draw needn't show every extreme that they name: `timesteps`: each is (k + 0.5) / 1000 for a whole number k.
All inputs are finite; a program needn't handle non-finite values.
Results may differ from a plain program's by a relative error of at most 0.012.
The roundings to bfloat16 on the way count: a program that leaves them out, or rounds other values in their place, can miss the bound.
Values may be sent and summed in bfloat16 or wider, within the bound.
A program may use at most 256 MiB of HBM per device.

v0:
```python
import math

import jax
import jax.numpy as jnp
from jax import lax
from jax.sharding import PartitionSpec as P

D = 768
HEADS = 12
HEAD_DIM = 64
FF = 3072
FREQ = 256
GRID = 16
PATCH_IN = 16
CLASSES = 32


EPSILON = 1e-06
TINY = 1e-30
DECAY = 0.9
LEARN_RATE = 100.0
TIME_OFFSET = 0.25


def exact_dot(left, right):
    return jnp.dot(left, right, precision=lax.Precision.HIGHEST, preferred_element_type=jnp.float32)


def exact_tdot(left, right):
    return lax.dot_general(
        left,
        right,
        (((0,), (0,)), ((), ())),
        precision=lax.Precision.HIGHEST,
        preferred_element_type=jnp.float32,
    )


def exact_ndot(left, right):
    return lax.dot_general(
        left,
        right,
        (((1,), (1,)), ((), ())),
        precision=lax.Precision.HIGHEST,
        preferred_element_type=jnp.float32,
    )


def fast_dot(left, right):
    return jnp.dot(left, right, preferred_element_type=jnp.float32)


def fast_tdot(left, right):
    return lax.dot_general(
        left, right, (((0,), (0,)), ((), ())), preferred_element_type=jnp.float32
    )


def fast_ndot(left, right):
    return lax.dot_general(
        left, right, (((1,), (1,)), ((), ())), preferred_element_type=jnp.float32
    )


def layer_norm(hidden):
    center = hidden - jnp.mean(hidden, axis=-1, keepdims=True)
    spread = jnp.mean(center * center, axis=-1, keepdims=True)
    return center * lax.rsqrt(spread + EPSILON)


def modulate(hidden, shift_rows, scale_rows):
    return layer_norm(hidden) * (1.0 + scale_rows) + shift_rows


def gelu_tanh(values):
    return jax.nn.gelu(values, approximate=True)


def position_rows(token_ids):
    quarter = D // 4
    omega = 1.0 / 10000.0 ** (jnp.arange(quarter, dtype=jnp.float32) / quarter)
    row_pos = (token_ids // GRID).astype(jnp.float32)[:, None] * omega[None, :]
    col_pos = (token_ids % GRID).astype(jnp.float32)[:, None] * omega[None, :]
    return jnp.concatenate(
        [jnp.sin(row_pos), jnp.cos(row_pos), jnp.sin(col_pos), jnp.cos(col_pos)], axis=1
    )


def time_features(times):
    half = FREQ // 2
    freqs = jnp.exp(-math.log(10000.0) * jnp.arange(half, dtype=jnp.float32) / half)
    angles = 1000.0 * times[:, None] * freqs[None, :]
    return jnp.concatenate([jnp.cos(angles), jnp.sin(angles)], axis=1)


def small_starts():
    counts = [PATCH_IN, 1, FREQ, 1, D, 1, CLASSES, PATCH_IN, 1, 1]
    starts = [0]
    for amount in counts:
        starts.append(starts[-1] + amount)
    return starts


def cut_parts(array, widths, axis):
    pieces = []
    offset = 0
    for width in widths:
        pieces.append(lax.slice_in_dim(array, offset, offset + width, axis=axis))
        offset = offset + width
    return pieces


def orthonormal(block):
    basis = []
    for index in range(block.shape[0]):
        vector = block[index]
        for earlier in basis:
            vector = vector - jnp.sum(vector * earlier) * earlier
        vector = vector * lax.rsqrt(jnp.sum(vector * vector) + TINY)
        basis.append(vector)
    return jnp.stack(basis)


def shards(
    clean_latents,
    noise_draw,
    timesteps,
    labels,
    col_weights,
    col_moments,
    col_errors,
    row_weights,
    row_moments,
    row_errors,
    bias_weights,
    bias_moments,
    small_weights,
    small_moments,
    head_bias,
    head_moments,
    right_factors,
):
    tensor_size = lax.axis_size("tensor")
    data_size = lax.axis_size("dp")
    tensor_rank = lax.axis_index("tensor")
    data_rank = lax.axis_index("dp")
    batch = clean_latents.shape[0]
    seq_len = clean_latents.shape[1]
    total_rows = batch * seq_len
    shard_rows = total_rows // tensor_size
    mod_width = 8 * D // tensor_size
    qkv_width = 3 * D // tensor_size
    ffn_width = FF // tensor_size
    proj_rows = D // tensor_size
    heads_local = HEADS // tensor_size
    count_all = data_size * total_rows * PATCH_IN
    col_widths = [mod_width, qkv_width, ffn_width]
    row_widths = [proj_rows, ffn_width]
    scale_factor = 1.0 / math.sqrt(HEAD_DIM)
    col_full, row_full, small_full = (
        lax.all_gather(col_weights.astype(jnp.bfloat16), "dp", axis=0, tiled=True),
        lax.all_gather(row_weights.astype(jnp.bfloat16), "dp", axis=2, tiled=True),
        lax.all_gather(small_weights.astype(jnp.bfloat16), "dp", axis=1, tiled=True),
    )
    col_full = col_full[:, 0, :]
    row_full = row_full[0]
    w_mod, w_qkv, w_fc1 = cut_parts(col_full, col_widths, 1)
    w_proj, w_fc2 = cut_parts(row_full, row_widths, 0)
    small_exact = small_full.astype(jnp.float32)
    starts = small_starts()
    w_patch = small_full[starts[0] : starts[1]]
    b_patch = small_exact[starts[1]]
    w_time_in = small_exact[starts[2] : starts[3]]
    b_time_in = small_exact[starts[3]]
    w_time_out = small_exact[starts[4] : starts[5]]
    b_time_out = small_exact[starts[5]]
    table = small_exact[starts[6] : starts[7]]
    w_head = small_full[starts[7] : starts[8]]
    b_proj = small_exact[starts[8]]
    b_fc2 = small_exact[starts[9]]
    bias_exact = lax.optimization_barrier(bias_weights[0].astype(jnp.bfloat16)).astype(jnp.float32)
    b_mod, b_qkv, b_fc1 = cut_parts(bias_exact, col_widths, 0)
    head_exact = lax.optimization_barrier(head_bias.astype(jnp.bfloat16)).astype(jnp.float32)
    time_feat = time_features(timesteps)
    time_hidden = exact_dot(time_feat, w_time_in) + b_time_in
    time_act = jax.nn.silu(time_hidden)
    onehot = (labels[:, None] == jnp.arange(CLASSES, dtype=jnp.int32)[None, :]).astype(jnp.float32)
    condition = exact_dot(time_act, w_time_out) + b_time_out + exact_dot(onehot, table)
    cond_act = jax.nn.silu(condition)
    w_mod_exact = w_mod.astype(jnp.float32)
    local_mod = exact_dot(cond_act, w_mod_exact) + b_mod
    full_mod = lax.all_gather(local_mod, "tensor", axis=1, tiled=True)
    row_ids = tensor_rank * shard_rows + jnp.arange(shard_rows, dtype=jnp.int32)
    select = (row_ids[:, None] // seq_len == jnp.arange(batch, dtype=jnp.int32)[None, :]).astype(
        jnp.float32
    )
    mod_rows = exact_dot(select, full_mod)

    def span(which):
        return mod_rows[:, which * D : (which + 1) * D]

    time_rows = exact_dot(select, timesteps[:, None])[:, 0]
    clean_rows = lax.dynamic_slice_in_dim(
        clean_latents.reshape(total_rows, PATCH_IN), tensor_rank * shard_rows, shard_rows, 0
    ).astype(jnp.float32)
    noise_rows = lax.dynamic_slice_in_dim(
        noise_draw.reshape(total_rows, PATCH_IN), tensor_rank * shard_rows, shard_rows, 0
    ).astype(jnp.float32)
    mixed = time_rows[:, None] * clean_rows + (1.0 - time_rows)[:, None] * noise_rows
    target = clean_rows - noise_rows
    mixed_low = mixed.astype(jnp.bfloat16)
    hidden0 = fast_dot(mixed_low, w_patch) + b_patch + position_rows(row_ids % seq_len)

    def spread(local_rows, weight):
        whole = lax.all_gather(local_rows, "tensor", axis=0, tiled=True)
        result = fast_dot(whole, weight)
        return (result, whole)

    def weight_grad(whole, grads_low):
        result = fast_tdot(whole, grads_low)
        return result

    def branch_sum(inputs_low, weight):
        return lax.psum_scatter(
            fast_dot(inputs_low, weight), "tensor", scatter_dimension=0, tiled=True
        )

    def input_grad(grads_low, weight):
        return lax.psum_scatter(
            fast_ndot(grads_low, weight), "tensor", scatter_dimension=0, tiled=True
        )

    def spread_grad(rows_low):
        return lax.all_gather(rows_low, "tensor", axis=0, tiled=True)

    attn_in = modulate(hidden0, span(0), span(1)).astype(jnp.bfloat16)
    qkv_raw, attn_whole = spread(attn_in, w_qkv)
    qkv_low = (
        (qkv_raw + b_qkv).astype(jnp.bfloat16).reshape(batch, seq_len, heads_local, 3, HEAD_DIM)
    )
    query = qkv_low[:, :, :, 0]
    keys = qkv_low[:, :, :, 1]
    values = qkv_low[:, :, :, 2]
    scores = (
        jnp.einsum("bqhd,bkhd->bhqk", query, keys, preferred_element_type=jnp.float32)
        * scale_factor
    )
    log_total = jax.nn.logsumexp(scores, axis=-1, keepdims=True)
    probs_low = jnp.exp(scores - log_total).astype(jnp.bfloat16)
    attended = jnp.einsum("bhqk,bkhd->bqhd", probs_low, values, preferred_element_type=jnp.float32)
    attended_low = attended.astype(jnp.bfloat16).reshape(total_rows, heads_local * HEAD_DIM)
    attn_out = branch_sum(attended_low, w_proj) + b_proj
    gate_one = span(2)
    hidden1 = hidden0 + gate_one * attn_out
    mlp_in = modulate(hidden1, span(3), span(4)).astype(jnp.bfloat16)
    fc1_raw, mlp_whole = spread(mlp_in, w_fc1)
    pre_act = fc1_raw + b_fc1
    mlp_act = gelu_tanh(pre_act).astype(jnp.bfloat16)
    mlp_out = branch_sum(mlp_act, w_fc2) + b_fc2
    gate_two = span(5)
    hidden2 = hidden1 + gate_two * mlp_out
    final_in = modulate(hidden2, span(6), span(7)).astype(jnp.bfloat16)
    predicted = fast_ndot(final_in, w_head) + head_exact
    weighting = 1.0 / (1.0 - time_rows + TIME_OFFSET)
    diff = predicted - target
    loss_part = jnp.sum(weighting[:, None] * diff * diff) / count_all
    d_pred = 2.0 * weighting[:, None] * diff / count_all
    g_bhead = jnp.sum(d_pred, axis=0)
    d_pred_low = d_pred.astype(jnp.bfloat16)
    g_head = fast_tdot(d_pred_low, final_in)
    d_final = fast_dot(d_pred_low, w_head)
    _, final_pull = jax.vjp(modulate, hidden2, span(6), span(7))
    d_hidden2, d_shift_f, d_scale_f = final_pull(d_final)
    d_gate_two = d_hidden2 * mlp_out
    g_bfc2 = jnp.sum(d_hidden2 * gate_two, axis=0)
    d_mlp_full = spread_grad((d_hidden2 * gate_two).astype(jnp.bfloat16))
    g_fc2 = fast_tdot(mlp_act, d_mlp_full)
    d_act = fast_ndot(d_mlp_full, w_fc2)
    _, gelu_pull = jax.vjp(gelu_tanh, pre_act)
    d_pre = gelu_pull(d_act)[0]
    g_bfc1 = jnp.sum(d_pre, axis=0)
    d_pre_low = d_pre.astype(jnp.bfloat16)
    g_fc1 = weight_grad(mlp_whole, d_pre_low)
    d_mlp_in = input_grad(d_pre_low, w_fc1)
    _, mlp_pull = jax.vjp(modulate, hidden1, span(3), span(4))
    d_hidden1_norm, d_shift_two, d_scale_two = mlp_pull(d_mlp_in)
    d_hidden1 = d_hidden2 + d_hidden1_norm
    d_gate_one = d_hidden1 * attn_out
    g_bproj = jnp.sum(d_hidden1 * gate_one, axis=0)
    d_attn_full = spread_grad((d_hidden1 * gate_one).astype(jnp.bfloat16))
    g_proj = fast_tdot(attended_low, d_attn_full)
    d_attended = (
        fast_ndot(d_attn_full, w_proj)
        .astype(jnp.bfloat16)
        .reshape(batch, seq_len, heads_local, HEAD_DIM)
    )
    scores_again = (
        jnp.einsum("bqhd,bkhd->bhqk", query, keys, preferred_element_type=jnp.float32)
        * scale_factor
    )
    probs_again = jnp.exp(scores_again - log_total)
    probs_again_low = probs_again.astype(jnp.bfloat16)
    d_values = jnp.einsum(
        "bhqk,bqhd->bkhd", probs_again_low, d_attended, preferred_element_type=jnp.float32
    )
    d_probs = jnp.einsum("bqhd,bkhd->bhqk", d_attended, values, preferred_element_type=jnp.float32)
    d_scores = probs_again * (d_probs - jnp.sum(probs_again * d_probs, axis=-1, keepdims=True))
    d_scores_low = d_scores.astype(jnp.bfloat16)
    d_query = (
        jnp.einsum("bhqk,bkhd->bqhd", d_scores_low, keys, preferred_element_type=jnp.float32)
        * scale_factor
    )
    d_keys = (
        jnp.einsum("bhqk,bqhd->bkhd", d_scores_low, query, preferred_element_type=jnp.float32)
        * scale_factor
    )
    d_qkv = jnp.stack([d_query, d_keys, d_values], axis=3).reshape(total_rows, qkv_width)
    g_bqkv = jnp.sum(d_qkv, axis=0)
    d_qkv_low = d_qkv.astype(jnp.bfloat16)
    g_qkv = weight_grad(attn_whole, d_qkv_low)
    d_attn_in = input_grad(d_qkv_low, w_qkv)
    _, attn_pull = jax.vjp(modulate, hidden0, span(0), span(1))
    d_hidden0_norm, d_shift_one, d_scale_one = attn_pull(d_attn_in)
    d_hidden0 = d_hidden1 + d_hidden0_norm
    g_bpatch = jnp.sum(d_hidden0, axis=0)
    g_patch = fast_tdot(mixed_low, d_hidden0.astype(jnp.bfloat16))
    rows_grad = jnp.concatenate(
        [
            d_shift_one,
            d_scale_one,
            d_gate_one,
            d_shift_two,
            d_scale_two,
            d_gate_two,
            d_shift_f,
            d_scale_f,
        ],
        axis=1,
    )
    latent_grad = exact_tdot(select, rows_grad)
    d_mod = lax.psum_scatter(latent_grad, "tensor", scatter_dimension=1, tiled=True)
    g_bmod = jnp.sum(d_mod, axis=0)
    g_mod = exact_tdot(cond_act, d_mod)
    d_cond_act = exact_ndot(d_mod, w_mod_exact)
    _, silu_pull = jax.vjp(jax.nn.silu, condition)
    d_condition = silu_pull(d_cond_act)[0]
    g_table = exact_tdot(onehot, d_condition)
    g_btout = jnp.sum(d_condition, axis=0)
    g_tout = exact_tdot(time_act, d_condition)
    d_time_act = exact_ndot(d_condition, w_time_out)
    _, time_pull = jax.vjp(jax.nn.silu, time_hidden)
    d_time_hidden = time_pull(d_time_act)[0]
    g_btin = jnp.sum(d_time_hidden, axis=0)
    g_tin = exact_tdot(time_feat, d_time_hidden)
    small_grad = jnp.concatenate(
        [
            g_patch,
            g_bpatch[None],
            g_tin,
            g_btin[None],
            g_tout,
            g_btout[None],
            g_table,
            g_head,
            g_bproj[None],
            g_bfc2[None],
        ],
        axis=0,
    )
    bias_grad = jnp.concatenate([g_bmod, g_bqkv, g_bfc1], axis=0)
    col_total = jnp.concatenate([g_mod, g_qkv, g_fc1], axis=1) + col_errors[0, 0]
    row_total = jnp.concatenate([g_proj, g_fc2], axis=0) + row_errors[0, 0]
    matrices = cut_parts(col_total, col_widths, 1) + cut_parts(row_total, row_widths, 0)
    right_pieces = cut_parts(right_factors[0], col_widths + [D, D], 1)
    left_pieces = []
    for index in range(5):
        left_pieces.append(exact_ndot(right_pieces[index], matrices[index]))
    left_local = jnp.concatenate(left_pieces, axis=1)
    share = D // data_size
    left_sum, bias_sum = lax.psum((left_local, bias_grad), "dp")
    small_sum, head_sum, loss_value = lax.psum((small_grad, g_bhead, loss_part), ("dp", "tensor"))
    small_step = lax.dynamic_slice_in_dim(small_sum, data_rank * share, share, 1)
    bases = [orthonormal(part) for part in cut_parts(left_sum, [D, D, D, proj_rows, ffn_width], 1)]
    right_local = jnp.concatenate(
        [exact_dot(bases[index], matrices[index]) for index in range(5)], axis=1
    )
    right_sum = lax.psum(right_local, "dp")
    right_split = cut_parts(right_sum, col_widths + [D, D], 1)
    approx = [exact_tdot(bases[index], right_split[index]) for index in range(5)]
    col_hat = jnp.concatenate(approx[:3], axis=1)
    row_hat = jnp.concatenate(approx[3:], axis=0)
    col_step = lax.dynamic_slice_in_dim(col_hat, data_rank * share, share, 0)[:, None, :]
    col_momentum = DECAY * col_moments + col_step
    col_new = col_weights - LEARN_RATE * col_momentum
    row_step = lax.dynamic_slice_in_dim(row_hat, data_rank * share, share, 1)[None]
    row_momentum = DECAY * row_moments + row_step
    row_new = row_weights - LEARN_RATE * row_momentum
    small_momentum = DECAY * small_moments + small_step
    small_new = small_weights - LEARN_RATE * small_momentum
    bias_momentum = DECAY * bias_moments + bias_sum[None]
    bias_new = bias_weights - LEARN_RATE * bias_momentum
    head_momentum = DECAY * head_moments + head_sum
    head_new = head_bias - LEARN_RATE * head_momentum
    col_residue = (col_total - col_hat / data_size)[None, None]
    row_residue = (row_total - row_hat / data_size)[None, None]
    left_factors = jnp.concatenate(bases, axis=1)[None]
    right_new = right_sum[None]
    return (
        loss_value,
        col_new,
        col_momentum,
        col_residue,
        row_new,
        row_momentum,
        row_residue,
        bias_new,
        bias_momentum,
        small_new,
        small_momentum,
        head_new,
        head_momentum,
        left_factors,
        right_new,
    )


def solution(mesh):
    placed = (
        P("dp", None, None),
        P("dp", None, None),
        P("dp"),
        P("dp"),
        P("dp", "tensor", None),
        P("dp", "tensor", None),
        P("dp", "tensor", None, None),
        P("tensor", None, "dp"),
        P("tensor", None, "dp"),
        P("dp", "tensor", None, None),
        P("tensor", None),
        P("tensor", None),
        P(None, "dp"),
        P(None, "dp"),
        P(),
        P(),
        P("tensor", None, None),
    )
    return jax.shard_map(
        shards,
        mesh=mesh,
        in_specs=placed,
        out_specs=(
            P(),
            P("dp", "tensor", None),
            P("dp", "tensor", None),
            P("dp", "tensor", None, None),
            P("tensor", None, "dp"),
            P("tensor", None, "dp"),
            P("dp", "tensor", None, None),
            P("tensor", None),
            P("tensor", None),
            P(None, "dp"),
            P(None, "dp"),
            P(),
            P(),
            P("tensor", None, None),
            P("tensor", None, None),
        ),
        check_vma=False,
    )
```

profile of v0, /device:TPU:0, one launch (start us, length us, event | category | flops | bytes accessed | tf_op | source)
XLA Modules:
  0.0 1408.2 jit_solution(12662267180313542215)
XLA Ops:
  16.7 42.8 %all-gather.8.cloned.1.call-done = bf16[1093,768]{0,1:T(8,128)(2,1)} async-done(((bf16[1093,96]{0,1:T(8,128)(2,1)}), bf16[1093,768]{0,1:T(8,128)(2,1)}) %all-gather.8.cloned.1.call-update) | async-done | bytes 1678864 | tf_op jit(solution)/shard_map/all_gather | solution.py:163
  65.5 73.3 %all-gather.10.cloned.1.call-done = bf16[768,1,2880]{2,0,1:T(8,128)(2,1)} async-done(((bf16[96,1,2880]{2,0,1:T(8,128)(2,1)}), bf16[768,1,2880]{2,0,1:T(8,128)(2,1)}) %all-gather.10.cloned.1.call-update) | async-done | bytes 4423696 | tf_op jit(solution)/shard_map/all_gather | solution.py:161
  166.7 25.8 %all-gather.12.cloned.1.call-done = bf16[2048,768]{1,0:T(8,128)(2,1)} async-done(((bf16[512,768]{1,0:T(8,128)(2,1)}), bf16[2048,768]{1,0:T(8,128)(2,1)}) %all-gather.12.cloned.1.call-update) | async-done | bytes 3145744 | tf_op jit(solution)/shard_map/all_gather | solution.py:215
  203.3 36.1 %all-gather.14.cloned.1.call-done = bf16[1,960,768]{1,2,0:T(8,128)(2,1)} async-done(((bf16[1,960,96]{1,2,0:T(8,128)(2,1)}), bf16[1,960,768]{1,2,0:T(8,128)(2,1)}) %all-gather.14.cloned.1.call-update) | async-done | bytes 1474576 | tf_op jit(solution)/shard_map/all_gather | solution.py:162
  244.2 57.3 %reduce-scatter.6.cloned.1.call-done = f32[512,768]{1,0:T(8,128)} async-done(((f32[2048,768]{1,0:T(8,128)}), f32[512,768]{1,0:T(8,128)}) %reduce-scatter.6.cloned.1.call-update) | async-done | bytes 1572880 | tf_op jit(solution)/shard_map/reduce_scatter | solution.py:224
  307.6 28.2 %all-gather.16.cloned.1.call-done = bf16[2048,768]{1,0:T(8,128)(2,1)} async-done(((bf16[512,768]{1,0:T(8,128)(2,1)}), bf16[2048,768]{1,0:T(8,128)(2,1)}) %all-gather.16.cloned.1.call-update) | async-done | bytes 3145744 | tf_op jit(solution)/shard_map/all_gather | solution.py:215
  350.4 57.9 %reduce-scatter.8.cloned.1.call-done = f32[512,768]{1,0:T(8,128)} async-done(((f32[2048,768]{1,0:T(8,128)}), f32[512,768]{1,0:T(8,128)}) %reduce-scatter.8.cloned.1.call-update) | async-done | bytes 1572880 | tf_op jit(solution)/shard_map/reduce_scatter | solution.py:224
  423.9 28.6 %all-gather.18.cloned.1.call-done = bf16[2048,768]{1,0:T(8,128)(2,1)} async-done(((bf16[512,768]{1,0:T(8,128)(2,1)}), bf16[2048,768]{1,0:T(8,128)(2,1)}) %all-gather.18.cloned.1.call-update) | async-done | bytes 3145744 | tf_op jit(solution)/shard_map/all_gather | solution.py:234
  469.6 58.5 %reduce-scatter.10.cloned.1.call-done = f32[512,768]{1,0:T(8,128)} async-done(((f32[2048,768]{1,0:T(8,128)}), f32[512,768]{1,0:T(8,128)}) %reduce-scatter.10.cloned.1.call-update) | async-done | bytes 1572880 | tf_op jit(solution)/shard_map/reduce_scatter | solution.py:229
  536.1 28.5 %all-gather.20.cloned.1.call-done = bf16[2048,768]{1,0:T(8,128)(2,1)} async-done(((bf16[512,768]{1,0:T(8,128)(2,1)}), bf16[2048,768]{1,0:T(8,128)(2,1)}) %all-gather.20.cloned.1.call-update) | async-done | bytes 3145744 | tf_op jit(solution)/shard_map/all_gather | solution.py:234
  608.9 40.8 %all-reduce = (f32[]{:T(128)}, f32[16]{0:T(128)S(1)}) all-reduce(f32[]{:T(128)S(6)} %div.158, f32[16]{0:T(128)S(1)} %get-tuple-element.115), channel_id=1, replica_groups=mesh['dp'=8,'tensor'=4] {'dp','tensor'}, use_global_device_ids=true, to_apply=%region_11.12 | all-reduce | flops 17 | bytes 136 | tf_op jit(solution)/shard_map/psum | solution.py:381
  700.4 15.6 %reduce-scatter.14.cloned.1.call-done = f32[8,1536]{1,0:T(8,128)} async-done(((f32[8,6144]{1,0:T(8,128)}), f32[8,1536]{1,0:T(8,128)}) %reduce-scatter.14.cloned.1.call-update) | async-done | bytes 49168 | tf_op jit(solution)/shard_map/reduce_scatter | solution.py:341
  731.8 10.6 bitcast_add_fusion
  756.0 37.1 %psum.45 = f32[1,2880]{1,0:T(1,128)S(1)} all-reduce(f32[1,2880]{1,0:T(1,128)S(1)} %broadcast_in_dim.41), channel_id=1, replica_groups=mesh['dp'=8,'tensor'=4] {'dp'}, use_global_device_ids=true, to_apply=%region_205.206 | all-reduce | flops 2880 | bytes 23040 | tf_op jit(solution)/shard_map/psum | solution.py:380
  806.4 59.2 %all-reduce.5.cloned.1.call-done = f32[8,3264]{1,0:T(8,128)} async-done(((f32[8,3264]{1,0:T(8,128)}), f32[8,3264]{1,0:T(8,128)}) %all-reduce.5.cloned.1.call-update) | async-done | bytes 104464 | tf_op jit(solution)/shard_map/psum | solution.py:380
  909.4 18.4 %subtract_multiply_fusion.30 = (f32[1,192]{1,0:T(1,128)S(1)}, f32[1,192]{1,0:T(1,128)S(1)}, f32[1,192]{1,0:T(1,128)S(1)}, f32[1,192]{1,0:T(1,128)S(1)}, f32[1,19...) fusion(f32[1,192]{1,0:T(1,128)S(1)} %get-tuple-element.438, f32[]{:T(128)S(6)} %rsqrt.187, ...), kind=kLoop, calls=%fused_computation.569 | loop fusion | flops 12096 | bytes 11660 | tf_op jit(solution)/shard_map/mul | solution.py:119
  976.8 18.6 %subtract_multiply_fusion.2 = (f32[1,768]{1,0:T(1,128)S(1)}, f32[1,768]{1,0:T(1,128)S(1)}, f32[1,768]{1,0:T(1,128)S(1)}, f32[1,768]{1,0:T(1,128)S(1)}, f32[1,768...) fusion(f32[1,768]{1,0:T(1,128)S(1)} %get-tuple-element.294, f32[8,3264]{1,0:T(8,128)} %all-reduce.5.cloned.1.call-done, ...), kind=kLoop, calls=%fused_computation.461 | loop fusion | flops 48384 | bytes 46220 | tf_op jit(solution)/shard_map/mul | solution.py:119
  1120.0 17.8 %subtract_multiply_fusion.16 = (f32[1,768]{1,0:T(1,128)S(1)}, f32[1,768]{1,0:T(1,128)S(1)}, f32[1,768]{1,0:T(1,128)S(1)}, f32[1,768]{1,0:T(1,128)S(1)}, f32[1,76...) fusion(f32[1,768]{1,0:T(1,128)S(1)} %get-tuple-element.434, f32[8,3264]{1,0:T(8,128)S(1)} %copy-done.56, ...), kind=kLoop, calls=%fused_computation.477 | loop fusion | flops 48384 | bytes 46220 | tf_op jit(solution)/shard_map/mul | solution.py:119
  1140.5 17.4 %subtract_multiply_fusion.9 = (f32[1,768]{1,0:T(1,128)S(1)}, f32[1,768]{1,0:T(1,128)S(1)}, f32[1,768]{1,0:T(1,128)S(1)}, f32[1,768]{1,0:T(1,128)S(1)}, f32[1,768...) fusion(f32[1,768]{1,0:T(1,128)S(1)} %get-tuple-element.436, f32[8,3264]{1,0:T(8,128)S(1)} %copy-done.56, ...), kind=kLoop, calls=%fused_computation.469 | loop fusion | flops 48384 | bytes 46220 | tf_op jit(solution)/shard_map/mul | solution.py:119
  1161.2 17.5 %subtract_multiply_fusion.23 = (f32[1,768]{1,0:T(1,128)S(1)}, f32[1,768]{1,0:T(1,128)S(1)}, f32[1,768]{1,0:T(1,128)S(1)}, f32[1,768]{1,0:T(1,128)S(1)}, f32[1,76...) fusion(f32[1,768]{1,0:T(1,128)S(1)} %get-tuple-element.432, f32[8,3264]{1,0:T(8,128)S(1)} %copy-done.56, ...), kind=kLoop, calls=%fused_computation.485 | loop fusion | flops 48384 | bytes 46220 | tf_op jit(solution)/shard_map/mul | solution.py:119
  1185.0 16.9 %concatenate.104 = f32[1093,768]{1,0:T(8,128)} concatenate(f32[16,768]{1,0:T(8,128)S(1)} %fusion.61, f32[1,768]{1,0:T(1,128)S(1)} %broadcast_in_dim.44, f32[256,768]{1,0:T(8,128)S(1)} %copy-done.45, f32[1,768]{1,0:T(1,128)S(1)} %copy-done.80, f32[768,768]{1,0:T(8,128)S(1)} %copy-done.31, f32[1,768]{1,0:T(1,128)S(1)} %copy-done.79, f32[32,768]{1,0:T(8,128)S(1)} %fusion.131, ...), dimensions={0} | concatenate | bytes 6715392 | tf_op jit(solution)/shard_map/concatenate | solution.py:355
  1213.7 40.8 %all-reduce.7.cloned.1.call-done = f32[8,4416]{1,0:T(8,128)} async-done(((f32[8,4416]{1,0:T(8,128)}), f32[8,4416]{1,0:T(8,128)}) %all-reduce.7.cloned.1.call-update) | async-done | bytes 141328 | tf_op jit(solution)/shard_map/psum | solution.py:387
  1291.1 13.3 multiply_subtract_fusion
  1325.4 72.0 %all-reduce.9.cloned.1.call-done = f32[1093,768]{1,0:T(8,128)} async-done(((f32[1093,768]{1,0:T(8,128)}), f32[1093,768]{1,0:T(8,128)}) %all-reduce.9.cloned.1.call-update) | async-done | bytes 3357712 | tf_op jit(solution)/shard_map/psum | solution.py:381
  (460 shorter events, 532.2 us)
Async XLA Ops:
  7.2 52.3 %all-gather.8.cloned.1.call-start = ((), (), s32[]{:S(2)}) async-start(), calls=%async_computation.5 | async-start | bytes 1990656 | tf_op jit(solution)/shard_map/all_gather | solution.py:163
  9.0 129.7 %all-gather.10.cloned.1.call-start = ((), (), s32[]{:S(2)}) async-start(), calls=%async_computation.6 | async-start | bytes 5087232 | tf_op jit(solution)/shard_map/all_gather | solution.py:161
  11.2 181.3 %all-gather.12.cloned.1.call-start = ((), (), s32[]{:S(2)}) async-start(), calls=%async_computation.7 | async-start | bytes 3932160 | tf_op jit(solution)/shard_map/all_gather | solution.py:215
  63.2 238.3 %copy-start.5 = (f32[512,768]{1,0:T(8,128)}, f32[512,768]{1,0:T(8,128)S(1)}, u32[]{:S(2)}) copy-start(f32[512,768]{1,0:T(8,128)S(1)} %get-tuple-element.455) | copy-start | bytes 4718596
  64.0 81.4 %copy-start.68 = (f32[8,768]{1,0:T(8,128)}, f32[8,768]{1,0:T(8,128)S(1)}, u32[]{:S(2)}) copy-start(f32[8,768]{1,0:T(8,128)S(1)} %convolution_add_fusion.4) | copy-start | bytes 73732
  65.5 79.9 %copy-start.57 = (f32[8,768]{1,0:T(8,128)}, f32[8,768]{1,0:T(8,128)S(1)}, u32[]{:S(2)}) copy-start(f32[8,768]{1,0:T(8,128)S(1)} %convolution_add_fusion.2) | copy-start | bytes 73732
  165.6 73.7 %all-gather.14.cloned.1.call-start = ((), (), s32[]{:S(2)}) async-start(), calls=%async_computation.8 | async-start | bytes 1769472 | tf_op jit(solution)/shard_map/all_gather | solution.py:162
  166.4 135.0 %reduce-scatter.6.cloned.1.call-start = ((), (), s32[]{:S(2)}) async-start(), calls=%async_computation.9 | async-start | bytes 7864320 | tf_op jit(solution)/shard_map/reduce_scatter | solution.py:224
  244.1 91.7 %all-gather.16.cloned.1.call-start = ((), (), s32[]{:S(2)}) async-start(), calls=%async_computation.10 | async-start | bytes 3932160 | tf_op jit(solution)/shard_map/all_gather | solution.py:215
  307.1 101.2 %reduce-scatter.8.cloned.1.call-start = ((), (), s32[]{:S(2)}) async-start(), calls=%async_computation.11 | async-start | bytes 7864320 | tf_op jit(solution)/shard_map/reduce_scatter | solution.py:224
  349.7 102.8 %all-gather.18.cloned.1.call-start = ((), (), s32[]{:S(2)}) async-start(), calls=%async_computation.12 | async-start | bytes 3932160 | tf_op jit(solution)/shard_map/all_gather | solution.py:234
  423.8 104.2 %reduce-scatter.10.cloned.1.call-start = ((), (), s32[]{:S(2)}) async-start(), calls=%async_computation.13 | async-start | bytes 7864320 | tf_op jit(solution)/shard_map/reduce_scatter | solution.py:229
  469.5 95.1 %all-gather.20.cloned.1.call-start = ((), (), s32[]{:S(2)}) async-start(), calls=%async_computation.14 | async-start | bytes 3932160 | tf_op jit(solution)/shard_map/all_gather | solution.py:234
  535.9 141.0 %reduce-scatter.12.cloned.1.call-start = ((), (), s32[]{:S(2)}) async-start(), calls=%async_computation.15 | async-start | bytes 7864320 | tf_op jit(solution)/shard_map/reduce_scatter | solution.py:229
  594.4 121.6 %reduce-scatter.14.cloned.1.call-start = ((), (), s32[]{:S(2)}) async-start(), calls=%async_computation.16 | async-start | bytes 245760 | tf_op jit(solution)/shard_map/reduce_scatter | solution.py:341
  695.6 170.0 %all-reduce.5.cloned.1.call-start = ((), (), s32[]{:S(2)}) async-start(), calls=%async_computation.17 | async-start | bytes 212992 | tf_op jit(solution)/shard_map/psum | solution.py:380
  795.9 131.9 %copy-start.8 = (f32[960,768]{1,0:T(8,128)S(1)}, f32[960,768]{1,0:T(8,128)}, u32[]{:S(2)}) copy-start(f32[960,768]{1,0:T(8,128)} %copy-done.7) | copy-start | bytes 8847364
  800.2 454.4 %all-reduce.7.cloned.1.call-start = ((), (), s32[]{:S(2)}) async-start(), calls=%async_computation.18 | async-start | bytes 286720 | tf_op jit(solution)/shard_map/psum | solution.py:387
  931.4 188.5 %copy-start.56 = (f32[8,3264]{1,0:T(8,128)S(1)}, f32[8,3264]{1,0:T(8,128)}, u32[]{:S(2)}) copy-start(f32[8,3264]{1,0:T(8,128)} %all-reduce.5.cloned.1.call-done) | copy-start | bytes 313348
  995.4 217.6 %copy-start.59 = (f32[8,768]{1,0:T(8,128)}, f32[8,768]{1,0:T(8,128)S(1)}, u32[]{:S(2)}) copy-start(f32[8,768]{1,0:T(8,128)S(1)} %stack.26) | copy-start | bytes 73732
  1184.6 212.8 %all-reduce.9.cloned.1.call-start = ((), (), s32[]{:S(2)}) async-start(), calls=%async_computation.19 | async-start | bytes 6733824 | tf_op jit(solution)/shard_map/psum | solution.py:381
  1321.7 75.7 %copy-start.48 = (f32[1093,96]{1,0:T(8,128)S(1)}, f32[1093,96]{1,0:T(8,128)}, u32[]{:S(2)}) copy-start(f32[1093,96]{1,0:T(8,128)} %copy.147) | copy-start | bytes 1259140
  1321.7 75.7 %copy-start.49 = (f32[1093,96]{1,0:T(8,128)S(1)}, f32[1093,96]{1,0:T(8,128)}, u32[]{:S(2)}) copy-start(f32[1093,96]{1,0:T(8,128)} %copy.146) | copy-start | bytes 1259140
  1325.4 75.4 %copy-start.53 = (f32[8,4416]{1,0:T(8,128)S(1)}, f32[8,4416]{1,0:T(8,128)}, u32[]{:S(2)}) copy-start(f32[8,4416]{1,0:T(8,128)} %all-reduce.7.cloned.1.call-done) | copy-start | bytes 423940
  (88 other events, 872.2 us)
Sparse Core Ops, SparseCore 0:
  10.8 48.6 all-gather.7
  62.2 76.4 all-gather.9
  165.8 26.7 all-gather.11
  195.1 44.1 all-gather.13
  244.2 57.1 reduce-scatter.5
  307.2 28.5 all-gather.15
  349.8 58.3 reduce-scatter.7
  423.9 28.5 all-gather.17
  469.6 58.3 reduce-scatter.9
  536.0 28.5 all-gather.19
  594.5 59.5 reduce-scatter.11
  695.7 20.2 reduce-scatter.13
  800.3 65.1 all-reduce.4
  1184.7 69.8 all-reduce.6
  1260.0 137.3 all-reduce.8
where the time goes:
time: 1420 us; the launch traced here: 1410 us
  waiting for transfers between devices  625 us (44%)
  other arithmetic  367 us (26%)
  matrix products  161 us (11%)
  local copies, waits for them, and re-layouts  127 us (9%)
  blocking collectives  83.5 us (6%)
  between operations  43.3 us (3%)
    reduce_sum x46, other arithmetic, orthonormal(): vector = vector - jnp.sum(vector * earlier) * earlier  140 us
    reduce_scatter x2, waiting for transfers between devices, branch_sum(): lax.psum_scatter(fast_dot(inputs_low, weight), 'tensor', scatter_dimensio...  115 us
    mul x6, other arithmetic, orthonormal(): vector = vector * lax.rsqrt(jnp.sum(vector * vector) + TINY)  90.6 us
    all_gather x1, waiting for transfers between devices, shards(): lax.all_gather(col_weights.astype(jnp.bfloat16), 'dp', axis=0, tiled=True)  73.3 us
    psum x1, waiting for transfers between devices, shards(): lax.psum((small_grad, g_bhead, loss_part), ('dp', 'tensor'))  72 us
    psum x1, waiting for transfers between devices, shards(): left_sum, bias_sum = lax.psum((left_local, bias_grad), 'dp')  59.2 us
    reduce_scatter x2, waiting for transfers between devices, input_grad(): lax.psum_scatter(fast_ndot(grads_low, weight), 'tensor', scatter_dimensio...  58.5 us
    all_gather x2, waiting for transfers between devices, spread_grad(): return lax.all_gather(rows_low, 'tensor', axis=0, tiled=True)  57.1 us
  transfers between devices with their start and end apart: 15, of which 14 were waited for; matrix products, arithmetic and copies ran while one was open for 12% of the time, Pallas kernels for 0%

commit v1 on v0

v1 whole, which is shorter than its diff:
```python
import functools
import math

import jax
import jax.numpy as jnp
from jax import lax
from jax.experimental import pallas as pl
from jax.experimental.pallas import tpu as pltpu
from jax.sharding import PartitionSpec as P

D = 768
HEADS = 12
HEAD_DIM = 64
FF = 3072
FREQ = 256
GRID = 16
PATCH_IN = 16
CLASSES = 32
SEQ = 256

EPSILON = 1e-06
TINY = 1e-30
DECAY = 0.9
LEARN_RATE = 100.0
TIME_OFFSET = 0.25
F32 = jnp.float32
BF = jnp.bfloat16
SCALE = 1.0 / math.sqrt(HEAD_DIM)
GELU_C = math.sqrt(2.0 / math.pi)


def exact_dot(left, right):
    return jnp.dot(left, right, precision=lax.Precision.HIGHEST, preferred_element_type=F32)


def exact_tdot(left, right):
    return lax.dot_general(left, right, (((0,), (0,)), ((), ())), precision=lax.Precision.HIGHEST, preferred_element_type=F32)


def exact_ndot(left, right):
    return lax.dot_general(left, right, (((1,), (1,)), ((), ())), precision=lax.Precision.HIGHEST, preferred_element_type=F32)


def dot(a,b): return lax.dot_general(a,b,(((1,),(0,)),((),())),preferred_element_type=F32)
def ndot(a,b): return lax.dot_general(a,b,(((1,),(1,)),((),())),preferred_element_type=F32)
def tdot(a,b): return lax.dot_general(a,b,(((0,),(0,)),((),())),preferred_element_type=F32)

def ln(h):
    c=h-jnp.mean(h,axis=-1,keepdims=True)
    v=jnp.mean(c*c,axis=-1,keepdims=True)
    r=lax.rsqrt(v+EPSILON)
    return c*r,r

def ln_back(dout,xh,r,scale):
    dx=dout*(1.0+scale)
    return r*(dx-jnp.mean(dx,axis=-1,keepdims=True)-xh*jnp.mean(dx*xh,axis=-1,keepdims=True))

def colsum(v): return jnp.sum(v,axis=0,keepdims=True)

def block_kernel(base_ref,times_ref,clean_ref,noise_ref,mod_ref,wall_ref,pe_ref,wp_ref,bp_ref,wh_ref,bh_ref,bo_ref,b2_ref,bq_ref,b1_ref,
           a_ref,m_ref,dy_ref,dz_ref,o_ref,dq_ref,g_ref,du_ref,dmod_ref,small_ref,dbq_ref,db1_ref,dbh_ref,loss_ref,
           r_s,p_s,gp_s,xh1_s,xh2_s,y_s,z_s,h_s,acc_s,r1_s,r2_s,*,count_all):
    step=pl.program_id(0)
    base=base_ref[0]
    t=times_ref[step]
    lo=lax.broadcasted_iota(jnp.int32,(1,128),1)<64
    @pl.when(step==0)
    def _():
        small_ref[...]=jnp.zeros_like(small_ref); dbq_ref[...]=jnp.zeros_like(dbq_ref); db1_ref[...]=jnp.zeros_like(db1_ref)
        dbh_ref[...]=jnp.zeros_like(dbh_ref); loss_ref[...]=jnp.zeros_like(loss_ref)
    clean=clean_ref[0].astype(F32); noise=noise_ref[0].astype(F32)
    mixed=(t*clean+(1.0-t)*noise).astype(BF)
    mod=lambda i: mod_ref[0,i:i+1,:]
    h0=dot(mixed,wp_ref[...])+bp_ref[...]+pe_ref[...]
    h_s[...]=h0
    xh,r=ln(h0)
    xh1_s[...]=xh; r1_s[...]=r
    a_ref[0]=(xh*(1.0+mod(1))+mod(0)).astype(BF)
    y_s[...]=jnp.zeros_like(y_s)
    zero=jnp.zeros((),BF)
    roll=lambda v: pltpu.roll(v.astype(F32),64,1).astype(BF)
    def softmax_store(s,idx):
        s=s*SCALE
        e=jnp.exp(s-jnp.max(s,axis=-1,keepdims=True))
        p=e/jnp.sum(e,axis=-1,keepdims=True)
        p_s[idx]=p
        return p.astype(BF)
    @pl.loop(0,4)
    def _(jj):
        j=lax.rem(base+jj,4)
        r_s[jj]=(dot(a_ref[0],wall_ref[j,:,0:768])+bq_ref[j]).astype(BF)
        blk=lambda i: r_s[jj,:,128*i:128*(i+1)]
        b0,b1,b2,b3,b4=[blk(i) for i in range(5)]
        p0=softmax_store(ndot(jnp.where(lo,b0,zero),roll(b0)),3*jj)
        p1=softmax_store(ndot(jnp.where(lo,zero,b1),roll(b2)),3*jj+1)
        p2=softmax_store(ndot(jnp.where(lo,b3,zero),roll(b3)),3*jj+2)
        o01=jnp.where(lo,dot(p0,b1),dot(p1,b2)).astype(BF)
        o2=jnp.where(lo,dot(p2,b4),0.0).astype(BF)
        @pl.when(jj<2)
        def _():
            o_ref[jj,0,:,0:128]=o01; o_ref[jj,0,:,128:256]=o2
        ro=roll(o01)
        ob4=jnp.where(lo,zero,ro)
        ob5=jnp.where(lo,ro,roll(o2))
        y_s[...]+=ndot(jnp.concatenate([ob4,ob5],axis=1),wall_ref[j,:,512:768])
    y=y_s[...]+bo_ref[...]
    y_s[...]=y
    h1=h_s[...]+mod(2)*y
    h_s[...]=h1
    xh,r=ln(h1)
    xh2_s[...]=xh; r2_s[...]=r
    m_ref[0]=(xh*(1.0+mod(4))+mod(3)).astype(BF)
    z_s[...]=jnp.zeros_like(z_s)
    @pl.loop(0,4)
    def _(jj):
        j=lax.rem(base+jj,4)
        u=dot(m_ref[0],wall_ref[j,:,768:1536])+b1_ref[j]
        uu=u*u
        th=jnp.tanh(GELU_C*(u+0.044715*(uu*u)))
        cdf=0.5*(1.0+th)
        g=(u*cdf).astype(BF)
        gp_s[jj]=cdf+0.5*u*(1.0-th*th)*(GELU_C*(1.0+3.0*0.044715*uu))
        @pl.when(jj<2)
        def _(): g_ref[jj,0]=g
        z_s[...]+=ndot(g,wall_ref[j,:,1536:2304])
    z=z_s[...]+b2_ref[...]
    z_s[...]=z
    h2=h_s[...]+mod(5)*z
    xh,r=ln(h2)
    fi=(xh*(1.0+mod(7))+mod(6)).astype(BF)
    pred=ndot(fi,wh_ref[...])+bh_ref[...]
    diff=pred-(clean-noise)
    weight=1.0/(1.0-t+0.25)
    loss_ref[...]+=jnp.sum(colsum(weight*diff*diff),axis=1,keepdims=True)*(1.0/count_all)
    dpred=2.0*weight*diff*(1.0/count_all)
    dbh_ref[...]+=colsum(dpred)
    dpl=dpred.astype(BF)
    small_ref[16:32]+=tdot(dpl,fi)
    dfi=dot(dpl,wh_ref[...])
    dmod_ref[0,6:7]=colsum(dfi); dmod_ref[0,7:8]=colsum(dfi*xh)
    dh=ln_back(dfi,xh,r,mod(7))
    h_s[...]=dh
    dmod_ref[0,5:6]=colsum(dh*z_s[...])
    dzf=dh*mod(5)
    small_ref[34:35]+=colsum(dzf)
    dz_ref[0]=dzf.astype(BF)
    acc_s[...]=jnp.zeros_like(acc_s)
    @pl.loop(0,4)
    def _(jj):
        j=lax.rem(base+jj,4)
        du=dot(dz_ref[0],wall_ref[j,:,1536:2304])*gp_s[jj]
        dul=du.astype(BF)
        @pl.when(jj<2)
        def _():
            du_ref[jj,0]=dul
            db1_ref[jj]+=colsum(du)
        acc_s[...]+=ndot(dul,wall_ref[j,:,768:1536])
    dm=acc_s[...]
    xh=xh2_s[...]
    dmod_ref[0,3:4]=colsum(dm); dmod_ref[0,4:5]=colsum(dm*xh)
    dh=h_s[...]+ln_back(dm,xh,r2_s[...],mod(4))
    h_s[...]=dh
    dmod_ref[0,2:3]=colsum(dh*y_s[...])
    dyf=dh*mod(2)
    small_ref[33:34]+=colsum(dyf)
    dy_ref[0]=dyf.astype(BF)
    acc_s[...]=jnp.zeros_like(acc_s)
    @pl.loop(0,4)
    def _(jj):
        j=lax.rem(base+jj,4)
        do=dot(dy_ref[0],wall_ref[j,:,512:768]).astype(BF)
        r4=roll(do[:,0:128]); r5=roll(do[:,128:256])
        do0=jnp.where(lo,r4,zero); do1=jnp.where(lo,zero,r5); do2=jnp.where(lo,r5,zero)
        blk=lambda i: r_s[jj,:,128*i:128*(i+1)]
        b0,b1,b2,b3,b4=[blk(i) for i in range(5)]
        def head(h,doh,v,):
            p=p_s[3*jj+h]
            dv=tdot(p.astype(BF),doh)
            dp=ndot(doh,v)
            ds=(p*(dp-jnp.sum(p*dp,axis=-1,keepdims=True))).astype(BF)
            return dv,ds
        dv0,ds0=head(0,do0,b1)
        dv1,ds1=head(1,do1,b2)
        dv2,ds2=head(2,do2,b4)
        rb0=roll(b0); rb3=roll(b3)
        n0=jnp.where(lo,dot(ds0,rb0),tdot(ds0,rb0))*SCALE
        dq1=dot(ds1,roll(b2))*SCALE; dk1=tdot(ds1,roll(b1))*SCALE
        n1=jnp.where(lo,dv0,dq1); n2=jnp.where(lo,dk1,dv1)
        n3=jnp.where(lo,dot(ds2,rb3),tdot(ds2,rb3))*SCALE
        n4=jnp.where(lo,dv2,0.0)
        dqkv=jnp.concatenate([n0,n1,n2,n3,n4],axis=1)
        dl=dqkv.astype(BF)
        @pl.when(jj<2)
        def _():
            dq_ref[jj,0]=dl
            dbq_ref[jj]+=colsum(dqkv)
        acc_s[...]+=ndot(dl,wall_ref[j,:,0:640])
    da=acc_s[...]
    xh=xh1_s[...]
    dmod_ref[0,0:1]=colsum(da); dmod_ref[0,1:2]=colsum(da*xh)
    dh=h_s[...]+ln_back(da,xh,r1_s[...],mod(1))
    small_ref[32:33]+=colsum(dh)
    small_ref[0:16]+=tdot(mixed,dh.astype(BF))

def run_block(base,times,clean,noise,mod,wall,pe,wp,bp,wh,bh,bo,b2,bq,b1,count_all):
    L=clean.shape[0]
    full=lambda a: pl.BlockSpec(a.shape,lambda i,*_: (0,)*a.ndim,pipeline_mode=pl.Buffered(1))
    lat=lambda *s: pl.BlockSpec((1,)+s,lambda i,*_:(i,)+(0,)*len(s))
    pair=lambda w: pl.BlockSpec((2,1,SEQ,w),lambda i,*_:(0,i,0,0))
    const=lambda *s: pl.BlockSpec(s,lambda i,*_:(0,)*len(s))
    S=jax.ShapeDtypeStruct
    outs=[S((L,SEQ,D),BF)]*4+[S((2,L,SEQ,256),BF),S((2,L,SEQ,640),BF),S((2,L,SEQ,768),BF),S((2,L,SEQ,768),BF),
        S((L,8,D),F32),S((40,D),F32),S((2,1,640),F32),S((2,1,768),F32),S((1,PATCH_IN),F32),S((1,1),F32)]
    ospecs=[lat(SEQ,D)]*4+[pair(256),pair(640),pair(768),pair(768),lat(8,D),const(40,D),const(2,1,640),const(2,1,768),const(1,PATCH_IN),const(1,1)]
    V=pltpu.VMEM
    f=lambda: V((SEQ,D),F32)
    return pl.pallas_call(functools.partial(block_kernel,count_all=count_all),
        grid_spec=pltpu.PrefetchScalarGridSpec(num_scalar_prefetch=2,grid=(L,),
            in_specs=[lat(SEQ,PATCH_IN),lat(SEQ,PATCH_IN),lat(8,D)]+[full(v) for v in (wall,pe,wp,bp,wh,bh,bo,b2,bq,b1)],
            out_specs=ospecs,
            scratch_shapes=[V((4,SEQ,768),BF),V((12,SEQ,SEQ),F32),V((4,SEQ,768),F32),f(),f(),f(),f(),f(),f(),V((SEQ,1),F32),V((SEQ,1),F32)]),
        out_shape=outs,
        compiler_params=pltpu.CompilerParams(vmem_limit_bytes=60*1024*1024),
        name="block",
    )(base,times,clean,noise,mod,wall,pe,wp,bp,wh,bh,bo,b2,bq,b1)


def position_rows(token_ids):
    quarter = D // 4
    omega = 1.0 / 10000.0 ** (jnp.arange(quarter, dtype=jnp.float32) / quarter)
    row_pos = (token_ids // GRID).astype(jnp.float32)[:, None] * omega[None, :]
    col_pos = (token_ids % GRID).astype(jnp.float32)[:, None] * omega[None, :]
    return jnp.concatenate(
        [jnp.sin(row_pos), jnp.cos(row_pos), jnp.sin(col_pos), jnp.cos(col_pos)], axis=1
    )


def time_features(times):
    half = FREQ // 2
    freqs = jnp.exp(-math.log(10000.0) * jnp.arange(half, dtype=jnp.float32) / half)
    angles = 1000.0 * times[:, None] * freqs[None, :]
    return jnp.concatenate([jnp.cos(angles), jnp.sin(angles)], axis=1)


def small_starts():
    counts = [PATCH_IN, 1, FREQ, 1, D, 1, CLASSES, PATCH_IN, 1, 1]
    starts = [0]
    for amount in counts:
        starts.append(starts[-1] + amount)
    return starts


def cut_parts(array, widths, axis):
    pieces = []
    offset = 0
    for width in widths:
        pieces.append(lax.slice_in_dim(array, offset, offset + width, axis=axis))
        offset = offset + width
    return pieces


def ortho_kernel(x_ref, o_ref):
    count = x_ref.shape[0]
    rows = [x_ref[index] for index in range(count)]
    for index in range(count):
        vector = rows[index]
        vector = vector * lax.rsqrt(jnp.sum(vector * vector, axis=-1, keepdims=True) + TINY)
        o_ref[index] = vector
        for later in range(index + 1, count):
            rows[later] = rows[later] - jnp.sum(rows[later] * vector, axis=-1, keepdims=True) * vector


def orthonormal_all(parts):
    stacked = jnp.stack([jnp.pad(part, ((0, 0), (0, D - part.shape[1]))) for part in parts], axis=1)
    stacked = jnp.pad(stacked, ((0, 0), (0, 8 - len(parts)), (0, 0)))
    out = pl.pallas_call(ortho_kernel, out_shape=jax.ShapeDtypeStruct(stacked.shape, F32), name="ortho")(stacked)
    return [out[:, index, : part.shape[1]] for index, part in enumerate(parts)]


def rounded(values):
    return lax.optimization_barrier(values.astype(BF)).astype(F32)


def silu_slope(values):
    gate = jax.nn.sigmoid(values)
    return gate * (1.0 + values * (1.0 - gate))


def shards(
    clean_latents,
    noise_draw,
    timesteps,
    labels,
    col_weights,
    col_moments,
    col_errors,
    row_weights,
    row_moments,
    row_errors,
    bias_weights,
    bias_moments,
    small_weights,
    small_moments,
    head_bias,
    head_moments,
    right_factors,
):
    tensor_size = lax.axis_size("tensor")
    data_size = lax.axis_size("dp")
    tensor_rank = lax.axis_index("tensor")
    data_rank = lax.axis_index("dp")
    batch = clean_latents.shape[0]
    half = batch // 2
    share = D // data_size
    mod_width = 8 * D // tensor_size
    qkv_width = 3 * D // tensor_size
    ffn_width = FF // tensor_size
    proj_rows = D // tensor_size
    count_all = data_size * batch * SEQ * PATCH_IN
    col_widths = [mod_width, qkv_width, ffn_width]
    core = lax.rem(tensor_rank, 2)
    base = tensor_rank - core
    pair = [(index, index + 1 - 2 * (index % 2)) for index in range(tensor_size)]

    def swap(values):
        return lax.ppermute(values, "tensor", pair)

    col_low = col_weights[:, 0, :].astype(BF)
    row_low = row_weights[0].astype(BF).T
    packed = jnp.concatenate(
        [
            col_low[:, mod_width : mod_width + qkv_width],
            row_low[:, :proj_rows],
            col_low[:, mod_width + qkv_width :],
            row_low[:, proj_rows:],
        ],
        axis=1,
    )
    wall = lax.all_gather(lax.all_gather(packed, "dp", axis=0, tiled=True), "tensor", axis=0)
    starts = small_starts()
    small_low = small_weights.astype(BF)
    small_exact = rounded(small_weights)
    picked = jnp.concatenate([small_low[: starts[2]], small_low[starts[7] :]], axis=0)
    emb = lax.all_gather(picked.astype(F32), "dp", axis=1, tiled=True)
    w_patch = emb[:16].astype(BF)
    b_patch = emb[16:17]
    w_head = emb[17:33].astype(BF)
    b_proj = emb[33:34]
    b_fc2 = emb[34:35]
    w_tin = small_exact[starts[2] : starts[3]]
    b_tin = small_exact[starts[3]]
    w_tout = small_exact[starts[4] : starts[5]]
    b_tout = small_exact[starts[5]]
    table = small_exact[starts[6] : starts[7]]
    bias_exact = rounded(bias_weights[0])
    head_exact = rounded(head_bias)
    w_mod = rounded(col_weights[:, 0, :mod_width])
    bias_all = lax.all_gather(bias_exact, "tensor", axis=0)
    times_all = lax.all_gather(timesteps, "dp", axis=0, tiled=True)
    labels_all = lax.all_gather(labels, "dp", axis=0, tiled=True)
    time_feat = time_features(times_all)
    time_hidden = exact_dot(time_feat, w_tin) + b_tin
    time_act = lax.all_gather(jax.nn.silu(time_hidden), "dp", axis=1, tiled=True)
    onehot = (labels_all[:, None] == jnp.arange(CLASSES, dtype=jnp.int32)[None, :]).astype(F32)
    condition = exact_dot(time_act, w_tout) + b_tout + exact_dot(onehot, table)
    cond_act = jax.nn.silu(condition)
    mod_part = exact_dot(cond_act, w_mod)
    mod_own = lax.psum_scatter(mod_part, "dp", scatter_dimension=0, tiled=True) + bias_exact[:mod_width]
    mod_full = lax.all_gather(mod_own, "tensor", axis=1, tiled=True).reshape(batch, 8, D)
    cond_rows = lax.all_to_all(cond_act, "dp", split_axis=0, concat_axis=1, tiled=True)

    def mine(values):
        return lax.dynamic_slice_in_dim(values, core * half, half, 0)

    bq = jnp.pad(bias_all[:, mod_width : mod_width + qkv_width], ((0, 0), (0, 768 - qkv_width)))[:, None]
    b1 = bias_all[:, mod_width + qkv_width :][:, None]
    positions = position_rows(jnp.arange(SEQ, dtype=jnp.int32))
    (a, m, dy, dz, o, dq, g, du, dmod, small, dbq, db1, dbh, loss) = run_block(
        base.reshape(1),
        mine(timesteps),
        mine(clean_latents),
        mine(noise_draw),
        mine(mod_full),
        wall,
        positions,
        w_patch,
        b_patch,
        w_head,
        head_exact[None],
        b_proj,
        b_fc2,
        bq,
        b1,
        count_all,
    )
    rows = half * SEQ

    def flat(values):
        return values.reshape(rows, values.shape[-1])

    def pick(values, which):
        return lax.dynamic_index_in_dim(values, which, 0, keepdims=False)

    def gradients(which):
        return (
            tdot(flat(a), flat(pick(dq, which))[:, :qkv_width]),
            tdot(flat(m), flat(pick(du, which))),
            tdot(flat(pick(o, which))[:, :proj_rows], flat(dy)),
            tdot(flat(pick(g, which)), flat(dz)),
            pick(dbq, which)[0, :qkv_width],
            pick(db1, which)[0],
        )

    other = swap(gradients(1 - core))
    own = gradients(core)
    g_qkv, g_fc1, g_proj, g_fc2, g_bqkv, g_bfc1 = [left + right for left, right in zip(own, other)]
    dmod_own = dmod.reshape(half, 8 * D)
    dmod_other = swap(dmod_own)
    dmod_group = jnp.where(
        core == 0,
        jnp.concatenate([dmod_own, dmod_other], axis=0),
        jnp.concatenate([dmod_other, dmod_own], axis=0),
    )
    d_mod = lax.dynamic_slice_in_dim(dmod_group, tensor_rank * mod_width, mod_width, 1)
    g_bmod = jnp.sum(d_mod, axis=0)
    g_mod = exact_tdot(cond_rows, d_mod)
    d_mod_all = lax.all_gather(d_mod, "dp", axis=0, tiled=True)
    d_cond = lax.psum(exact_ndot(d_mod_all, w_mod), "tensor") * silu_slope(condition)
    g_table = exact_tdot(onehot, d_cond)
    g_btout = jnp.sum(d_cond, axis=0)
    g_tout = exact_tdot(time_act, d_cond)
    d_time = lax.psum_scatter(exact_ndot(d_cond, w_tout), "dp", scatter_dimension=1, tiled=True)
    d_time = d_time * silu_slope(time_hidden)
    g_btin = jnp.sum(d_time, axis=0)
    g_tin = exact_tdot(time_feat, d_time)
    small_own = lax.psum(lax.psum_scatter(small, "dp", scatter_dimension=1, tiled=True), "tensor") * 0.5
    head_sum, loss_value = lax.psum((dbh[0] * 0.5, loss[0, 0] * 0.5), ("dp", "tensor"))
    small_step = jnp.concatenate(
        [
            small_own[:16],
            small_own[32:33],
            g_tin,
            g_btin[None],
            g_tout,
            g_btout[None],
            g_table,
            small_own[16:32],
            small_own[33:34],
            small_own[34:35],
        ],
        axis=0,
    )
    bias_sum = lax.psum(jnp.concatenate([g_bmod, g_bqkv, g_bfc1], axis=0), "dp")
    col_cuts = cut_parts(col_errors[0, 0], col_widths, 1)
    row_cuts = cut_parts(row_errors[0, 0], [proj_rows, ffn_width], 0)
    matrices = [
        g_mod + col_cuts[0],
        g_qkv + col_cuts[1],
        g_fc1 + col_cuts[2],
        g_proj + row_cuts[0],
        g_fc2 + row_cuts[1],
    ]
    right_pieces = cut_parts(right_factors[0], col_widths + [D, D], 1)
    left_local = jnp.concatenate([exact_ndot(right_pieces[i], matrices[i]) for i in range(5)], axis=1)
    left_sum = lax.psum(left_local, "dp")
    bases = orthonormal_all(cut_parts(left_sum, [D, D, D, proj_rows, ffn_width], 1))
    right_local = jnp.concatenate([exact_dot(bases[i], matrices[i]) for i in range(5)], axis=1)
    right_sum = lax.psum(right_local, "dp")
    right_split = cut_parts(right_sum, col_widths + [D, D], 1)
    approx = [exact_tdot(bases[i], right_split[i]) for i in range(5)]
    rest = [matrices[i] - approx[i] / data_size for i in range(5)]
    col_residue = jnp.concatenate(rest[:3], axis=1)[None, None]
    row_residue = jnp.concatenate(rest[3:], axis=0)[None, None]

    def own_columns(values):
        return lax.dynamic_slice_in_dim(values, data_rank * share, share, 1)

    col_step = jnp.concatenate(
        [exact_tdot(own_columns(bases[i]), right_split[i]) for i in range(3)], axis=1
    )[:, None, :]
    row_step = jnp.concatenate(
        [exact_tdot(bases[i], own_columns(right_split[i])) for i in (3, 4)], axis=0
    )[None]
    col_momentum = DECAY * col_moments + col_step
    col_new = col_weights - LEARN_RATE * col_momentum
    row_momentum = DECAY * row_moments + row_step
    row_new = row_weights - LEARN_RATE * row_momentum
    small_momentum = DECAY * small_moments + small_step
    small_new = small_weights - LEARN_RATE * small_momentum
    bias_momentum = DECAY * bias_moments + bias_sum[None]
    bias_new = bias_weights - LEARN_RATE * bias_momentum
    head_momentum = DECAY * head_moments + head_sum
    head_new = head_bias - LEARN_RATE * head_momentum
    left_factors = jnp.concatenate(bases, axis=1)[None]
    right_new = right_sum[None]
    return (
        loss_value,
        col_new,
        col_momentum,
        col_residue,
        row_new,
        row_momentum,
        row_residue,
        bias_new,
        bias_momentum,
        small_new,
        small_momentum,
        head_new,
        head_momentum,
        left_factors,
        right_new,
    )


def solution(mesh):
    placed = (
        P("dp", None, None),
        P("dp", None, None),
        P("dp"),
        P("dp"),
        P("dp", "tensor", None),
        P("dp", "tensor", None),
        P("dp", "tensor", None, None),
        P("tensor", None, "dp"),
        P("tensor", None, "dp"),
        P("dp", "tensor", None, None),
        P("tensor", None),
        P("tensor", None),
        P(None, "dp"),
        P(None, "dp"),
        P(),
        P(),
        P("tensor", None, None),
    )
    return jax.shard_map(
        shards,
        mesh=mesh,
        in_specs=placed,
        out_specs=(
            P(),
            P("dp", "tensor", None),
            P("dp", "tensor", None),
            P("dp", "tensor", None, None),
            P("tensor", None, "dp"),
            P("tensor", None, "dp"),
            P("dp", "tensor", None, None),
            P("tensor", None),
            P("tensor", None),
            P(None, "dp"),
            P(None, "dp"),
            P(),
            P(),
            P("tensor", None, None),
            P("tensor", None, None),
        ),
        check_vma=False,
    )
```

time: 1420 us -> 840 us (0.59)
  waiting for transfers between devices: 625 us -> 274 us
  other arithmetic: 367 us -> 20.5 us
  blocking collectives: 83.5 us -> 231 us
  Pallas kernels: 0 us -> 120 us
  matrix products: 161 us -> 87.3 us
  local copies, waits for them, and re-layouts: 127 us -> 76.4 us
  between operations: 43.3 us -> 17.3 us
    reduce_sum x84 -> x2, other arithmetic: 206 us -> 1.45 us  [the longest x1 1.4 us: shards(): g_btout = jnp.sum(d_cond, axis=0)]
    reduce_scatter x5 -> x1, waiting for transfers between devices: 189 us -> 3.85 us  [shards(): lax.psum_scatter(mod_part, 'dp', scatter_dimension=0, tiled=True)]
    all_gather x7 -> x2, waiting for transfers between devices: 263 us -> 86.9 us  [the longest x1 84 us: shards(): lax.all_gather(lax.all_gather(packed, 'dp', axis=0, tiled=True), 'tensor'...]
    pallas_call x0 -> x2, Pallas kernels: none -> 120 us  [the longest x1 117 us: run_block(): pl.pallas_call(functools.partial(block_kernel, count_all=count_all), grid...]
    all_gather x1 -> x4, blocking collectives: 5.61 us -> 99.4 us  [the longest x1 31.7 us: shards(): lax.all_gather(jax.nn.silu(time_hidden), 'dp', axis=1, tiled=True)]
    mul x7 -> x2, other arithmetic: 90.7 us -> 0.01 us  [the longest x1 0.01 us: shards(): lax.psum(lax.psum_scatter(small, 'dp', scatter_dimension=1, tiled=True),...]
    psum x2 -> x1, waiting for transfers between devices: 131 us -> 65.5 us  [shards(): left_sum = lax.psum(left_local, 'dp')]
    dot_general x23 -> x8, matrix products: 82.5 us -> 24 us  [tdot(): lax.dot_general(a, b, (((0,), (0,)), ((), ())), preferred_element_type=F32)]
  transfers between devices with their start and end apart: 15 -> 15, of which waited for: 14 -> 7; matrix products, arithmetic and copies ran while one was open for 12% -> 11% of each run, Pallas kernels for 0% -> 0%
where the time goes in v1:
time: 840 us; the launch traced here: 832 us
  waiting for transfers between devices  274 us (33%)
  blocking collectives  231 us (28%)
  Pallas kernels  120 us (14%)
  matrix products  87.3 us (10%)
  local copies, waits for them, and re-layouts  76.4 us (9%)
  other arithmetic  20.5 us (2%)
  between operations  17.3 us (2%)
    pallas_call x1, Pallas kernels, run_block(): pl.pallas_call(functools.partial(block_kernel, count_all=count_all), grid...  117 us
    all_gather x1, waiting for transfers between devices, shards(): lax.all_gather(lax.all_gather(packed, 'dp', axis=0, tiled=True), 'tensor'...  84 us
    psum x1, waiting for transfers between devices, shards(): right_sum = lax.psum(right_local, 'dp')  67 us
    psum x1, waiting for transfers between devices, shards(): left_sum = lax.psum(left_local, 'dp')  65.5 us
    unnamed x9, waiting for transfers between devices  48.1 us
    unnamed x3, blocking collectives  42.6 us
    psum x1, blocking collectives, shards(): lax.psum((dbh[0] * 0.5, loss[0, 0] * 0.5), ('dp', 'tensor'))  40.3 us
    unnamed x129, local copies, waits for them, and re-layouts  37.6 us
  transfers between devices with their start and end apart: 15, of which 7 were waited for; matrix products, arithmetic and copies ran while one was open for 11% of the time, Pallas kernels for 0%

profile of v1, /device:TPU:0, one launch (start us, length us, event | category | flops | bytes accessed | tf_op | source)
XLA Modules:
  0.0 832.0 jit_solution(18017420227265972636)
XLA Ops:
  12.0 23.3 %all-reduce.3 = f32[64]{0:T(128)S(1)} all-reduce(f32[64]{0:T(128)S(1)} %dynamic-update-slice), channel_id=1, replica_groups=mesh['dp'=8,'tensor'=4] {'dp'}, use_global_device_ids=true, to_apply=%add.3 | all-reduce | flops 64 | bytes 512
  35.8 31.7 %all-gather.2 = f32[8,96,64]{1,2,0:T(8,128)S(1)} all-gather(f32[1,96,64]{1,2,0:T(8,128)S(1)} %multiply_bitcast_fusion), channel_id=1, replica_groups=mesh['dp'=8,'tensor'=4] {'dp'}, dimensions={0}, use_global_device_ids=true | all-gather | bytes 221184 | tf_op jit(solution)/shard_map/all_gather | solution.py:363
  68.0 8.7 %all-reduce.4 = s32[64]{0:T(128)S(1)} all-reduce(s32[64]{0:T(128)S(1)} %dynamic-update-slice.1), channel_id=1, replica_groups=mesh['dp'=8,'tensor'=4] {'dp'}, use_global_device_ids=true, to_apply=%add.4 | all-reduce | flops 64 | bytes 512
  82.8 10.6 %all-reduce.5 = f32[11520]{0:T(1024)S(1)} all-reduce(f32[11520]{0:T(1024)S(1)} %convert_dynamic-update-slice_fusion), channel_id=3, replica_groups=mesh['dp'=8,'tensor'=4] {'tensor'}, use_global_device_ids=true, to_apply=%add.5 | all-reduce | flops 11520 | bytes 92160
  96.0 30.6 %all-gather.3 = f32[8,96,35]{1,2,0:T(8,128)S(1)} all-gather(f32[1,96,35]{1,2,0:T(8,128)S(1)} %convert_bitcast_fusion.1), channel_id=1, replica_groups=mesh['dp'=8,'tensor'=4] {'dp'}, dimensions={0}, use_global_device_ids=true | all-gather | bytes 120960 | tf_op jit(solution)/shard_map/all_gather | solution.py:344
  128.0 9.4 %copy.105 = f32[1,1,768,2880]{3,2,1,0:T(8,128)} copy(f32[1,1,768,2880]{2,3,1,0:T(8,128)} %param.23) | data formatting | bytes 17694720 | tf_op args[6]
  146.8 6.1 all_gather.36
  153.6 84.0 %all-gather.9.cloned.1.call-done = bf16[3072,2304]{1,0:T(8,128)(2,1)} async-done(((bf16[768,2304]{1,0:T(8,128)(2,1)}), bf16[3072,2304]{1,0:T(8,128)(2,1)}) %all-gather.9.cloned.1.call-update) | async-done | bytes 14155792 | tf_op jit(solution)/shard_map/all_gather | solution.py:339
  237.6 117.3 %block.1 = (bf16[4,256,768]{2,1,0:T(8,128)(2,1)}, bf16[4,256,768]{2,1,0:T(8,128)(2,1)}, bf16[4,256,768]{2,1,0:T(8,128)(2,1)}, bf16[4,256,768]{2,1,0:T(8,128)(2,1...) custom-call(s32[1]{0:T(128)} %bitcast.base_ref, ...), custom_call_target="tpu_custom_call" | custom-call | tf_op jit(solution)/shard_map/block/pallas_call | solution.py:217
  376.7 4.7 fusion.88
  382.1 40.3 %all-reduce.6 = (f32[]{:T(128)}, f32[16]{0:T(128)S(1)}) all-reduce(f32[]{:T(128)} %bitcast.18, f32[16]{0:T(128)S(1)} %multiply_bitcast_fusion.1), channel_id=1, replica_groups=mesh['dp'=8,'tensor'=4] {'dp','tensor'}, use_global_device_ids=true, to_apply=%region_1.2 | all-reduce | flops 17 | bytes 136 | tf_op jit(solution)/shard_map/psum | solution.py:437
  427.6 37.1 %psum.52 = f32[1,2880]{1,0:T(1,128)S(1)} all-reduce(f32[1,2880]{1,0:T(1,128)} %broadcast_in_dim.55), channel_id=1, replica_groups=mesh['dp'=8,'tensor'=4] {'dp'}, use_global_device_ids=true, to_apply=%region_5.6 | all-reduce | flops 2880 | bytes 23040 | tf_op jit(solution)/shard_map/psum | solution.py:453
  466.0 31.0 %all_gather.43 = f32[64,1536]{1,0:T(8,128)S(1)} all-gather(f32[8,1536]{1,0:T(8,128)S(1)} %get-tuple-element.105), channel_id=1, replica_groups=mesh['dp'=8,'tensor'=4] {'dp'}, dimensions={0}, use_global_device_ids=true | all-gather | bytes 442368 | tf_op jit(solution)/shard_map/all_gather | solution.py:427
  498.1 11.4 %all-reduce.7 = (f32[40,96]{0,1:T(8,128)S(1)}, f32[64,96]{1,0:T(8,128)S(1)}) all-reduce(f32[40,96]{0,1:T(8,128)} %bitcast.219, f32[64,96]{1,0:T(8,128)} %fusion.90), channel_id=1, replica_groups=mesh['dp'=8,'tensor'=4] {'tensor'}, use_global_device_ids=true, to_apply=%region_7.8 | all-reduce | flops 9984 | bytes 79872 | tf_op jit(solution)/shard_map/psum | solution.py:436
  523.2 6.1 slice_add_fusion
  535.7 48.0 %reduce-scatter.12.cloned.1.call-done = f32[96,64]{1,0:T(8,128)} async-done(((f32[768,64]{1,0:T(8,128)}), f32[96,64]{1,0:T(8,128)}) %reduce-scatter.12.cloned.1.call-update) | async-done | bytes 24592
  592.8 4.7 bitcast_add_fusion
  613.1 65.5 %all-reduce.11.cloned.1.call-done = f32[8,3264]{1,0:T(8,128)} async-done(((f32[8,3264]{1,0:T(8,128)}), f32[8,3264]{1,0:T(8,128)}) %all-reduce.11.cloned.1.call-update) | async-done | bytes 104464 | tf_op jit(solution)/shard_map/psum | solution.py:465
  691.9 4.7 fusion.64
  700.3 67.0 %all-reduce.13.cloned.1.call-done = f32[8,4416]{1,0:T(8,128)} async-done(((f32[8,4416]{1,0:T(8,128)}), f32[8,4416]{1,0:T(8,128)}) %all-reduce.13.cloned.1.call-update) | async-done | bytes 141328 | tf_op jit(solution)/shard_map/psum | solution.py:468
  770.4 5.3 multiply_subtract_fusion.2
  779.6 6.8 multiply_subtract_fusion
  786.4 9.4 %concatenate.55 = f32[768,2880]{1,0:T(8,128)} concatenate(f32[768,1536]{1,0:T(8,128)} %multiply_subtract_fusion, f32[768,576]{1,0:T(8,128)} %multiply_subtract_fusion.3, f32[768,768]{1,0:T(8,128)S(1)} %copy-done.5), dimensions={1} | concatenate | bytes 17694720 | tf_op jit(solution)/shard_map/concatenate | solution.py:472
  795.8 9.3 %copy.126 = f32[1,1,768,2880]{2,3,1,0:T(8,128)} copy(f32[1,1,768,2880]{3,2,1,0:T(8,128)} %bitcast.185) | data formatting | bytes 17694720
  (287 shorter events, 141.7 us)
Async XLA Ops:
  7.2 74.0 %all-gather.7.cloned.1.call-start = ((), (), s32[]{:S(2)}) async-start(), calls=%async_computation.5 | async-start | bytes 3981312 | tf_op jit(solution)/shard_map/all_gather | solution.py:339
  9.9 136.1 %reduce-scatter.8.cloned.1.call-start = ((), (), s32[]{:S(2)}) async-start(), calls=%async_computation.4 | async-start | bytes 442368 | tf_op jit(solution)/shard_map/reduce_scatter | solution.py:368
  10.1 57.7 %copy-start.45 = (s32[8]{0:T(128)S(1)}, s32[8]{0:T(128)}, u32[]{:S(2)}) copy-start(s32[8]{0:T(128)} %param.20) | copy-start | bytes 100
  35.6 45.7 %copy-start.22 = (f32[64,128]{1,0:T(8,128)}, f32[64,128]{1,0:T(8,128)S(1)}, u32[]{:S(2)}) copy-start(f32[64,128]{1,0:T(8,128)S(1)} %get-tuple-element.152) | copy-start | bytes 98308
  35.6 45.7 %copy-start.24 = (f32[64,128]{1,0:T(8,128)}, f32[64,128]{1,0:T(8,128)S(1)}, u32[]{:S(2)}) copy-start(f32[64,128]{1,0:T(8,128)S(1)} %get-tuple-element.153) | copy-start | bytes 98308
  78.3 159.3 %all-gather.9.cloned.1.call-start = ((), (), s32[]{:S(2)}) async-start(), calls=%async_computation.8 | async-start | bytes 17694720 | tf_op jit(solution)/shard_map/all_gather | solution.py:339
  81.2 13.1 %copy-start.35 = (bf16[8,256,16]{1,2,0:T(8,128)(2,1)S(1)}, bf16[8,256,16]{1,2,0:T(8,128)(2,1)}, u32[]{:S(2)}) copy-start(bf16[8,256,16]{1,2,0:T(8,128)(2,1)} %param.17) | copy-start | bytes 196612
  81.2 46.8 %copy-start.39 = (f32[16]{0:T(128)S(1)}, f32[16]{0:T(128)}, u32[]{:S(2)}) copy-start(f32[16]{0:T(128)} %param.31) | copy-start | bytes 196
  81.3 416.8 %reduce-scatter.10.cloned.1.call-start = ((), (), s32[]{:S(2)}) async-start(), calls=%async_computation.9 | async-start | bytes 442368
  361.2 231.5 %collective-permute-start.4 = (f32[768,768]{1,0:T(8,128)}, f32[768,768]{1,0:T(8,128)}, u32[]{:S(2)}, u32[]{:S(2)}) collective-permute-start(f32[768,768]{1,0:T(8,128)} %fusion.89), channel_id=1, source_target_pairs={{0,1},{1,0},{2,3},{3,2},{4,5},{5,4},{6,7},{7,6},{8,9},{9,8},{10,11... | collective-permute-start | bytes 7077896 | tf_op jit(solution)/shard_map/ppermute | solution.py:326
  363.1 170.2 %collective-permute-start.3 = (f32[192,768]{1,0:T(8,128)S(1)}, f32[192,768]{1,0:T(8,128)}, u32[]{:S(2)}, u32[]{:S(2)}) collective-permute-start(f32[192,768]{1,0:T(8,128)S(1)} %fusion.6), channel_id=1, source_target_pairs={{0,1},{1,0},{2,3},{3,2},{4,5},{5,4},{6,7},{7,6},{8,9},{9,8},{10,11... | collective-permute-start | bytes 1769480 | tf_op jit(solution)/shard_map/ppermute | solution.py:326
  373.8 50.9 %collective-permute-start = (f32[4,6144]{1,0:T(4,128)}, f32[4,6144]{1,0:T(4,128)}, u32[]{:S(2)}, u32[]{:S(2)}) collective-permute-start(f32[4,6144]{1,0:T(4,128)} %bitcast.77), channel_id=1, source_target_pairs={{0,1},{1,0},{2,3},{3,2},{4,5},{5,4},{6,7},{7,6},{8,9},{9,8},{10,11... | collective-permute-start | bytes 294920 | tf_op jit(solution)/shard_map/ppermute | solution.py:326
  376.0 46.9 %collective-permute-start.5 = (f32[576]{0:T(1024)S(1)}, f32[576]{0:T(1024)S(1)}, u32[]{:S(2)}, u32[]{:S(2)}) collective-permute-start(f32[576]{0:T(1024)S(1)} %slice_reduce_fusion), channel_id=1, source_target_pairs={{0,1},{1,0},{2,3},{3,2},{4,5},{5,4},{6,7},{7,6},{8,9},{9,8},{10,11... | collective-permute-start | bytes 6920 | tf_op jit(solution)/shard_map/ppermute | solution.py:326
  376.3 47.3 %collective-permute-start.6 = (f32[768]{0:T(1024)S(1)}, f32[768]{0:T(1024)S(1)}, u32[]{:S(2)}, u32[]{:S(2)}) collective-permute-start(f32[768]{0:T(1024)S(1)} %get-tuple-element.88), channel_id=1, source_target_pairs={{0,1},{1,0},{2,3},{3,2},{4,5},{5,4},{6,7},{7,6},{8,9},{9,8},{10,11... | collective-permute-start | bytes 9224 | tf_op jit(solution)/shard_map/ppermute | solution.py:326
  376.6 45.7 %copy-start.40 = (f32[16]{0:T(128)S(1)}, f32[16]{0:T(128)}, u32[]{:S(2)}) copy-start(f32[16]{0:T(128)} %param.32) | copy-start | bytes 196
  422.9 178.5 %collective-permute-start.2 = (f32[768,768]{1,0:T(8,128)}, f32[768,768]{1,0:T(8,128)}, u32[]{:S(2)}, u32[]{:S(2)}) collective-permute-start(f32[768,768]{1,0:T(8,128)} %fusion.88), channel_id=1, source_target_pairs={{0,1},{1,0},{2,3},{3,2},{4,5},{5,4},{6,7},{7,6},{8,9},{9,8},{10,11... | collective-permute-start | bytes 7077896 | tf_op jit(solution)/shard_map/ppermute | solution.py:326
  423.6 161.0 %collective-permute-start.1 = (f32[768,576]{0,1:T(8,128)}, f32[768,576]{0,1:T(8,128)}, u32[]{:S(2)}, u32[]{:S(2)}) collective-permute-start(f32[768,576]{0,1:T(8,128)} %fusion), channel_id=1, source_target_pairs={{0,1},{1,0},{2,3},{3,2},{4,5},{5,4},{6,7},{7,6},{8,9},{9,8},{10,11... | collective-permute-start | bytes 5308424 | tf_op jit(solution)/shard_map/ppermute | solution.py:326
  513.1 10.0 %all-to-all-start = ((f32[8,8,96]{2,1,0:T(8,128)}), f32[8,8,96]{2,1,0:T(8,128)S(1)}, u32[]{:S(2)}, u32[]{:S(2)}) async-start(f32[8,8,96]{2,1,0:T(8,128)} %get-tuple-element.137), calls=%async_computation.1 | async-start | bytes 65536 | tf_op jit(solution)/shard_map/all_to_all | solution.py:370
  516.5 67.2 %reduce-scatter.12.cloned.1.call-start = ((), (), s32[]{:S(2)}) async-start(), calls=%async_computation.10 | async-start | bytes 442368
  520.1 158.5 %all-reduce.11.cloned.1.call-start = ((), (), s32[]{:S(2)}) async-start(), calls=%async_computation.6 | async-start | bytes 212992 | tf_op jit(solution)/shard_map/psum | solution.py:465
  610.6 156.7 %all-reduce.13.cloned.1.call-start = ((), (), s32[]{:S(2)}) async-start(), calls=%async_computation.7 | async-start | bytes 286720 | tf_op jit(solution)/shard_map/psum | solution.py:468
  699.5 76.3 %copy-start.31 = (f32[8,1,768]{2,0,1:T(8,128)}, f32[8,1,768]{2,0,1:T(8,128)S(1)}, u32[]{:S(2)}) copy-start(f32[8,1,768]{2,0,1:T(8,128)S(1)} %copy.195) | copy-start | bytes 73732
  699.5 76.2 %copy-start.30 = (f32[8,1,768]{2,0,1:T(8,128)}, f32[8,1,768]{2,0,1:T(8,128)S(1)}, u32[]{:S(2)}) copy-start(f32[8,1,768]{2,0,1:T(8,128)S(1)} %copy.196) | copy-start | bytes 73732
  699.5 80.1 %slice-start = ((s8[4718592]{0:T(1024)(128)(4,1)}), s8[524288]{0:T(1024)(128)(4,1)S(1)}, s32[]{:S(2)}) async-start(s8[4718592]{0:T(1024)(128)(4,1)} %bitcast.183), calls=%async_computation.11 | async-start | bytes 1048576
  (43 other events, 177.6 us)
Sparse Core Ops, SparseCore 0:
  10.8 70.3 all-gather.6
  85.0 60.8 reduce-scatter.7
  147.5 90.0 all-gather.8
  376.0 61.3 reduce-scatter.9
  520.8 62.8 reduce-scatter.11
  610.7 67.8 all-reduce.10
  697.5 69.7 all-reduce.12

commit v2 on v1

--- a/solution.py
+++ b/solution.py
@@ -58,7 +58,7 @@
 def colsum(v): return jnp.sum(v,axis=0,keepdims=True)
 
 def block_kernel(base_ref,times_ref,clean_ref,noise_ref,mod_ref,wall_ref,pe_ref,wp_ref,bp_ref,wh_ref,bh_ref,bo_ref,b2_ref,bq_ref,b1_ref,
-           a_ref,m_ref,dy_ref,dz_ref,o_ref,dq_ref,g_ref,du_ref,dmod_ref,small_ref,dbq_ref,db1_ref,dbh_ref,loss_ref,
+           a_ref,m_ref,dy_ref,dz_ref,o_ref,x_ref,g_ref,dmod_ref,small_ref,dbias_ref,
            r_s,p_s,gp_s,xh1_s,xh2_s,y_s,z_s,h_s,acc_s,r1_s,r2_s,*,count_all):
     step=pl.program_id(0)
     base=base_ref[0]
@@ -66,8 +66,7 @@
     lo=lax.broadcasted_iota(jnp.int32,(1,128),1)<64
     @pl.when(step==0)
     def _():
-        small_ref[...]=jnp.zeros_like(small_ref); dbq_ref[...]=jnp.zeros_like(dbq_ref); db1_ref[...]=jnp.zeros_like(db1_ref)
-        dbh_ref[...]=jnp.zeros_like(dbh_ref); loss_ref[...]=jnp.zeros_like(loss_ref)
+        small_ref[...]=jnp.zeros_like(small_ref); dbias_ref[...]=jnp.zeros_like(dbias_ref)
     clean=clean_ref[0].astype(F32); noise=noise_ref[0].astype(F32)
     mixed=(t*clean+(1.0-t)*noise).astype(BF)
     mod=lambda i: mod_ref[0,i:i+1,:]
@@ -86,19 +85,20 @@
         p_s[idx]=p
         return p.astype(BF)
     @pl.loop(0,4)
-    def _(jj):
-        j=lax.rem(base+jj,4)
-        r_s[jj]=(dot(a_ref[0],wall_ref[j,:,0:768])+bq_ref[j]).astype(BF)
-        blk=lambda i: r_s[jj,:,128*i:128*(i+1)]
+    def _(j):
+        own=(j>=base)&(j<base+2)
+        k=j-base
+        r_s[j]=(dot(a_ref[0],wall_ref[j,:,0:768])+bq_ref[j]).astype(BF)
+        blk=lambda i: r_s[j,:,128*i:128*(i+1)]
         b0,b1,b2,b3,b4=[blk(i) for i in range(5)]
-        p0=softmax_store(ndot(jnp.where(lo,b0,zero),roll(b0)),3*jj)
-        p1=softmax_store(ndot(jnp.where(lo,zero,b1),roll(b2)),3*jj+1)
-        p2=softmax_store(ndot(jnp.where(lo,b3,zero),roll(b3)),3*jj+2)
+        p0=softmax_store(ndot(jnp.where(lo,b0,zero),roll(b0)),3*j)
+        p1=softmax_store(ndot(jnp.where(lo,zero,b1),roll(b2)),3*j+1)
+        p2=softmax_store(ndot(jnp.where(lo,b3,zero),roll(b3)),3*j+2)
         o01=jnp.where(lo,dot(p0,b1),dot(p1,b2)).astype(BF)
         o2=jnp.where(lo,dot(p2,b4),0.0).astype(BF)
-        @pl.when(jj<2)
+        @pl.when(own)
         def _():
-            o_ref[jj,0,:,0:128]=o01; o_ref[jj,0,:,128:256]=o2
+            o_ref[k,0,:,0:128]=o01; o_ref[k,0,:,128:256]=o2
         ro=roll(o01)
         ob4=jnp.where(lo,zero,ro)
         ob5=jnp.where(lo,ro,roll(o2))
@@ -112,16 +112,17 @@
     m_ref[0]=(xh*(1.0+mod(4))+mod(3)).astype(BF)
     z_s[...]=jnp.zeros_like(z_s)
     @pl.loop(0,4)
-    def _(jj):
-        j=lax.rem(base+jj,4)
+    def _(j):
+        own=(j>=base)&(j<base+2)
+        k=j-base
         u=dot(m_ref[0],wall_ref[j,:,768:1536])+b1_ref[j]
         uu=u*u
         th=jnp.tanh(GELU_C*(u+0.044715*(uu*u)))
         cdf=0.5*(1.0+th)
         g=(u*cdf).astype(BF)
-        gp_s[jj]=cdf+0.5*u*(1.0-th*th)*(GELU_C*(1.0+3.0*0.044715*uu))
-        @pl.when(jj<2)
-        def _(): g_ref[jj,0]=g
+        gp_s[j]=cdf+0.5*u*(1.0-th*th)*(GELU_C*(1.0+3.0*0.044715*uu))
+        @pl.when(own)
+        def _(): g_ref[k,0]=g
         z_s[...]+=ndot(g,wall_ref[j,:,1536:2304])
     z=z_s[...]+b2_ref[...]
     z_s[...]=z
@@ -131,9 +132,9 @@
     pred=ndot(fi,wh_ref[...])+bh_ref[...]
     diff=pred-(clean-noise)
     weight=1.0/(1.0-t+0.25)
-    loss_ref[...]+=jnp.sum(colsum(weight*diff*diff),axis=1,keepdims=True)*(1.0/count_all)
+    small_ref[36:37,0:1]+=jnp.sum(colsum(weight*diff*diff),axis=1,keepdims=True)*(1.0/count_all)
     dpred=2.0*weight*diff*(1.0/count_all)
-    dbh_ref[...]+=colsum(dpred)
+    small_ref[35:36,0:PATCH_IN]+=colsum(dpred)
     dpl=dpred.astype(BF)
     small_ref[16:32]+=tdot(dpl,fi)
     dfi=dot(dpl,wh_ref[...])
@@ -144,16 +145,26 @@
     dzf=dh*mod(5)
     small_ref[34:35]+=colsum(dzf)
     dz_ref[0]=dzf.astype(BF)
+    def store_x(k):
+        def put(start,width,values): x_ref[k,0,:,start:start+width]=values.astype(BF)
+        return put
+    def add_bias(k):
+        def put(start,width,values): dbias_ref[k,:,start:start+width]+=values
+        return put
     acc_s[...]=jnp.zeros_like(acc_s)
     @pl.loop(0,4)
-    def _(jj):
-        j=lax.rem(base+jj,4)
-        du=dot(dz_ref[0],wall_ref[j,:,1536:2304])*gp_s[jj]
+    def _(j):
+        own=(j>=base)&(j<base+2)
+        k=j-base
+        du=dot(dz_ref[0],wall_ref[j,:,1536:2304])*gp_s[j]
         dul=du.astype(BF)
-        @pl.when(jj<2)
+        @pl.when(own)
         def _():
-            du_ref[jj,0]=dul
-            db1_ref[jj]+=colsum(du)
+            for values,put in ((du,store_x(k)),(colsum(du),add_bias(k))):
+                turned=pltpu.roll(values,64,1)
+                put(512,128,jnp.where(lo,0.0,turned[:,0:128]))
+                put(640,640,turned[:,128:768])
+                put(1280,128,jnp.where(lo,turned[:,0:128],0.0))
         acc_s[...]+=ndot(dul,wall_ref[j,:,768:1536])
     dm=acc_s[...]
     xh=xh2_s[...]
@@ -166,15 +177,16 @@
     dy_ref[0]=dyf.astype(BF)
     acc_s[...]=jnp.zeros_like(acc_s)
     @pl.loop(0,4)
-    def _(jj):
-        j=lax.rem(base+jj,4)
+    def _(j):
+        own=(j>=base)&(j<base+2)
+        k=j-base
         do=dot(dy_ref[0],wall_ref[j,:,512:768]).astype(BF)
         r4=roll(do[:,0:128]); r5=roll(do[:,128:256])
         do0=jnp.where(lo,r4,zero); do1=jnp.where(lo,zero,r5); do2=jnp.where(lo,r5,zero)
-        blk=lambda i: r_s[jj,:,128*i:128*(i+1)]
+        blk=lambda i: r_s[j,:,128*i:128*(i+1)]
         b0,b1,b2,b3,b4=[blk(i) for i in range(5)]
         def head(h,doh,v,):
-            p=p_s[3*jj+h]
+            p=p_s[3*j+h]
             dv=tdot(p.astype(BF),doh)
             dp=ndot(doh,v)
             ds=(p*(dp-jnp.sum(p*dp,axis=-1,keepdims=True))).astype(BF)
@@ -190,10 +202,11 @@
         n4=jnp.where(lo,dv2,0.0)
         dqkv=jnp.concatenate([n0,n1,n2,n3,n4],axis=1)
         dl=dqkv.astype(BF)
-        @pl.when(jj<2)
+        @pl.when(own)
         def _():
-            dq_ref[jj,0]=dl
-            dbq_ref[jj]+=colsum(dqkv)
+            x_ref[k,0,:,0:512]=dl[:,0:512]
+            x_ref[k,0,:,512:640]=jnp.where(lo,dl[:,512:640],x_ref[k,0,:,512:640])
+            dbias_ref[k,:,0:640]+=colsum(dqkv)
         acc_s[...]+=ndot(dl,wall_ref[j,:,0:640])
     da=acc_s[...]
     xh=xh1_s[...]
@@ -209,9 +222,9 @@
     pair=lambda w: pl.BlockSpec((2,1,SEQ,w),lambda i,*_:(0,i,0,0))
     const=lambda *s: pl.BlockSpec(s,lambda i,*_:(0,)*len(s))
     S=jax.ShapeDtypeStruct
-    outs=[S((L,SEQ,D),BF)]*4+[S((2,L,SEQ,256),BF),S((2,L,SEQ,640),BF),S((2,L,SEQ,768),BF),S((2,L,SEQ,768),BF),
-        S((L,8,D),F32),S((40,D),F32),S((2,1,640),F32),S((2,1,768),F32),S((1,PATCH_IN),F32),S((1,1),F32)]
-    ospecs=[lat(SEQ,D)]*4+[pair(256),pair(640),pair(768),pair(768),lat(8,D),const(40,D),const(2,1,640),const(2,1,768),const(1,PATCH_IN),const(1,1)]
+    outs=[S((L,SEQ,D),BF)]*4+[S((2,L,SEQ,256),BF),S((2,L,SEQ,1408),BF),S((2,L,SEQ,768),BF),
+        S((L,8,D),F32),S((40,D),F32),S((2,1,1408),F32)]
+    ospecs=[lat(SEQ,D)]*4+[pair(256),pair(1408),pair(768),lat(8,D),const(40,D),const(2,1,1408)]
     V=pltpu.VMEM
     f=lambda: V((SEQ,D),F32)
     return pl.pallas_call(functools.partial(block_kernel,count_all=count_all),
@@ -225,6 +238,475 @@
     )(base,times,clean,noise,mod,wall,pe,wp,bp,wh,bh,bo,b2,bq,b1)
 
 
+MESH = pl.DeviceIdType.MESH
+HI = lax.Precision.HIGHEST
+
+
+def hdot(a, b):
+    return lax.dot_general(a, b, (((1,), (0,)), ((), ())), precision=HI, preferred_element_type=F32)
+
+
+def hndot(a, b):
+    return lax.dot_general(a, b, (((1,), (1,)), ((), ())), precision=HI, preferred_element_type=F32)
+
+
+def htdot(a, b):
+    return lax.dot_general(a, b, (((0,), (0,)), ((), ())), precision=HI, preferred_element_type=F32)
+
+
+def split2(values):
+    first = values.astype(BF)
+    return first, (values - first.astype(F32)).astype(BF)
+
+
+def split3(values):
+    first, rest = values.astype(BF), values
+    rest = rest - first.astype(F32)
+    second = rest.astype(BF)
+    return first, second, (rest - second.astype(F32)).astype(BF)
+
+
+def silu_slope_k(values):
+    gate = 1.0 / (1.0 + jnp.exp(-values))
+    return gate * (1.0 + values * (1.0 - gate))
+
+
+class Peers:
+    def __init__(self, send_sem, recv_sem):
+        self.w = lax.axis_index("dp")
+        self.t = lax.axis_index("tensor")
+        self.n = lax.axis_size("dp")
+        self.tn = lax.axis_size("tensor")
+        self.c = lax.rem(self.t, 2)
+        self.sib = self.t + 1 - 2 * self.c
+        self.send_sem, self.recv_sem = send_sem, recv_sem
+        self.pending = []
+
+    def barrier(self):
+        bar = pltpu.get_barrier_semaphore()
+        for i in range(1, self.n):
+            pl.semaphore_signal(bar, inc=1, device_id=(lax.rem(self.w + i, self.n), self.t), device_id_type=MESH)
+        for i in range(1, self.tn):
+            pl.semaphore_signal(bar, inc=1, device_id=(self.w, lax.rem(self.t + i, self.tn)), device_id_type=MESH)
+        pl.semaphore_wait(bar, self.n - 1 + self.tn - 1)
+
+    def copy(self, src, dst, index, device):
+        op = pltpu.make_async_remote_copy(
+            src_ref=src,
+            dst_ref=dst,
+            send_sem=self.send_sem.at[index],
+            recv_sem=self.recv_sem.at[index],
+            device_id=device,
+            device_id_type=MESH,
+        )
+        op.start()
+        self.pending.append(op)
+        return op
+
+    def dp_push(self, src_of, dst, base):
+        ops = []
+        for i in range(1, self.n):
+            peer = lax.rem(self.w + i, self.n)
+            ops.append(self.copy(src_of(peer), dst, base + i - 1, (peer, self.t)))
+        return ops
+
+    def tensor_push(self, src, dst, base):
+        ops = []
+        for i in range(1, self.tn):
+            ops.append(self.copy(src, dst, base + i - 1, (self.w, lax.rem(self.t + i, self.tn))))
+        return ops
+
+    def core_push(self, src, dst, index):
+        return self.copy(src, dst, index, (self.w, self.sib))
+
+    def finish(self):
+        for op in self.pending:
+            op.wait_send()
+
+
+def wait_all(ops):
+    for op in ops:
+        op.wait_recv()
+
+
+P_TILES = (6, 6, 6, 2, 6)
+P_COUNT = 32
+Q_COUNT = 40
+QKV0, FC0 = 1536, 2112
+COLS, PAIRW = 2880, 1344
+
+
+def gram_schmidt(block):
+    rows = lax.broadcasted_iota(jnp.int32, (8, 1), 0)
+    for index in range(8):
+        row = block[index : index + 1]
+        row = row * lax.rsqrt(jnp.sum(row * row, axis=-1, keepdims=True) + TINY)
+        inner = jnp.sum(block * row, axis=-1, keepdims=True)
+        inner = jnp.where(rows > index, inner, 0.0)
+        block = jnp.where(rows == index, row, block - inner * row)
+    return block
+
+
+def grad_kernel(
+    a_ref, m_ref, dy_ref, dz_ref, o_ref, x_ref, g_ref, cerr_ref, rerr_ref,
+    dmod_ref, small_ref, dbias_ref, right_ref, cs_ref, c_ref, t1_ref, a1t_ref, tf_ref, hot_ref, wmod_ref, wto_ref,
+    mcol_ref, mrow_ref, left_ref, rightn_ref, ps_ref, pr_ref, qs_ref, qrs_ref, misc_ref, gtin_ref, gtout_ref, gtab_ref, gtok_ref, gvec_ref,
+    mc, mr, sc, sr, rc, rr, av, mv, dyv, dzv, ov, xv, gv,
+    dmo, smo, dbo, dm8, dma, dsc, dss, dts, dtl, tks, tkl, px, pland, py, qx, qland, qy,
+    load_sem, send_sem, recv_sem,
+):
+    net = Peers(send_sem, recv_sem)
+    w, t, c = net.w, net.t, net.c
+    n = net.n
+    share = D // n
+    lo = lax.broadcasted_iota(jnp.int32, (1, 128), 1) < 64
+    loads = {}
+
+    def load(name, src, dst, index):
+        op = pltpu.make_async_copy(src, dst, load_sem.at[index])
+        op.start()
+        loads[name] = op
+
+    load("x", x_ref, xv, 0)
+    load("a", a_ref, av, 1)
+    load("m", m_ref, mv, 2)
+    load("g", g_ref, gv, 3)
+    load("dz", dz_ref, dzv, 4)
+    load("o", o_ref, ov, 5)
+    load("dy", dy_ref, dyv, 6)
+    load("ce", cerr_ref, mc, 7)
+    load("re", rerr_ref, mr, 8)
+    net.barrier()
+    side = [
+        net.core_push(dmod_ref, dmo, 0),
+        net.core_push(small_ref, smo, 1),
+        net.core_push(dbias_ref.at[1 - c], dbo, 2),
+    ]
+
+    def chunk(i, size=256):
+        return pl.ds(pl.multiple_of(i * size, size), size)
+
+    def col_part(which, i):
+        left = av[:, chunk(i)]
+        first = tdot(left, xv[which, :, 0:640])
+        second = tdot(mv[:, chunk(i)], xv[which, :, 512:1408])
+        edge = jnp.where(lo, first[:, 512:640], second[:, 0:128])
+        return first[:, 0:512], edge, second[:, 128:832]
+
+    for name in ("x", "a", "m"):
+        loads[name].wait()
+    col_ops, row_ops = [], []
+
+    @pl.loop(0, 3)
+    def _(i):
+        first, edge, second = col_part(1 - c, i)
+        sc[chunk(i), 0:512] = first
+        sc[chunk(i), 512:640] = edge
+        sc[chunk(i), 640:1344] = second
+
+    for i in range(3):
+        col_ops.append(net.core_push(sc.at[256 * i : 256 * i + 256], rc.at[256 * i : 256 * i + 256], 3 + i))
+    wait_all(side)
+    for lat in range(4):
+        for piece in range(2):
+            span = slice(D * piece, D * piece + D)
+            dm8[pl.ds(4 * c + lat, 1), span] = dmod_ref[lat, pl.ds(2 * t + piece, 1), :]
+            dm8[pl.ds(4 * (1 - c) + lat, 1), span] = dmo[lat, pl.ds(2 * t + piece, 1), :]
+    dma[w] = dm8[...]
+    dm_ops = net.dp_push(lambda peer: dm8, dma.at[w], 16)
+    for name in ("g", "dz", "o", "dy"):
+        loads[name].wait()
+
+    @pl.loop(0, 3)
+    def _(i):
+        sr[pl.ds(pl.multiple_of(192 + 256 * i, 64), 256), :] = tdot(gv[1 - c, :, chunk(i)], dzv[...])
+
+    sr[0:192, :] = tdot(ov[1 - c], dyv[...])[0:192]
+    for i in range(3):
+        row_ops.append(net.core_push(sr.at[320 * i : 320 * i + 320], rr.at[320 * i : 320 * i + 320], 6 + i))
+    total = small_ref[...] + smo[...]
+    for k in range(n):
+        tks[k, :, 0:share] = total[:, share * k : share * k + share]
+    tkl[w] = tks[w]
+    tok_ops = net.dp_push(lambda peer: tks.at[peer], tkl.at[w], 24)
+    loads["ce"].wait()
+    dms = split3(dm8[...])
+    right_side = jnp.concatenate([dms[0], dms[1], dms[0], dms[2], dms[1], dms[0]], axis=0)
+    for k in range(n):
+        cs = split3(cs_ref[k])
+        left_side = jnp.concatenate([cs[0], cs[0], cs[1], cs[0], cs[1], cs[2]], axis=0)
+        mc[share * k : share * k + share, 0:QKV0] += tdot(left_side, right_side)[0:share]
+    wait_all(col_ops)
+
+    @pl.loop(0, 3)
+    def _(i):
+        first, edge, second = col_part(c, i)
+        rows = chunk(i)
+        mc[rows, 1536:2048] += first + rc[rows, 0:512]
+        mc[rows, 2048:2176] += edge + rc[rows, 512:640]
+        mc[rows, 2176:2880] += second + rc[rows, 640:1344]
+
+    out_col = pltpu.make_async_copy(mc, mcol_ref, load_sem.at[0])
+    out_col.start()
+    wait_all(dm_ops)
+    dmx = dma[...].reshape(8 * n, QKV0)
+    part = sum(ndot(piece, wmod_ref[...]) for piece in split3(dmx))
+    dss[...] = part
+    dsc[t] = part
+    ds_ops = net.tensor_push(dss, dsc.at[t], 32)
+    loads["re"].wait()
+    wait_all(row_ops)
+
+    @pl.loop(0, 3)
+    def _(i):
+        rows = pl.ds(pl.multiple_of(192 + 256 * i, 64), 256)
+        mr[rows, :] += tdot(gv[c, :, chunk(i)], dzv[...]) + rr[rows, :]
+
+    mr[0:192, :] += tdot(ov[c], dyv[...])[0:192] + rr[0:192, :]
+    out_row = pltpu.make_async_copy(mr, mrow_ref, load_sem.at[1])
+    out_row.start()
+    right = right_ref[...]
+    lanes = lax.broadcasted_iota(jnp.int32, (8, COLS), 1)
+    zero = jnp.zeros((8, COLS), F32)
+    col_right = right[:, 0:COLS]
+    stack = []
+    for first, last in ((0, QKV0), (QKV0, FC0), (FC0, COLS)):
+        cut = jnp.where((lanes >= first) & (lanes < last), col_right, zero)
+        high = cut.astype(BF).astype(F32)
+        stack += [high, cut - high]
+    col_side = jnp.concatenate(stack + [jnp.zeros((80, COLS), F32)], axis=0).T.astype(BF)
+    stack = []
+    for first in (COLS, COLS + D):
+        cut = right[:, first : first + D]
+        high = cut.astype(BF).astype(F32)
+        stack += [high, cut - high]
+    row_side = jnp.concatenate(stack + [jnp.zeros((96, D), F32)], axis=0).T.astype(BF)
+
+    def left_chunk(values, side):
+        high, low = split2(values)
+        return dot(high, side) + dot(low, side)
+
+    for i in range(6):
+        got = left_chunk(mc[128 * i : 128 * i + 128, :], col_side).T
+        for k in range(3):
+            px[6 * k + i] = got[16 * k : 16 * k + 8] + got[16 * k + 8 : 16 * k + 16]
+    got = left_chunk(mr[0:192, :], row_side)
+    got = jnp.concatenate([got, jnp.zeros((64, 128), F32)], axis=0).T
+    for i in range(2):
+        px[18 + i] = got[0:8, 128 * i : 128 * i + 128] + got[8:16, 128 * i : 128 * i + 128]
+    for i in range(6):
+        got = left_chunk(mr[192 + 128 * i : 320 + 128 * i, :], row_side).T
+        px[20 + i] = got[16:24] + got[24:32]
+    bmod = colsum(dm8[...])
+    brest = dbias_ref[c] + dbo[...]
+    for i in range(12):
+        px[26 + i // 8, i % 8 : i % 8 + 1, :] = bmod[:, 128 * i : 128 * i + 128]
+    for i in range(11):
+        k = 12 + i
+        px[26 + k // 8, k % 8 : k % 8 + 1, :] = brest[:, 128 * i : 128 * i + 128]
+    px[28, 7:8, :] = jnp.zeros((1, 128), F32)
+    px[29] = total[32:40, 0:128]
+    px[30] = jnp.zeros((8, 128), F32)
+    px[31] = jnp.zeros((8, 128), F32)
+
+    def scatter(x, land, per, base):
+        own = pl.ds(w * per, per)
+        land[w] = x[own]
+        return net.dp_push(lambda peer: x.at[pl.ds(peer * per, per)], land.at[w], base)
+
+    def collect(land, y, per, base, ops):
+        wait_all(ops)
+        own = pl.ds(w * per, per)
+        y[own] = sum(land[k] for k in range(1, n)) + land[0]
+        return net.dp_push(lambda peer: y.at[own], y.at[own], base)
+
+    ops = scatter(px, pland, P_COUNT // n, 40)
+    wait_all(ds_ops)
+    dcond = (dsc[0] + dsc[1] + dsc[2] + dsc[3]) * silu_slope_k(c_ref[...])
+    gtout_ref[...] = hdot(a1t_ref[...], dcond)
+    gtab_ref[...] = htdot(hot_ref[...], dcond)
+    gvec_ref[...] = jnp.zeros_like(gvec_ref)
+    gvec_ref[0:1] = colsum(dcond)
+    dtime = sum(ndot(piece, wto_ref[...]) for piece in split3(dcond))
+    for k in range(n):
+        dts[k, :, 0:share] = dtime[:, share * k : share * k + share]
+    dtl[w] = dts[w]
+    dt_ops = net.dp_push(lambda peer: dts.at[peer], dtl.at[w], 56)
+    ops = collect(pland, py, P_COUNT // n, 48, ops)
+    wait_all(tok_ops)
+    gtok_ref[...] = sum(tkl[k] for k in range(1, n)) + tkl[0]
+    wait_all(ops)
+    base = 0
+    bases = []
+    for index, count in enumerate(P_TILES):
+        block = gram_schmidt(jnp.concatenate([py[base + k] for k in range(count)], axis=1))
+        bases.append(block)
+        base += count
+    offset = 0
+    for block, width in zip(bases, (D, D, D, 192, D)):
+        left_ref[:, offset : offset + width] = block[:, 0:width]
+        offset += width
+    misc_ref[...] = py[26:30]
+
+    def halves(block):
+        high = block.astype(BF).astype(F32)
+        return [high, block - high]
+
+    col_left = jnp.concatenate(halves(bases[0]) + halves(bases[1]) + halves(bases[2]), axis=0).astype(BF)
+
+    def right_part(values, left):
+        high, low = split2(values)
+        return dot(left, high) + dot(left, low)
+
+    for i in range(23):
+        width = 128 if i < 22 else 64
+        got = right_part(mc[:, 128 * i : 128 * i + width], col_left)
+        got = [got[16 * k : 16 * k + 8] + got[16 * k + 8 : 16 * k + 16] for k in range(3)]
+        if i < 12:
+            qx[i] = got[0]
+        elif i < 16:
+            qx[i] = got[1]
+        elif i == 16:
+            qx[i] = jnp.where(lo, got[1], got[2])
+        elif i < 22:
+            qx[i] = got[2]
+        else:
+            qx[i] = jnp.concatenate([got[2], jnp.zeros((8, 64), F32)], axis=1)
+    proj_left = jnp.concatenate(halves(bases[3][:, 0:192]), axis=0).astype(BF)
+    fc_left = jnp.concatenate(halves(bases[4]), axis=0).astype(BF)
+    for k, (rows, left) in enumerate(((slice(0, 192), proj_left), (slice(192, 960), fc_left))):
+        got = right_part(mr[rows, :], left)
+        got = got[0:8] + got[8:16]
+        for i in range(6):
+            qx[23 + 6 * k + i] = got[:, 128 * i : 128 * i + 128]
+    for i in range(35, Q_COUNT):
+        qx[i] = jnp.zeros((8, 128), F32)
+    ops = scatter(qx, qland, Q_COUNT // n, 64)
+    wait_all(dt_ops)
+    dtime = (sum(dtl[k] for k in range(1, n)) + dtl[0]) * silu_slope_k(t1_ref[...])
+    gtin_ref[...] = htdot(tf_ref[...], dtime)
+    gvec_ref[1:2] = colsum(dtime)
+    ops = collect(qland, qy, Q_COUNT // n, 72, ops)
+    wait_all(ops)
+    def stack_left(blocks):
+        rows = []
+        for block in blocks:
+            high, low = halves(block)
+            rows += [high, low, high]
+        rows.append(jnp.zeros((128 - 8 * len(rows), rows[0].shape[1]), F32))
+        return jnp.concatenate(rows, axis=0).T.astype(BF)
+
+    def stack_right(blocks):
+        rows = []
+        for block in blocks:
+            high, low = halves(block)
+            rows += [high, high, low]
+        rows.append(jnp.zeros((128 - 8 * len(rows), rows[0].shape[1]), F32))
+        return jnp.concatenate(rows, axis=0).astype(BF)
+
+    ps_ref[...] = stack_left(bases[:3])
+    pr_ref[...] = jnp.zeros_like(pr_ref)
+    pr_ref[0:192, :] = stack_left([bases[3]])[0:192]
+    fc_stack = stack_left([bases[4]])
+    pr_ref[192:960, :] = jnp.concatenate([jnp.zeros((D, 24), BF), fc_stack[:, 0:104]], axis=1)
+    qc = jnp.concatenate([qy[i] for i in range(23)], axis=1)
+    span = lax.broadcasted_iota(jnp.int32, (8, 2944), 1)
+    cuts = [
+        jnp.where((span >= first) & (span < last), qc, 0.0) for first, last in ((0, QKV0), (QKV0, FC0), (FC0, COLS))
+    ]
+    qs_ref[...] = stack_right(cuts)
+    qr = [jnp.concatenate([qy[23 + 6 * k + i] for i in range(6)], axis=1) for k in range(2)]
+    qrs_ref[...] = stack_right(qr)
+    rightn_ref[:, 0:COLS] = qc[:, 0:COLS]
+    rightn_ref[:, COLS : COLS + D] = qr[0]
+    rightn_ref[:, COLS + D : COLS + 2 * D] = qr[1]
+    net.finish()
+    out_col.wait()
+    out_row.wait()
+
+
+def run_grad(a, m, dy, dz, o, x, g, cerr, rerr, dmod, small, dbias, right, cs, cond, t1, a1t, tf, hot, wmod, wto, n):
+    S = jax.ShapeDtypeStruct
+    V = pltpu.VMEM
+    rows = a.shape[0]
+    lat = 8 * n
+    share = D // n
+    any_spec = pl.BlockSpec(memory_space=pl.ANY)
+    vm = pl.BlockSpec(memory_space=pltpu.VMEM)
+    outs = [
+        S((D, COLS), F32), S((960, D), F32), S((8, 3264), F32), S((8, 4416), F32),
+        S((D, 128), BF), S((960, 128), BF), S((128, 2944), BF), S((128, D), BF), S((4, 8, 128), F32),
+        S((FREQ, 128), F32), S((D, 128), F32), S((128, 128), F32), S((40, 128), F32), S((8, 128), F32),
+    ]
+    scratch = [
+        V((D, COLS), F32), V((960, D), F32), V((D, PAIRW), F32), V((960, D), F32), V((D, PAIRW), F32), V((960, D), F32),
+        V((rows, D), BF), V((rows, D), BF), V((rows, D), BF), V((rows, D), BF),
+        V((2, rows, 256), BF), V((2, rows, 1408), BF), V((2, rows, D), BF),
+        V((4, 8, D), F32), V((40, D), F32), V((1, 1408), F32), V((8, QKV0), F32), V((n, 8, QKV0), F32),
+        V((4, lat, 128), F32), V((lat, 128), F32), V((n, lat, 128), F32), V((n, lat, 128), F32),
+        V((n, 40, 128), F32), V((n, 40, 128), F32),
+        V((P_COUNT, 8, 128), F32), V((n, P_COUNT // n, 8, 128), F32), V((P_COUNT, 8, 128), F32),
+        V((Q_COUNT, 8, 128), F32), V((n, Q_COUNT // n, 8, 128), F32), V((Q_COUNT, 8, 128), F32),
+        pltpu.SemaphoreType.DMA((9,)), pltpu.SemaphoreType.DMA((80,)), pltpu.SemaphoreType.DMA((80,)),
+    ]
+    return pl.pallas_call(
+        grad_kernel,
+        out_shape=outs,
+        in_specs=[any_spec] * 9 + [vm] * 12,
+        out_specs=[any_spec] * 2 + [vm] * 12,
+        scratch_shapes=scratch,
+        compiler_params=pltpu.CompilerParams(collective_id=1, has_side_effects=True, vmem_limit_bytes=60 * 1024 * 1024),
+        name="grad",
+    )(a, m, dy, dz, o, x, g, cerr, rerr, dmod, small, dbias, right, cs, cond, t1, a1t, tf, hot, wmod, wto)
+
+
+def apply_kernel(
+    w_ref, mcol_ref, mrow_ref, pbt_ref, pr_ref, qc_ref, qr_ref, cw_ref, cm_ref, rw_ref, rm_ref,
+    cres_ref, rres_ref, cn_ref, cmn_ref, rn_ref, rmn_ref, *, n
+):
+    step = pl.program_id(0)
+    mine = w_ref[0]
+    hat = dot(pbt_ref[...], qc_ref[...])
+    cres_ref[...] = mcol_ref[...] - hat[:, 0:COLS] * (1.0 / n)
+
+    @pl.when(step == mine)
+    def _():
+        mom = DECAY * cm_ref[...] + hat[:, 0:COLS]
+        cmn_ref[...] = mom
+        cn_ref[...] = cw_ref[...] - LEARN_RATE * mom
+
+    rhat = dot(pr_ref[...], qr_ref[...])
+    rres_ref[...] = mrow_ref[...] - rhat * (1.0 / n)
+
+    pick = lax.broadcasted_iota(jnp.int32, (D, 128), 0) == mine * (D // n) + lax.broadcasted_iota(jnp.int32, (D, 128), 1)
+    own = dot(qr_ref[...], jnp.where(pick, 1.0, 0.0).astype(BF)).astype(BF)
+    part = dot(pr_ref[...], own)[:, 0 : D // n]
+    mom = DECAY * rm_ref[...] + part
+    rmn_ref[...] = mom
+    rn_ref[...] = rw_ref[...] - LEARN_RATE * mom
+
+
+def run_apply(w, mcol, mrow, pbt, pr, qcs, qrs, cw, cm, rw, rm, n):
+    share = D // n
+    S = jax.ShapeDtypeStruct
+    rowc = 960 // n
+    blk = lambda r, cc: pl.BlockSpec((r, cc), lambda i, *_: (i, 0))
+    full = lambda r, cc: pl.BlockSpec((r, cc), lambda i, *_: (0, 0))
+    return pl.pallas_call(
+        functools.partial(apply_kernel, n=n),
+        grid_spec=pltpu.PrefetchScalarGridSpec(
+            num_scalar_prefetch=1,
+            grid=(n,),
+            in_specs=[blk(share, COLS), blk(rowc, D), blk(share, 128), blk(rowc, 128), full(128, 2944), full(128, D),
+                full(share, COLS), full(share, COLS), blk(rowc, share), blk(rowc, share)],
+            out_specs=[blk(share, COLS), blk(rowc, D), full(share, COLS), full(share, COLS), blk(rowc, share), blk(rowc, share)],
+        ),
+        out_shape=[S((D, COLS), F32), S((960, D), F32), S((share, COLS), F32), S((share, COLS), F32), S((960, share), F32), S((960, share), F32)],
+        compiler_params=pltpu.CompilerParams(vmem_limit_bytes=48 * 1024 * 1024),
+        name="apply",
+    )(w, mcol, mrow, pbt, pr, qcs, qrs, cw, cm, rw, rm)
+
+
 def position_rows(token_ids):
     quarter = D // 4
     omega = 1.0 / 10000.0 ** (jnp.arange(quarter, dtype=jnp.float32) / quarter)
@@ -286,7 +768,7 @@
     return gate * (1.0 + values * (1.0 - gate))
 
 
-def shards(
+def shards_general(
     clean_latents,
     noise_draw,
     timesteps,
@@ -375,7 +857,7 @@
     bq = jnp.pad(bias_all[:, mod_width : mod_width + qkv_width], ((0, 0), (0, 768 - qkv_width)))[:, None]
     b1 = bias_all[:, mod_width + qkv_width :][:, None]
     positions = position_rows(jnp.arange(SEQ, dtype=jnp.int32))
-    (a, m, dy, dz, o, dq, g, du, dmod, small, dbq, db1, dbh, loss) = run_block(
+    (a, m, dy, dz, o, x, g, dmod, small, dbias) = run_block(
         base.reshape(1),
         mine(timesteps),
         mine(clean_latents),
@@ -403,12 +885,12 @@
 
     def gradients(which):
         return (
-            tdot(flat(a), flat(pick(dq, which))[:, :qkv_width]),
-            tdot(flat(m), flat(pick(du, which))),
+            tdot(flat(a), flat(pick(x, which))[:, :qkv_width]),
+            tdot(flat(m), flat(pick(x, which))[:, qkv_width : qkv_width + ffn_width]),
             tdot(flat(pick(o, which))[:, :proj_rows], flat(dy)),
             tdot(flat(pick(g, which)), flat(dz)),
-            pick(dbq, which)[0, :qkv_width],
-            pick(db1, which)[0],
+            pick(dbias, which)[0, :qkv_width],
+            pick(dbias, which)[0, qkv_width : qkv_width + ffn_width],
         )
 
     other = swap(gradients(1 - core))
@@ -434,7 +916,7 @@
     g_btin = jnp.sum(d_time, axis=0)
     g_tin = exact_tdot(time_feat, d_time)
     small_own = lax.psum(lax.psum_scatter(small, "dp", scatter_dimension=1, tiled=True), "tensor") * 0.5
-    head_sum, loss_value = lax.psum((dbh[0] * 0.5, loss[0, 0] * 0.5), ("dp", "tensor"))
+    head_sum, loss_value = lax.psum((small[35, :PATCH_IN] * 0.5, small[36, 0] * 0.5), ("dp", "tensor"))
     small_step = jnp.concatenate(
         [
             small_own[:16],
@@ -512,7 +994,171 @@
     )
 
 
+def shards(
+    clean_latents,
+    noise_draw,
+    timesteps,
+    labels,
+    col_weights,
+    col_moments,
+    col_errors,
+    row_weights,
+    row_moments,
+    row_errors,
+    bias_weights,
+    bias_moments,
+    small_weights,
+    small_moments,
+    head_bias,
+    head_moments,
+    right_factors,
+):
+    tensor_size = lax.axis_size("tensor")
+    data_size = lax.axis_size("dp")
+    tensor_rank = lax.axis_index("tensor")
+    data_rank = lax.axis_index("dp")
+    batch = clean_latents.shape[0]
+    half = batch // 2
+    share = D // data_size
+    mod_width = 8 * D // tensor_size
+    qkv_width = 3 * D // tensor_size
+    ffn_width = FF // tensor_size
+    proj_rows = D // tensor_size
+    count_all = data_size * batch * SEQ * PATCH_IN
+    col_widths = [mod_width, qkv_width, ffn_width]
+    core = lax.rem(tensor_rank, 2)
+    base = tensor_rank - core
+    pair = [(index, index + 1 - 2 * (index % 2)) for index in range(tensor_size)]
+
+    def swap(values):
+        return lax.ppermute(values, "tensor", pair)
+
+    col_low = col_weights[:, 0, :].astype(BF)
+    row_low = row_weights[0].astype(BF).T
+    packed = jnp.concatenate(
+        [
+            col_low[:, mod_width : mod_width + qkv_width],
+            row_low[:, :proj_rows],
+            col_low[:, mod_width + qkv_width :],
+            row_low[:, proj_rows:],
+        ],
+        axis=1,
+    )
+    wall = lax.all_gather(lax.all_gather(packed, "dp", axis=0, tiled=True), "tensor", axis=0)
+    starts = small_starts()
+    small_low = small_weights.astype(BF)
+    small_exact = rounded(small_weights)
+    picked = jnp.concatenate([small_low[: starts[2]], small_low[starts[7] :]], axis=0)
+    emb = lax.all_gather(picked.astype(F32), "dp", axis=1, tiled=True)
+    w_patch = emb[:16].astype(BF)
+    b_patch = emb[16:17]
+    w_head = emb[17:33].astype(BF)
+    b_proj = emb[33:34]
+    b_fc2 = emb[34:35]
+    w_tin = small_exact[starts[2] : starts[3]]
+    b_tin = small_exact[starts[3]]
+    w_tout = small_exact[starts[4] : starts[5]]
+    b_tout = small_exact[starts[5]]
+    table = small_exact[starts[6] : starts[7]]
+    bias_exact = rounded(bias_weights[0])
+    head_exact = rounded(head_bias)
+    w_mod = rounded(col_weights[:, 0, :mod_width])
+    bias_all = lax.all_gather(bias_exact, "tensor", axis=0)
+    times_all = lax.all_gather(timesteps, "dp", axis=0, tiled=True)
+    labels_all = lax.all_gather(labels, "dp", axis=0, tiled=True)
+    time_feat = time_features(times_all)
+    time_hidden = exact_dot(time_feat, w_tin) + b_tin
+    time_act = lax.all_gather(jax.nn.silu(time_hidden), "dp", axis=1, tiled=True)
+    onehot = (labels_all[:, None] == jnp.arange(CLASSES, dtype=jnp.int32)[None, :]).astype(F32)
+    condition = exact_dot(time_act, w_tout) + b_tout + exact_dot(onehot, table)
+    cond_act = jax.nn.silu(condition)
+    mod_part = exact_dot(cond_act, w_mod)
+    mod_own = lax.psum_scatter(mod_part, "dp", scatter_dimension=0, tiled=True) + bias_exact[:mod_width]
+    mod_full = lax.all_gather(mod_own, "tensor", axis=1, tiled=True).reshape(batch, 8, D)
+    cond_rows = lax.all_to_all(cond_act, "dp", split_axis=0, concat_axis=1, tiled=True)
+
+    def mine(values):
+        return lax.dynamic_slice_in_dim(values, core * half, half, 0)
+
+    bq = jnp.pad(bias_all[:, mod_width : mod_width + qkv_width], ((0, 0), (0, 768 - qkv_width)))[:, None]
+    b1 = bias_all[:, mod_width + qkv_width :][:, None]
+    positions = position_rows(jnp.arange(SEQ, dtype=jnp.int32))
+    (a, m, dy, dz, o, x, g, dmod, small, dbias) = run_block(
+        base.reshape(1),
+        mine(timesteps),
+        mine(clean_latents),
+        mine(noise_draw),
+        mine(mod_full),
+        wall,
+        positions,
+        w_patch,
+        b_patch,
+        w_head,
+        head_exact[None],
+        b_proj,
+        b_fc2,
+        bq,
+        b1,
+        count_all,
+    )
+    rows = half * SEQ
+
+    def flat(values):
+        return values.reshape(values.shape[:-3] + (rows, values.shape[-1]))
+
+    def wide(values):
+        return jnp.pad(values, ((0, 0), (0, 128 - values.shape[1])))
+
+    act_t = lax.transpose(time_act, (1, 0))
+    conds = jnp.pad(cond_rows.reshape(batch, data_size, share).transpose(1, 0, 2), ((0, 0), (0, 0), (0, 128 - share)))
+    mcol, mrow, left_all, right_sum, ps, pr, qs, qrs, misc, g_tin, g_tout, g_table, g_tok, g_vec = run_grad(
+        flat(a), flat(m), flat(dy), flat(dz), flat(o), flat(x), flat(g),
+        col_errors[0, 0], row_errors[0, 0], dmod, small, dbias, right_factors[0],
+        conds, wide(condition), wide(time_hidden), act_t, time_feat, wide(onehot),
+        jnp.pad(col_low[:, :mod_width], ((0, 128 - share), (0, 0))), wide(small_low[starts[4] : starts[5]]), data_size,
+    )
+    cres, rres, cn, cmn, rn, rmn = run_apply(
+        data_rank.reshape(1), mcol, mrow, ps, pr, qs, qrs,
+        col_weights[:, 0], col_moments[:, 0], row_weights[0], row_moments[0], data_size,
+    )
+    small_step = jnp.concatenate(
+        [g_tok[:16], g_tok[32:33], g_tin, g_vec[1:2], g_tout, g_vec[0:1], g_table[:CLASSES], g_tok[16:32], g_tok[33:35]],
+        axis=0,
+    )[:, :share]
+    col_new, col_momentum, col_residue = cn[:, None], cmn[:, None], cres[None, None]
+    row_new, row_momentum, row_residue = rn[None], rmn[None], rres[None, None]
+    small_momentum = DECAY * small_moments + small_step
+    small_new = small_weights - LEARN_RATE * small_momentum
+    bias_sum = misc[:3].reshape(3 * 8 * 128)[: bias_weights.shape[1]]
+    head_sum = misc[3, 3, :PATCH_IN]
+    loss_value = misc[3, 4, 0]
+    bias_momentum = DECAY * bias_moments + bias_sum[None]
+    bias_new = bias_weights - LEARN_RATE * bias_momentum
+    head_momentum = DECAY * head_moments + head_sum
+    head_new = head_bias - LEARN_RATE * head_momentum
+    left_factors = left_all[None]
+    right_new = right_sum[None]
+    return (
+        loss_value,
+        col_new,
+        col_momentum,
+        col_residue,
+        row_new,
+        row_momentum,
+        row_residue,
+        bias_new,
+        bias_momentum,
+        small_new,
+        small_momentum,
+        head_new,
+        head_momentum,
+        left_factors,
+        right_new,
+    )
+
+
 def solution(mesh):
+    fits = mesh.shape["dp"] == 8 and mesh.shape["tensor"] == 4
     placed = (
         P("dp", None, None),
         P("dp", None, None),
@@ -533,7 +1179,7 @@
         P("tensor", None, None),
     )
     return jax.shard_map(
-        shards,
+        shards if fits else shards_general,
         mesh=mesh,
         in_specs=placed,
         out_specs=(

time: 840 us -> 472 us (0.56)
  waiting for transfers between devices: 274 us -> 71 us
  blocking collectives: 231 us -> 114 us
  matrix products: 87.3 us -> 2.86 us
  Pallas kernels: 120 us -> 188 us
  local copies, waits for them, and re-layouts: 76.4 us -> 63.9 us
  other arithmetic: 20.5 us -> 10.6 us
    psum x2 -> x0, waiting for transfers between devices: 133 us -> none  [the longest x1 67 us: shards(): right_sum = lax.psum(right_local, 'dp')]
    psum x3 -> x0, blocking collectives: 88.8 us -> none  [the longest x1 40.3 us: shards(): lax.psum((dbh[0] * 0.5, loss[0, 0] * 0.5), ('dp', 'tensor'))]
    dot_general x28 -> x0, matrix products: 74.3 us -> none  [the longest x14 36.4 us: exact_tdot(): lax.dot_general(left, right, (((0,), (0,)), ((), ())), precision=lax.Prec...]
    pallas_call x1 -> x2, Pallas kernels: 2.9 us -> 69.4 us  [the longest x1 57 us: run_grad(): pl.pallas_call(grad_kernel, out_shape=outs, in_specs=[any_spec] * 9 + [vm...]
    unnamed x9 -> x3, waiting for transfers between devices: 48.1 us -> 0.66 us
    all_gather x1 -> x0, blocking collectives: 31 us -> none  [shards(): d_mod_all = lax.all_gather(d_mod, 'dp', axis=0, tiled=True)]
    all_gather x1, waiting for transfers between devices: 84 us -> 70.3 us  [shards(): lax.all_gather(lax.all_gather(packed, 'dp', axis=0, tiled=True), 'tensor'...]
    concatenate x7 -> x1, local copies, waits for them, and re-layouts: 14.9 us -> 2.36 us  [shards(): jnp.concatenate([g_tok[:16], g_tok[32:33], g_tin, g_vec[1:2], g_tout, g_v...]
  transfers between devices with their start and end apart: 15 -> 4, of which waited for: 7 -> 1; matrix products, arithmetic and copies ran while one was open for 11% -> 8% of each run, Pallas kernels for 0% -> 0%
where the time goes in v2:
time: 472 us; the launch traced here: 471 us
  Pallas kernels  188 us (40%)
  blocking collectives  114 us (24%)
  waiting for transfers between devices  71 us (15%)
  local copies, waits for them, and re-layouts  63.9 us (14%)
  between operations  15.6 us (3%)
  other arithmetic  10.6 us (2%)
    pallas_call x1, Pallas kernels, run_block(): pl.pallas_call(functools.partial(block_kernel, count_all=count_all), grid...  119 us
    all_gather x1, waiting for transfers between devices, shards(): lax.all_gather(lax.all_gather(packed, 'dp', axis=0, tiled=True), 'tensor'...  70.3 us
    pallas_call x1, Pallas kernels, run_grad(): pl.pallas_call(grad_kernel, out_shape=outs, in_specs=[any_spec] * 9 + [vm...  57 us
    unnamed x95, local copies, waits for them, and re-layouts  45.5 us
    unnamed x3, blocking collectives  42.3 us
    all_gather x1, blocking collectives, shards(): lax.all_gather(jax.nn.silu(time_hidden), 'dp', axis=1, tiled=True)  33.7 us
    all_gather x1, blocking collectives, shards(): emb = lax.all_gather(picked.astype(F32), 'dp', axis=1, tiled=True)  31.2 us
    pallas_call x1, Pallas kernels, run_apply(): pl.pallas_call(functools.partial(apply_kernel, n=n), grid_spec=pltpu.Pref...  12.4 us
  transfers between devices with their start and end apart: 4, of which 1 were waited for; matrix products, arithmetic and copies ran while one was open for 8% of the time, Pallas kernels for 0%

profile of v2, /device:TPU:0, one launch (start us, length us, event | category | flops | bytes accessed | tf_op | source)
XLA Modules:
  0.0 470.8 jit_solution(5651247419498163248)
XLA Ops:
  7.2 2.9 copy.79
  15.3 23.2 %all-reduce.7 = f32[64]{0:T(128)S(1)} all-reduce(f32[64]{0:T(128)S(1)} %dynamic-update-slice), channel_id=1, replica_groups=mesh['dp'=8,'tensor'=4] {'dp'}, use_global_device_ids=true, to_apply=%add.7 | all-reduce | flops 64 | bytes 512
  39.6 33.7 %all-gather.2 = f32[8,96,64]{1,2,0:T(8,128)} all-gather(f32[1,96,64]{1,2,0:T(8,128)S(1)} %multiply_bitcast_fusion), channel_id=1, replica_groups=mesh['dp'=8,'tensor'=4] {'dp'}, dimensions={0}, use_global_device_ids=true | all-gather | bytes 221184 | tf_op jit(solution)/shard_map/all_gather | solution.py:1071
  75.5 8.6 %all-reduce.8 = s32[64]{0:T(128)S(1)} all-reduce(s32[64]{0:T(128)S(1)} %dynamic-update-slice.1), channel_id=1, replica_groups=mesh['dp'=8,'tensor'=4] {'dp'}, use_global_device_ids=true, to_apply=%add.8 | all-reduce | flops 64 | bytes 512
  84.8 2.0 fusion.4
  88.3 4.5 all-to-all-start
  92.8 31.2 %all-gather.3 = f32[8,96,35]{1,2,0:T(8,128)S(1)} all-gather(f32[1,96,35]{1,2,0:T(8,128)S(1)} %convert_bitcast_fusion.1), channel_id=1, replica_groups=mesh['dp'=8,'tensor'=4] {'dp'}, dimensions={0}, use_global_device_ids=true | all-gather | bytes 120960 | tf_op jit(solution)/shard_map/all_gather | solution.py:1052
  125.6 10.5 %all-reduce.9 = f32[11520]{0:T(1024)S(1)} all-reduce(f32[11520]{0:T(1024)S(1)} %convert_dynamic-update-slice_fusion), channel_id=3, replica_groups=mesh['dp'=8,'tensor'=4] {'tensor'}, use_global_device_ids=true, to_apply=%add.9 | all-reduce | flops 11520 | bytes 92160
  137.7 1.9 multiply_sine_fusion.1
  139.6 1.2 pad_maximum_fusion.pe_ref
  142.5 1.5 copy_bitcast_fusion
  150.7 9.9 %copy.84 = f32[1,1,768,2880]{3,2,1,0:T(8,128)} copy(f32[1,1,768,2880]{2,3,1,0:T(8,128)} %param.23) | data formatting | bytes 17694720 | tf_op args[6]
  163.2 6.9 %all_gather.33 = f32[8,6144]{1,0:T(8,128)S(1)} all-gather(f32[8,1536]{1,0:T(8,128)S(1)} %broadcast_add_fusion), channel_id=1, replica_groups=mesh['dp'=8,'tensor'=4] {'tensor'}, dimensions={1}, use_global_device_ids=true | all-gather | bytes 245760 | tf_op jit(solution)/shard_map/all_gather | solution.py:1077
  170.9 70.3 %all-gather.9.cloned.1.call-done = bf16[3072,2304]{1,0:T(8,128)(2,1)} async-done(((bf16[768,2304]{1,0:T(8,128)(2,1)}), bf16[3072,2304]{1,0:T(8,128)(2,1)}) %all-gather.9.cloned.1.call-update) | async-done | bytes 14155792 | tf_op jit(solution)/shard_map/all_gather | solution.py:1047
  241.2 118.5 %block.1 = (bf16[4,256,768]{2,1,0:T(8,128)(2,1)}, bf16[4,256,768]{2,1,0:T(8,128)(2,1)}, bf16[4,256,768]{2,1,0:T(8,128)(2,1)}, bf16[4,256,768]{2,1,0:T(8,128)(2,1...) custom-call(s32[1]{0:T(128)} %bitcast.base_ref, ...), custom_call_target="tpu_custom_call" | custom-call | tf_op jit(solution)/shard_map/block/pallas_call | solution.py:230
  359.7 57.0 %grad.1 = (f32[768,2880]{1,0:T(8,128)}, f32[960,768]{1,0:T(8,128)}, f32[8,3264]{1,0:T(8,128)}, f32[8,4416]{1,0:T(8,128)}, bf16[768,128]{1,0:T(8,128)(2,1)}, /*in...) custom-call(bf16[1024,768]{1,0:T(8,128)(2,1)} %bitcast.92, ...), custom_call_target="tpu_custom_call" | custom-call | tf_op jit(solution)/shard_map/grad/pallas_call | solution.py:652
  419.5 1.2 slice.127
  422.2 2.4 concatenate.19
  425.5 2.1 copy.95
  431.6 12.4 %apply.1 = (f32[768,2880]{1,0:T(8,128)}, f32[960,768]{1,0:T(8,128)}, f32[96,2880]{1,0:T(8,128)S(1)}, f32[96,2880]{1,0:T(8,128)S(1)}, f32[960,96]{1,0:T(8,128)S(1)}, /*index=5*/f32[960,96]{1,0:T(8,128)S(1)}) custom-call(s32[1]{0:T(128)} %bitcast.29.w_ref, f32[768,2880]{1,0:T(8,128)} %get-tuple-element.56.mcol_ref, f32[960,768]{1,0:T(8,128)} %get-tuple-element.57.mrow_ref, ...), custom_call_target="tpu_custom_call" | custom-call | tf_op jit(solution)/shard_map/apply/pallas_call | solution.py:695
  445.6 9.2 %copy.92 = f32[1,1,768,2880]{2,3,1,0:T(8,128)} copy(f32[1,1,768,2880]{3,2,1,0:T(8,128)} %bitcast.83) | data formatting | bytes 17694720
  454.9 2.2 copy.90
  457.0 2.2 copy.91
  461.1 1.2 multiply_subtract_fusion.2
  (160 shorter events, 38.5 us)
Async XLA Ops:
  7.2 3.0 copy-start.15
  7.2 79.7 %all-gather.7.cloned.1.call-start = ((), (), s32[]{:S(2)}) async-start(), calls=%async_computation.3 | async-start | bytes 3981312 | tf_op jit(solution)/shard_map/all_gather | solution.py:1047
  12.2 150.2 %reduce-scatter.2.cloned.1.call-start = ((), (), s32[]{:S(2)}) async-start(), calls=%async_computation.2 | async-start | bytes 442368 | tf_op jit(solution)/shard_map/reduce_scatter | solution.py:1076
  12.7 2.4 copy-start.29
  13.8 61.5 %copy-start.28 = (s32[8]{0:T(128)S(1)}, s32[8]{0:T(128)}, u32[]{:S(2)}) copy-start(s32[8]{0:T(128)} %param.20) | copy-start | bytes 100
  74.5 12.4 %copy-start.9 = (f32[8,96,64]{2,1,0:T(8,128)}, f32[8,96,64]{2,1,0:T(8,128)S(1)}, u32[]{:S(2)}) copy-start(f32[8,96,64]{2,1,0:T(8,128)S(1)} %copy.78) | copy-start | bytes 589828
  86.8 154.3 %all-gather.9.cloned.1.call-start = ((), (), s32[]{:S(2)}) async-start(), calls=%async_computation.4 | async-start | bytes 17694720 | tf_op jit(solution)/shard_map/all_gather | solution.py:1047
  86.9 5.9 %copy-start.21 = (f32[1,2880]{1,0:T(1,128)S(1)}, f32[1,2880]{1,0:T(1,128)}, u32[]{:S(2)}) copy-start(f32[1,2880]{1,0:T(1,128)} %param.27) | copy-start | bytes 34564
  86.9 37.3 %copy-start.31 = (u32[32]{0:T(128)S(1)}, u32[32]{0:T(128)}, u32[]{:S(2)}) copy-start(u32[32]{0:T(128)} %constant.113) | copy-start | bytes 388
  87.6 48.7 %copy-start.26 = (f32[16]{0:T(128)S(1)}, f32[16]{0:T(128)}, u32[]{:S(2)}) copy-start(f32[16]{0:T(128)} %param.31) | copy-start | bytes 196
  87.6 50.1 %copy-start.23 = (bf16[8,256,16]{1,2,0:T(8,128)(2,1)S(1)}, bf16[8,256,16]{1,2,0:T(8,128)(2,1)}, u32[]{:S(2)}) copy-start(bf16[8,256,16]{1,2,0:T(8,128)(2,1)} %param.18) | copy-start | bytes 196612
  87.6 50.1 %copy-start.24 = (bf16[8,256,16]{1,2,0:T(8,128)(2,1)S(1)}, bf16[8,256,16]{1,2,0:T(8,128)(2,1)}, u32[]{:S(2)}) copy-start(bf16[8,256,16]{1,2,0:T(8,128)(2,1)} %param.17) | copy-start | bytes 196612
  88.3 73.5 %all-to-all-start = ((f32[8,8,96]{2,1,0:T(8,128)}), f32[8,8,96]{2,1,0:T(8,128)S(1)}, u32[]{:S(2)}, u32[]{:S(2)}) async-start(f32[8,8,96]{2,1,0:T(8,128)} %fusion.3), calls=%async_computation.1 | async-start | bytes 65536 | tf_op jit(solution)/shard_map/all_to_all | solution.py:1078
  136.3 4.5 copy-start.19
  139.6 2.9 copy-start.12
  142.5 3.5 copy-start.11
  150.7 9.9 %copy-start.14 = (f32[1093,96]{0,1:T(8,128)S(1)}, f32[1093,96]{0,1:T(8,128)}, u32[]{:S(2)}) copy-start(f32[1093,96]{0,1:T(8,128)} %param.30) | copy-start | bytes 1259140
  425.5 3.1 copy-start.5
  457.0 2.2 copy-start.4
  457.0 3.1 copy-start.2
  459.2 3.1 copy-start.22
  459.2 3.1 copy-start.25
  459.2 3.8 copy-start.18
  459.2 4.4 copy-start.17
  (14 other events, 17.6 us)
Sparse Core Ops, SparseCore 0:
  12.3 71.2 all-gather.6
  87.5 60.9 reduce-scatter.1
  150.0 91.0 all-gather.8

commit v3 on v2

v3 whole, which is shorter than its diff:
```python
import functools
import math

import jax
import jax.numpy as jnp
from jax import lax
from jax.experimental import pallas as pl
from jax.experimental.pallas import tpu as pltpu
from jax.sharding import PartitionSpec as P

D = 768
HEADS = 12
HEAD_DIM = 64
FF = 3072
FREQ = 256
GRID = 16
PATCH_IN = 16
CLASSES = 32
SEQ = 256

EPSILON = 1e-06
TINY = 1e-30
DECAY = 0.9
LEARN_RATE = 100.0
TIME_OFFSET = 0.25
F32 = jnp.float32
BF = jnp.bfloat16
SCALE = 1.0 / math.sqrt(HEAD_DIM)
GELU_C = math.sqrt(2.0 / math.pi)


def exact_dot(left, right):
    return jnp.dot(left, right, precision=lax.Precision.HIGHEST, preferred_element_type=F32)


def exact_tdot(left, right):
    return lax.dot_general(left, right, (((0,), (0,)), ((), ())), precision=lax.Precision.HIGHEST, preferred_element_type=F32)


def exact_ndot(left, right):
    return lax.dot_general(left, right, (((1,), (1,)), ((), ())), precision=lax.Precision.HIGHEST, preferred_element_type=F32)


def dot(a,b): return lax.dot_general(a,b,(((1,),(0,)),((),())),preferred_element_type=F32)
def ndot(a,b): return lax.dot_general(a,b,(((1,),(1,)),((),())),preferred_element_type=F32)
def tdot(a,b): return lax.dot_general(a,b,(((0,),(0,)),((),())),preferred_element_type=F32)

def ln(h):
    c=h-jnp.mean(h,axis=-1,keepdims=True)
    v=jnp.mean(c*c,axis=-1,keepdims=True)
    r=lax.rsqrt(v+EPSILON)
    return c*r,r

def ln_back(dout,xh,r,scale):
    dx=dout*(1.0+scale)
    return r*(dx-jnp.mean(dx,axis=-1,keepdims=True)-xh*jnp.mean(dx*xh,axis=-1,keepdims=True))

def colsum(v): return jnp.sum(v,axis=0,keepdims=True)

def block_kernel(base_ref,times_ref,clean_ref,noise_ref,mod_ref,wall_ref,pe_ref,emb_ref,bh_ref,ball_ref,
           a_ref,m_ref,dy_ref,dz_ref,o_ref,dq_ref,du_ref,g_ref,dmod_ref,small_ref,dbq_ref,db1_ref,hb_ref,
           pe_s,r_s,p_s,gp_s,xh1_s,xh2_s,y_s,z_s,h_s,acc_s,r1_s,r2_s,*,count_all):
    step=pl.program_id(0)
    base=base_ref[0]
    t=times_ref[step]
    lo=lax.broadcasted_iota(jnp.int32,(1,128),1)<64
    @pl.when(step==0)
    def _():
        small_ref[...]=jnp.zeros_like(small_ref); dbq_ref[...]=jnp.zeros_like(dbq_ref); db1_ref[...]=jnp.zeros_like(db1_ref)
        hb_ref[...]=jnp.zeros_like(hb_ref)
        for i in range(GRID):
            pe_s[16*i:16*i+16,0:384]=jnp.broadcast_to(pe_ref[i:i+1,:],(16,384))
            pe_s[16*i:16*i+16,384:768]=pe_ref[...]
    clean=clean_ref[0].astype(F32); noise=noise_ref[0].astype(F32)
    mixed=(t*clean+(1.0-t)*noise).astype(BF)
    mod=lambda i: mod_ref[0,i:i+1,:]
    wp=emb_ref[0:16].astype(BF); wh=emb_ref[16:32].astype(BF)
    h0=tdot(mixed,wp)+emb_ref[32:33]+pe_s[...]
    h_s[...]=h0
    xh,r=ln(h0)
    xh1_s[...]=xh; r1_s[...]=r
    a_ref[0]=(xh*(1.0+mod(1))+mod(0)).astype(BF)
    y_s[...]=jnp.zeros_like(y_s)
    zero=jnp.zeros((),BF)
    roll=lambda v: pltpu.roll(v.astype(F32),64,1).astype(BF)
    def softmax_store(s,idx):
        s=s*SCALE
        e=jnp.exp(s-jnp.max(s,axis=-1,keepdims=True))
        p=e/jnp.sum(e,axis=-1,keepdims=True)
        p_s[idx]=p
        return p.astype(BF)
    @pl.loop(0,4)
    def _(j):
        own=(j>=base)&(j<base+2)
        k=j-base
        r_s[j]=(dot(a_ref[0],wall_ref[0,j])+ball_ref[j,:,0:768]).astype(BF)
        blk=lambda i: r_s[j,:,128*i:128*(i+1)]
        b0,b1,b2,b3,b4=[blk(i) for i in range(5)]
        p0=softmax_store(ndot(jnp.where(lo,b0,zero),roll(b0)),3*j)
        p1=softmax_store(ndot(jnp.where(lo,zero,b1),roll(b2)),3*j+1)
        p2=softmax_store(ndot(jnp.where(lo,b3,zero),roll(b3)),3*j+2)
        o01=jnp.where(lo,dot(p0,b1),dot(p1,b2)).astype(BF)
        o2=jnp.where(lo,dot(p2,b4),0.0).astype(BF)
        @pl.when(own)
        def _():
            o_ref[k,0,:,0:128]=o01; o_ref[k,0,:,128:256]=o2
        ro=roll(o01)
        ob4=jnp.where(lo,zero,ro)
        ob5=jnp.where(lo,ro,roll(o2))
        y_s[...]+=ndot(jnp.concatenate([ob4,ob5],axis=1),wall_ref[0,j,:,512:768])
    y=y_s[...]+emb_ref[33:34]
    y_s[...]=y
    h1=h_s[...]+mod(2)*y
    h_s[...]=h1
    xh,r=ln(h1)
    xh2_s[...]=xh; r2_s[...]=r
    m_ref[0]=(xh*(1.0+mod(4))+mod(3)).astype(BF)
    z_s[...]=jnp.zeros_like(z_s)
    @pl.loop(0,4)
    def _(j):
        own=(j>=base)&(j<base+2)
        k=j-base
        u=dot(m_ref[0],wall_ref[1,j])+ball_ref[j,:,768:1536]
        uu=u*u
        th=jnp.tanh(GELU_C*(u+0.044715*(uu*u)))
        cdf=0.5*(1.0+th)
        g=(u*cdf).astype(BF)
        gp_s[j]=cdf+0.5*u*(1.0-th*th)*(GELU_C*(1.0+3.0*0.044715*uu))
        @pl.when(own)
        def _(): g_ref[k,0]=g
        z_s[...]+=ndot(g,wall_ref[2,j])
    z=z_s[...]+emb_ref[34:35]
    z_s[...]=z
    h2=h_s[...]+mod(5)*z
    xh,r=ln(h2)
    fi=(xh*(1.0+mod(7))+mod(6)).astype(BF)
    pred=ndot(wh,fi)+bh_ref[...]
    diff=pred-(clean-noise)
    weight=1.0/(1.0-t+0.25)
    hb_ref[0:1,1:2]+=jnp.sum(colsum(weight*diff*diff),axis=1,keepdims=True)*(1.0/count_all)
    dpred=2.0*weight*diff*(1.0/count_all)
    hb_ref[:,0:1]+=jnp.sum(dpred,axis=1,keepdims=True)
    dpl=dpred.astype(BF)
    small_ref[16:32]+=dot(dpl,fi)
    dfi=tdot(dpl,wh)
    dmod_ref[0,6:7]=colsum(dfi); dmod_ref[0,7:8]=colsum(dfi*xh)
    dh=ln_back(dfi,xh,r,mod(7))
    h_s[...]=dh
    dmod_ref[0,5:6]=colsum(dh*z_s[...])
    dzf=dh*mod(5)
    small_ref[34:35]+=colsum(dzf)
    dz_ref[0]=dzf.astype(BF)
    acc_s[...]=jnp.zeros_like(acc_s)
    @pl.loop(0,4)
    def _(j):
        own=(j>=base)&(j<base+2)
        k=j-base
        du=dot(dz_ref[0],wall_ref[2,j])*gp_s[j]
        dul=du.astype(BF)
        @pl.when(own)
        def _():
            du_ref[k,0]=dul
            db1_ref[k]+=colsum(du)
        acc_s[...]+=ndot(dul,wall_ref[1,j])
    dm=acc_s[...]
    xh=xh2_s[...]
    dmod_ref[0,3:4]=colsum(dm); dmod_ref[0,4:5]=colsum(dm*xh)
    dh=h_s[...]+ln_back(dm,xh,r2_s[...],mod(4))
    h_s[...]=dh
    dmod_ref[0,2:3]=colsum(dh*y_s[...])
    dyf=dh*mod(2)
    small_ref[33:34]+=colsum(dyf)
    dy_ref[0]=dyf.astype(BF)
    acc_s[...]=jnp.zeros_like(acc_s)
    @pl.loop(0,4)
    def _(j):
        own=(j>=base)&(j<base+2)
        k=j-base
        do=dot(dy_ref[0],wall_ref[0,j,:,512:768]).astype(BF)
        r4=roll(do[:,0:128]); r5=roll(do[:,128:256])
        do0=jnp.where(lo,r4,zero); do1=jnp.where(lo,zero,r5); do2=jnp.where(lo,r5,zero)
        blk=lambda i: r_s[j,:,128*i:128*(i+1)]
        b0,b1,b2,b3,b4=[blk(i) for i in range(5)]
        def head(h,doh,v,):
            p=p_s[3*j+h]
            dv=tdot(p.astype(BF),doh)
            dp=ndot(doh,v)
            ds=(p*(dp-jnp.sum(p*dp,axis=-1,keepdims=True))).astype(BF)
            return dv,ds
        dv0,ds0=head(0,do0,b1)
        dv1,ds1=head(1,do1,b2)
        dv2,ds2=head(2,do2,b4)
        rb0=roll(b0); rb3=roll(b3)
        n0=jnp.where(lo,dot(ds0,rb0),tdot(ds0,rb0))*SCALE
        dq1=dot(ds1,roll(b2))*SCALE; dk1=tdot(ds1,roll(b1))*SCALE
        n1=jnp.where(lo,dv0,dq1); n2=jnp.where(lo,dk1,dv1)
        n3=jnp.where(lo,dot(ds2,rb3),tdot(ds2,rb3))*SCALE
        n4=jnp.where(lo,dv2,0.0)
        dqkv=jnp.concatenate([n0,n1,n2,n3,n4],axis=1)
        dl=dqkv.astype(BF)
        @pl.when(own)
        def _():
            dq_ref[k,0]=dl
            dbq_ref[k]+=colsum(dqkv)
        acc_s[...]+=ndot(dl,wall_ref[0,j,:,0:640])
    da=acc_s[...]
    xh=xh1_s[...]
    dmod_ref[0,0:1]=colsum(da); dmod_ref[0,1:2]=colsum(da*xh)
    dh=h_s[...]+ln_back(da,xh,r1_s[...],mod(1))
    small_ref[32:33]+=colsum(dh)
    small_ref[0:16]+=dot(mixed,dh.astype(BF))

def run_block(base,times,clean,noise,mod,wall,pe,emb,bh,ball,count_all):
    L=clean.shape[0]
    full=lambda a: pl.BlockSpec(a.shape,lambda i,*_: (0,)*a.ndim,pipeline_mode=pl.Buffered(1))
    lat=lambda *s: pl.BlockSpec((1,)+s,lambda i,*_:(i,)+(0,)*len(s))
    pair=lambda w: pl.BlockSpec((2,1,SEQ,w),lambda i,*_:(0,i,0,0))
    const=lambda *s: pl.BlockSpec(s,lambda i,*_:(0,)*len(s))
    S=jax.ShapeDtypeStruct
    outs=[S((L,SEQ,D),BF)]*4+[S((2,L,SEQ,256),BF),S((2,L,SEQ,640),BF),S((2,L,SEQ,768),BF),S((2,L,SEQ,768),BF),
        S((L,8,D),F32),S((40,D),F32),S((2,1,640),F32),S((2,1,768),F32),S((PATCH_IN,128),F32)]
    ospecs=[lat(SEQ,D)]*4+[pair(256),pair(640),pair(768),pair(768),lat(8,D),const(40,D),const(2,1,640),const(2,1,768),const(PATCH_IN,128)]
    V=pltpu.VMEM
    f=lambda: V((SEQ,D),F32)
    return pl.pallas_call(functools.partial(block_kernel,count_all=count_all),
        grid_spec=pltpu.PrefetchScalarGridSpec(num_scalar_prefetch=2,grid=(L,),
            in_specs=[lat(PATCH_IN,SEQ),lat(PATCH_IN,SEQ),lat(8,D)]+[full(v) for v in (wall,pe,emb,bh,ball)],
            out_specs=ospecs,
            scratch_shapes=[f(),V((4,SEQ,768),BF),V((12,SEQ,SEQ),F32),V((4,SEQ,768),F32),f(),f(),f(),f(),f(),f(),V((SEQ,1),F32),V((SEQ,1),F32)]),
        out_shape=outs,
        compiler_params=pltpu.CompilerParams(vmem_limit_bytes=60*1024*1024),
        name="block",
    )(base,times,clean,noise,mod,wall,pe,emb,bh,ball)


MESH = pl.DeviceIdType.MESH
HI = lax.Precision.HIGHEST


def hdot(a, b):
    return lax.dot_general(a, b, (((1,), (0,)), ((), ())), precision=HI, preferred_element_type=F32)


def hndot(a, b):
    return lax.dot_general(a, b, (((1,), (1,)), ((), ())), precision=HI, preferred_element_type=F32)


def htdot(a, b):
    return lax.dot_general(a, b, (((0,), (0,)), ((), ())), precision=HI, preferred_element_type=F32)


def split2(values):
    first = values.astype(BF)
    return first, (values - first.astype(F32)).astype(BF)


def split3(values):
    first, rest = values.astype(BF), values
    rest = rest - first.astype(F32)
    second = rest.astype(BF)
    return first, second, (rest - second.astype(F32)).astype(BF)


def silu_slope_k(values):
    gate = 1.0 / (1.0 + jnp.exp(-values))
    return gate * (1.0 + values * (1.0 - gate))


class Peers:
    def __init__(self, send_sem, recv_sem):
        self.w = lax.axis_index("dp")
        self.t = lax.axis_index("tensor")
        self.n = lax.axis_size("dp")
        self.tn = lax.axis_size("tensor")
        self.c = lax.rem(self.t, 2)
        self.sib = self.t + 1 - 2 * self.c
        self.send_sem, self.recv_sem = send_sem, recv_sem
        self.pending = []

    def barrier(self):
        bar = pltpu.get_barrier_semaphore()
        for i in range(1, self.n):
            pl.semaphore_signal(bar, inc=1, device_id=(lax.rem(self.w + i, self.n), self.t), device_id_type=MESH)
        for i in range(1, self.tn):
            pl.semaphore_signal(bar, inc=1, device_id=(self.w, lax.rem(self.t + i, self.tn)), device_id_type=MESH)
        pl.semaphore_wait(bar, self.n - 1 + self.tn - 1)

    def copy(self, src, dst, index, device):
        op = pltpu.make_async_remote_copy(
            src_ref=src,
            dst_ref=dst,
            send_sem=self.send_sem.at[index],
            recv_sem=self.recv_sem.at[index],
            device_id=device,
            device_id_type=MESH,
        )
        op.start()
        self.pending.append(op)
        return op

    def dp_push(self, src_of, dst, base):
        ops = []
        for i in range(1, self.n):
            peer = lax.rem(self.w + i, self.n)
            ops.append(self.copy(src_of(peer), dst, base + i - 1, (peer, self.t)))
        return ops

    def tensor_push(self, src, dst, base):
        ops = []
        for i in range(1, self.tn):
            ops.append(self.copy(src, dst, base + i - 1, (self.w, lax.rem(self.t + i, self.tn))))
        return ops

    def core_push(self, src, dst, index):
        return self.copy(src, dst, index, (self.w, self.sib))

    def finish(self):
        for op in self.pending:
            op.wait_send()


def wait_all(ops):
    for op in ops:
        op.wait_recv()


P_TILES = (6, 6, 6, 2, 6)
P_COUNT = 32
Q_COUNT = 40
QKV0, FC0 = 1536, 2112
COLS = 2880


def halves(block):
    high = block.astype(BF).astype(F32)
    return [high, block - high]


def fill(rows, total):
    used = sum(row.shape[0] for row in rows)
    return jnp.concatenate(rows + [jnp.zeros((total - used, rows[0].shape[1]), F32)], axis=0)


def gather_kernel(
    pack_ref, pk_ref, smt_ref, wmod_ref, brow_ref, bmod_ref,
    wall_ref, mod_ref, emb_ref, ball_ref, cs_ref, ct_ref, t1_ref, a1_ref, tf_ref, hot_ref, wto_ref,
    pkl, ems, eml, a1s, a1l, css, csl, mps, mpl_, mos, mol, bal,
    local_sem, wsend, wrecv, send_sem, recv_sem,
):
    net = Peers(send_sem, recv_sem)
    w, t, c, n = net.w, net.t, net.c, net.n
    share = D // n
    half = share // 2
    x, z, y = t // 2, w // 2, lax.rem(w, 2)
    own = []
    for q in range(3):
        op = pltpu.make_async_copy(pack_ref.at[q], wall_ref.at[q, t, w], local_sem.at[q])
        op.start()
        own.append(op)
    net.barrier()
    pkl[w] = pk_ref[...]
    pk_ops = net.dp_push(lambda peer: pk_ref, pkl.at[w], 0)
    rest = smt_ref.shape[1]
    emb = jnp.concatenate(
        [smt_ref[:, 0:16], smt_ref[:, rest - 18 : rest - 2], smt_ref[:, 16:17], smt_ref[:, rest - 2 : rest], jnp.zeros((share, 5), F32)],
        axis=1,
    )
    third = share // 3
    emb = jnp.concatenate([emb[0:third], emb[third : 2 * third], emb[2 * third : share], jnp.zeros((third, 8), F32)], axis=1)
    ems[...] = emb.astype(BF)
    eml[w] = ems[...]
    em_ops = net.dp_push(lambda peer: ems, eml.at[w], 7)
    bal[t] = brow_ref[...]
    ba_ops = net.tensor_push(brow_ref, bal.at[t], 14)

    zs = [z, z + 1 - 2 * lax.rem(z, 2), lax.rem(z + 2, 4), 3 - z]
    xo = 1 - x
    mine, across = 2 * x + c, 2 * xo + c
    wy = lambda k: 2 * zs[k] + y
    wo = lambda k: 2 * zs[k] + (1 - y)
    to_z = lambda k: (2 * zs[k] + y, t)
    to_x, to_y, to_core = (w, across), (2 * z + (1 - y), t), (w, net.sib)
    sends = []

    def send(q, j, v, device, src=None):
        slot = wall_ref.at[q, j, v]
        op = pltpu.make_async_remote_copy(
            src_ref=slot if src is None else src, dst_ref=slot, send_sem=wsend.at[len(sends)],
            recv_sem=wrecv.at[q, j, v], device_id=device, device_id_type=MESH,
        )
        op.start()
        sends.append(op)

    def arrived(q, j, v):
        slot = wall_ref.at[q, j, v]
        pltpu.make_async_remote_copy(
            src_ref=slot, dst_ref=slot, send_sem=wsend.at[0], recv_sem=wrecv.at[q, j, v], device_id=to_core, device_id_type=MESH
        ).wait_recv()

    def column(q, k):
        if k == 0:
            src = pack_ref.at[q]
            send(q, mine, w, to_z(1), src)
            send(q, mine, w, to_z(2), src)
        else:
            src = None
            arrived(q, mine, wy(k))
            if k == 2:
                send(q, mine, wy(2), to_z(1))
        send(q, mine, wy(k), to_x, src)
        send(q, mine, wy(k), to_y, src)
        send(q, mine, wy(k), to_core, src)

    def by_y(q, k):
        return (q * 4 + k) % 3 == 0

    def side(q, k):
        arrived(q, across, wy(k))
        if by_y(q, k):
            send(q, across, wy(k), to_y)
        send(q, across, wy(k), to_core)
        arrived(q, mine, wo(k))
        if not by_y(q, k):
            send(q, mine, wo(k), to_x)
        send(q, mine, wo(k), to_core)

    def corner(q, k):
        arrived(q, across, wo(k))
        send(q, across, wo(k), to_core)

    def stage(q):
        column(q, 0)
        column(q, 1)
        side(q, 0)
        column(q, 2)
        side(q, 1)
        corner(q, 0)
        column(q, 3)
        side(q, 2)
        corner(q, 1)
        side(q, 3)
        corner(q, 2)
        corner(q, 3)

    def chain0():
        wait_all(pk_ops)
        feats = pkl[...].reshape(8 * n, 384)
        tf_ref[...] = feats[:, 0:FREQ]
        hot_ref[...] = feats[:, FREQ:384]
        small = smt_ref[...].astype(BF).astype(F32)
        t1 = hndot(small[:, 17:273], tf_ref[...]) + small[:, 273:274]
        t1_ref[...] = t1
        act = t1 / (1.0 + jnp.exp(-t1))
        a1s[...] = jnp.concatenate([act[0:half], act[half:share]], axis=1)
        a1l[w] = a1s[...]
        wto_ref[...] = small[:, 274:1042].astype(BF)
        return net.dp_push(lambda peer: a1s, a1l.at[w], 17)

    def chain1(ops):
        wait_all(ops)
        for k in range(n):
            a1_ref[share * k : share * k + half] = a1l[k][:, 0:64]
            a1_ref[share * k + half : share * k + share] = a1l[k][:, 64:128]
        small = smt_ref[...].astype(BF).astype(F32)
        cond = hdot(small[:, 274:1042], a1_ref[...]) + small[:, 1042:1043]
        cond = cond + hndot(small[:, 1043:1075], hot_ref[:, 0:CLASSES])
        ct_ref[...] = cond
        act = cond / (1.0 + jnp.exp(-cond))
        css[...] = jnp.concatenate([act[0:half], act[half:share]], axis=1)
        csl[w] = css[...]
        cs_ops = net.dp_push(lambda peer: css, csl.at[w], 24)
        parts = [tdot(piece, wmod_ref[...]) for piece in split3(act)]
        mps[...] = (parts[0] + parts[1] + parts[2]).reshape(n, 8, QKV0)
        mpl_[w] = mps[w]
        return cs_ops, net.dp_push(lambda peer: mps.at[peer], mpl_.at[w], 31)

    def chain2(ops):
        wait_all(ops)
        total = mpl_[0]
        for k in range(1, n):
            total = total + mpl_[k]
        mos[...] = total + bmod_ref[...]
        mol[t] = mos[...]
        return net.tensor_push(mos, mol.at[t], 38)

    def chain3(cs_ops, ops):
        wait_all(em_ops)
        rows = []
        for k in range(n):
            piece = eml[k].astype(F32)
            rows += [piece[:, 40 * i : 40 * i + 40] for i in range(3)]
        rows = jnp.concatenate(rows, axis=0)
        emb_ref[...] = jnp.concatenate([rows, jnp.zeros((D, 88), F32)], axis=1).T[0:40]
        wait_all(ba_ops)
        ball_ref[...] = bal[...]
        wait_all(cs_ops)
        rows = []
        for k in range(n):
            rows += [csl[k][:, 0:64], csl[k][:, 64:128]]
        rows = jnp.concatenate(rows, axis=0)
        a1s_all = jnp.concatenate([rows, jnp.zeros((D, 64), F32)], axis=1).T
        cs_all = a1s_all[0:64].reshape(n, 8, D)
        picked = jnp.zeros((8, D), F32)
        for k in range(n):
            picked = jnp.where(w == k, cs_all[k], picked)
        cs_ref[...] = picked
        wait_all(ops)
        for lat in range(4):
            for j in range(4):
                for piece in range(2):
                    mod_ref[lat, 2 * j + piece : 2 * j + piece + 1, :] = mol[j, pl.ds(4 * c + lat, 1), D * piece : D * piece + D]

    ops = None
    stage(0)
    ops = chain0()
    stage(1)
    cs_ops, ops = chain1(ops)
    stage(2)
    ops = chain2(ops)
    chain3(cs_ops, ops)
    for q in range(3):
        for j in (2 * x + 1 - c, 2 * xo + 1 - c):
            for v in range(n):
                arrived(q, j, v)
    for op in own:
        op.wait()
    for op in sends:
        op.wait_send()
    net.finish()


def run_gather(pack, pk, smt, wmod, brow, bmod, n):
    S = jax.ShapeDtypeStruct
    V = pltpu.VMEM
    DMA = pltpu.SemaphoreType.DMA
    share = D // n
    lat = 8 * n
    any_spec = pl.BlockSpec(memory_space=pl.ANY)
    vm = pl.BlockSpec(memory_space=pltpu.VMEM)
    outs = [
        S((3, 4, n, share, D), BF), S((4, 8, D), F32), S((40, D), F32), S((4, 1, QKV0), F32), S((8, D), F32),
        S((share, lat), F32), S((share, lat), F32), S((D, lat), F32), S((lat, FREQ), F32), S((lat, 128), F32), S((share, D), BF),
    ]
    scratch = [
        V((n, 8, 384), F32), V((share // 3, 128), BF), V((n, share // 3, 128), BF),
        V((share // 2, 128), F32), V((n, share // 2, 128), F32), V((share // 2, 128), F32), V((n, share // 2, 128), F32),
        V((n, 8, QKV0), F32), V((n, 8, QKV0), F32), V((8, QKV0), F32), V((4, 8, QKV0), F32), V((4, 1, QKV0), F32),
        DMA((3,)), DMA((120,)), DMA((3, 4, n)), DMA((41,)), DMA((41,)),
    ]
    return pl.pallas_call(
        gather_kernel,
        out_shape=outs,
        in_specs=[any_spec] + [vm] * 5,
        out_specs=[any_spec] + [vm] * 10,
        scratch_shapes=scratch,
        compiler_params=pltpu.CompilerParams(collective_id=0, has_side_effects=True, vmem_limit_bytes=48 * 1024 * 1024),
        name="gather",
    )(pack, pk, smt, wmod, brow, bmod)


def gram_schmidt(block):
    rows = lax.broadcasted_iota(jnp.int32, (8, 1), 0)
    for index in range(8):
        row = block[index : index + 1]
        row = row * lax.rsqrt(jnp.sum(row * row, axis=-1, keepdims=True) + TINY)
        inner = jnp.sum(block * row, axis=-1, keepdims=True)
        inner = jnp.where(rows > index, inner, 0.0)
        block = jnp.where(rows == index, row, block - inner * row)
    return block


def grad_kernel(
    a_ref, m_ref, dy_ref, dz_ref, o_ref, dq_ref, du_ref, g_ref, cerr_ref, rerr_ref,
    dmod_ref, small_ref, dbq_ref, db1_ref, hb_ref, right_ref, cs_ref, ct_ref, t1_ref, a1_ref, tf_ref, hot_ref, wmod_ref, wto_ref,
    mcol_ref, mrow_ref, left_ref, rightn_ref, pst_ref, psr_ref, pc_ref, qst_ref, qsn_ref, qrs_ref, gb_ref, gh_ref, gsm_ref,
    mc, mr, sc, sr, rc, rr, av, mv, dyv, dzv, ov, qv, uv, gv,
    dmo, smo, dbo, dbo1, hbo, dm8, dma, dsc, dss, dts, dtl, tks, tkl, px, pland, py, qx, qland, qy,
    load_sem, send_sem, recv_sem,
):
    net = Peers(send_sem, recv_sem)
    w, t, c = net.w, net.t, net.c
    n = net.n
    share = D // n
    loads = {}

    def load(name, src, dst, index):
        op = pltpu.make_async_copy(src, dst, load_sem.at[index])
        op.start()
        loads[name] = op

    load("q", dq_ref, qv, 9)
    load("a", a_ref, av, 1)
    load("u", du_ref, uv, 0)
    load("m", m_ref, mv, 2)
    load("g", g_ref, gv, 3)
    load("dz", dz_ref, dzv, 4)
    load("o", o_ref, ov, 5)
    load("dy", dy_ref, dyv, 6)
    load("ce", cerr_ref, mc, 7)
    load("re", rerr_ref, mr, 8)
    net.barrier()
    side = [
        net.core_push(dmod_ref, dmo, 0),
        net.core_push(small_ref, smo, 1),
        net.core_push(dbq_ref.at[1 - c], dbo, 2),
        net.core_push(db1_ref.at[1 - c], dbo1, 9),
        net.core_push(hb_ref, hbo, 10),
    ]

    def chunk(i, size=256):
        return pl.ds(pl.multiple_of(i * size, size), size)

    def after(i, first):
        return pl.ds(pl.multiple_of(first + 256 * i, 64), 256)

    for name in ("q", "a"):
        loads[name].wait()
    col_ops, row_ops = [], []
    sc[0:256] = tdot(qv[1 - c, :, 0:256], av[...])
    sc[256:576] = tdot(qv[1 - c, :, 256:640], av[...])[0:320]
    col_ops.append(net.core_push(sc.at[0:576], rc.at[0:576], 3))
    for name in ("u", "m"):
        loads[name].wait()

    @pl.loop(0, 3)
    def _(i):
        sc[after(i, 576), :] = tdot(uv[1 - c, :, chunk(i)], mv[...])

    col_ops.append(net.core_push(sc.at[576:1344], rc.at[576:1344], 4))
    wait_all(side)
    for lat in range(4):
        for piece in range(2):
            span = slice(D * piece, D * piece + D)
            dm8[pl.ds(4 * c + lat, 1), span] = dmod_ref[lat, pl.ds(2 * t + piece, 1), :]
            dm8[pl.ds(4 * (1 - c) + lat, 1), span] = dmo[lat, pl.ds(2 * t + piece, 1), :]
    dma[w] = dm8[...]
    dm_ops = net.dp_push(lambda peer: dm8, dma.at[w], 16)
    for name in ("g", "dz", "o", "dy"):
        loads[name].wait()

    @pl.loop(0, 3)
    def _(i):
        sr[after(i, 192), :] = tdot(gv[1 - c, :, chunk(i)], dzv[...])

    sr[0:192, :] = tdot(ov[1 - c], dyv[...])[0:192]
    row_ops.append(net.core_push(sr, rr, 6))
    total = small_ref[...] + smo[...]
    for k in range(n):
        tks[k, :, 0:share] = total[:, share * k : share * k + share]
    tkl[w] = tks[w]
    tok_ops = net.dp_push(lambda peer: tks.at[peer], tkl.at[w], 24)
    loads["ce"].wait()
    dms = split3(dm8[...])
    cs = split3(cs_ref[...])
    left_side = jnp.concatenate([dms[0], dms[1], dms[0], dms[2], dms[1], dms[0]], axis=0)
    right_side = jnp.concatenate([cs[0], cs[0], cs[1], cs[0], cs[1], cs[2]], axis=0)
    for i in range(6):
        mc[256 * i : 256 * i + 256, :] += tdot(left_side[:, 256 * i : 256 * i + 256], right_side)
    wait_all(col_ops)
    mc[QKV0 : QKV0 + 256] += tdot(qv[c, :, 0:256], av[...]) + rc[0:256]
    mc[QKV0 + 256 : FC0] += tdot(qv[c, :, 256:640], av[...])[0:320] + rc[256:576]

    @pl.loop(0, 3)
    def _(i):
        mc[after(i, FC0), :] += tdot(uv[c, :, chunk(i)], mv[...]) + rc[after(i, 576), :]

    out_col = pltpu.make_async_copy(mc, mcol_ref, load_sem.at[0])
    out_col.start()
    wait_all(dm_ops)
    dmx = dma[...].reshape(8 * n, QKV0)
    part = sum(ndot(wmod_ref[...], piece) for piece in split3(dmx))
    dss[...] = part
    dsc[t] = part
    ds_ops = net.tensor_push(dss, dsc.at[t], 32)
    loads["re"].wait()
    wait_all(row_ops)

    @pl.loop(0, 3)
    def _(i):
        mr[after(i, 192), :] += tdot(gv[c, :, chunk(i)], dzv[...]) + rr[after(i, 192), :]

    mr[0:192, :] += tdot(ov[c], dyv[...])[0:192] + rr[0:192, :]
    out_row = pltpu.make_async_copy(mr, mrow_ref, load_sem.at[1])
    out_row.start()
    right = right_ref[...]

    def left_part(first, last):
        sides = jnp.concatenate(halves(right[:, first:last]), axis=0).astype(BF)
        high, low = split2(mc[first:last, :])
        got = dot(sides, high) + dot(sides, low)
        return got[0:8] + got[8:16]

    for k, spans in enumerate((((0, 512), (512, 1024), (1024, QKV0)), ((QKV0, FC0),), ((FC0, FC0 + 384), (FC0 + 384, COLS)))):
        got = sum(left_part(*span) for span in spans)
        for i in range(6):
            px[6 * k + i] = got[:, 128 * i : 128 * i + 128]
    row_side = fill(halves(right[:, COLS : COLS + D]) + halves(right[:, COLS + D : COLS + 2 * D]), 128).T.astype(BF)

    def row_chunk(values):
        high, low = split2(values)
        return dot(high, row_side) + dot(low, row_side)

    got = jnp.concatenate([row_chunk(mr[0:192, :]), jnp.zeros((64, 128), F32)], axis=0).T
    for i in range(2):
        px[18 + i] = got[0:8, 128 * i : 128 * i + 128] + got[8:16, 128 * i : 128 * i + 128]
    for i in range(3):
        got = row_chunk(mr[192 + 256 * i : 448 + 256 * i, :]).T
        got = got[16:24] + got[24:32]
        px[20 + 2 * i] = got[:, 0:128]
        px[21 + 2 * i] = got[:, 128:256]
    bias = jnp.concatenate(
        [colsum(dm8[...]), (dbq_ref[c] + dbo[...])[:, 0:576], db1_ref[c] + dbo1[...], jnp.zeros((1, 192), F32)], axis=1
    )
    for i in range(24):
        px[26 + i // 8, i % 8 : i % 8 + 1, :] = bias[:, 128 * i : 128 * i + 128]
    both = hb_ref[...] + hbo[...]
    px[29] = both[0:8]
    px[30] = both[8:16]
    px[31] = jnp.zeros((8, 128), F32)

    def scatter(v, land, per, base):
        own = pl.ds(w * per, per)
        land[w] = v[own]
        return net.dp_push(lambda peer: v.at[pl.ds(peer * per, per)], land.at[w], base)

    def collect(land, v, per, base, ops):
        wait_all(ops)
        own = pl.ds(w * per, per)
        v[own] = sum(land[k] for k in range(1, n)) + land[0]
        return net.dp_push(lambda peer: v.at[own], v.at[own], base)

    ops = scatter(px, pland, P_COUNT // n, 40)
    wait_all(ds_ops)
    dcond = (dsc[0] + dsc[1] + dsc[2] + dsc[3]) * silu_slope_k(ct_ref[...])
    dts[...] = sum(tdot(wto_ref[...], piece) for piece in split3(dcond)).reshape(n, share, 8 * n)
    dtl[w] = dts[w]
    dt_ops = net.dp_push(lambda peer: dts.at[peer], dtl.at[w], 56)
    gsm_ref[:, 274:1042] = hndot(dcond, a1_ref[...])
    gsm_ref[:, 1042:1043] = jnp.sum(dcond, axis=1, keepdims=True)
    gsm_ref[:, 1043:1075] = hdot(dcond, hot_ref[...])[:, 0:CLASSES]
    ops = collect(pland, py, P_COUNT // n, 48, ops)
    wait_all(tok_ops)
    tok = sum(tkl[k] for k in range(1, n)) + tkl[0]
    tok = jnp.concatenate([tok, jnp.zeros((88, 128), F32)], axis=0).T[0:share]
    gsm_ref[:, 0:16] = tok[:, 0:16]
    gsm_ref[:, 16:17] = tok[:, 32:33]
    gsm_ref[:, 1075:1091] = tok[:, 16:32]
    gsm_ref[:, 1091:1093] = tok[:, 33:35]
    wait_all(ops)
    base = 0
    bases = []
    for index, count in enumerate(P_TILES):
        bases.append(gram_schmidt(jnp.concatenate([py[base + k] for k in range(count)], axis=1)))
        base += count
    offset = 0
    for block, width in zip(bases, (D, D, D, 192, D)):
        left_ref[:, offset : offset + width] = block[:, 0:width]
        offset += width
    gb_ref[...] = jnp.concatenate([py[26 + i // 8, i % 8 : i % 8 + 1, :] for i in range(23)], axis=1)[:, 0:COLS]
    gh_ref[...] = jnp.concatenate([py[29], py[30]], axis=0)

    col_side = fill(halves(bases[0]) + halves(bases[1]) + halves(bases[2]), 128).T.astype(BF)

    def col_chunk(values):
        high, low = split2(values)
        return dot(high, col_side) + dot(low, col_side)

    def put(first, rows, k, tile):
        got = col_chunk(mc[first : first + rows, :])
        if rows % 128:
            got = jnp.concatenate([got, jnp.zeros((128 - rows % 128, 128), F32)], axis=0)
        got = got.T
        got = got[16 * k : 16 * k + 8] + got[16 * k + 8 : 16 * k + 16]
        for i in range(got.shape[1] // 128):
            qx[tile + i] = got[:, 128 * i : 128 * i + 128]

    for i in range(6):
        put(256 * i, 256, 0, 2 * i)
    put(QKV0, 256, 1, 12)
    put(QKV0 + 256, 320, 1, 14)
    for i in range(3):
        put(FC0 + 256 * i, 256, 2, 17 + 2 * i)
    for k, (rows, block) in enumerate(((slice(0, 192), bases[3][:, 0:192]), (slice(192, 960), bases[4]))):
        left = jnp.concatenate(halves(block), axis=0).astype(BF)
        high, low = split2(mr[rows, :])
        got = dot(left, high) + dot(left, low)
        got = got[0:8] + got[8:16]
        for i in range(6):
            qx[23 + 6 * k + i] = got[:, 128 * i : 128 * i + 128]
    for i in range(35, Q_COUNT):
        qx[i] = jnp.zeros((8, 128), F32)
    ops = scatter(qx, qland, Q_COUNT // n, 64)
    wait_all(dt_ops)
    dtime = (sum(dtl[k] for k in range(1, n)) + dtl[0]) * silu_slope_k(t1_ref[...])
    gsm_ref[:, 17:273] = hdot(dtime, tf_ref[...])
    gsm_ref[:, 273:274] = jnp.sum(dtime, axis=1, keepdims=True)

    def left_rows(blocks):
        rows = []
        for block in blocks:
            high, low = halves(block)
            rows += [high, low, high]
        return rows

    def right_rows(blocks):
        rows = []
        for block in blocks:
            high, low = halves(block)
            rows += [high, high, low]
        return rows

    pst_ref[...] = fill(left_rows(bases[:3]), 128).astype(BF)
    proj = jnp.concatenate([bases[3][:, 0:192], jnp.zeros((8, D), F32)], axis=1)
    fc = jnp.concatenate([jnp.zeros((8, 192), F32), bases[4]], axis=1)
    row_stack = fill(left_rows([proj, fc]), 128)
    pc_ref[...] = row_stack.astype(BF)
    row_stack = jnp.concatenate([row_stack, jnp.zeros((128, 64), F32)], axis=1)
    psr_ref[...] = row_stack.T[0:960].astype(BF)
    ops = collect(qland, qy, Q_COUNT // n, 72, ops)
    wait_all(ops)
    qkv = jnp.concatenate([qy[12 + i] for i in range(5)], axis=1)[:, 0:576]
    pieces = [jnp.concatenate([qy[i] for i in range(12)], axis=1), qkv, jnp.concatenate([qy[17 + i] for i in range(6)], axis=1)]
    pad = jnp.zeros((8, 64), F32)
    qc = jnp.concatenate(pieces + [pad], axis=1)
    span = lax.broadcasted_iota(jnp.int32, (8, 2944), 1)
    cuts = [
        jnp.where((span >= first) & (span < last), qc, 0.0) for first, last in ((0, QKV0), (QKV0, FC0), (FC0, COLS))
    ]
    stack = fill(right_rows(cuts), 128)
    qsn_ref[...] = stack.astype(BF)
    qst_ref[...] = stack.T[0:COLS].astype(BF)
    qr = [jnp.concatenate([qy[23 + 6 * k + i] for i in range(6)], axis=1) for k in range(2)]
    qrs_ref[...] = fill(right_rows(qr), 128).astype(BF)
    rightn_ref[:, 0:COLS] = qc[:, 0:COLS]
    rightn_ref[:, COLS : COLS + D] = qr[0]
    rightn_ref[:, COLS + D : COLS + 2 * D] = qr[1]
    net.finish()
    out_col.wait()
    out_row.wait()


def run_grad(operands, n):
    S = jax.ShapeDtypeStruct
    V = pltpu.VMEM
    rows = operands[0].shape[0]
    lat = 8 * n
    share = D // n
    any_spec = pl.BlockSpec(memory_space=pl.ANY)
    vm = pl.BlockSpec(memory_space=pltpu.VMEM)
    outs = [
        S((COLS, D), F32), S((960, D), F32), S((8, 3264), F32), S((8, 4416), F32),
        S((128, D), BF), S((960, 128), BF), S((128, 960), BF), S((COLS, 128), BF), S((128, 2944), BF), S((128, D), BF),
        S((1, COLS), F32), S((16, 128), F32), S((share, 1093), F32),
    ]
    scratch = [
        V((COLS, D), F32), V((960, D), F32), V((1344, D), F32), V((960, D), F32), V((1344, D), F32), V((960, D), F32),
        V((rows, D), BF), V((rows, D), BF), V((rows, D), BF), V((rows, D), BF),
        V((2, rows, 256), BF), V((2, rows, 640), BF), V((2, rows, D), BF), V((2, rows, D), BF),
        V((4, 8, D), F32), V((40, D), F32), V((1, 640), F32), V((1, D), F32), V((16, 128), F32),
        V((8, QKV0), F32), V((n, 8, QKV0), F32),
        V((4, share, lat), F32), V((share, lat), F32), V((n, share, lat), F32), V((n, share, lat), F32),
        V((n, 40, 128), F32), V((n, 40, 128), F32),
        V((P_COUNT, 8, 128), F32), V((n, P_COUNT // n, 8, 128), F32), V((P_COUNT, 8, 128), F32),
        V((Q_COUNT, 8, 128), F32), V((n, Q_COUNT // n, 8, 128), F32), V((Q_COUNT, 8, 128), F32),
        pltpu.SemaphoreType.DMA((10,)), pltpu.SemaphoreType.DMA((80,)), pltpu.SemaphoreType.DMA((80,)),
    ]
    return pl.pallas_call(
        grad_kernel,
        out_shape=outs,
        in_specs=[any_spec] * 10 + [vm] * 14,
        out_specs=[any_spec] * 2 + [vm] * 11,
        scratch_shapes=scratch,
        compiler_params=pltpu.CompilerParams(collective_id=1, has_side_effects=True, vmem_limit_bytes=60 * 1024 * 1024),
        name="grad",
    )(*operands)


def apply_kernel(
    w_ref, mcol_ref, mrow_ref, qst_ref, psr_ref, pst_ref, pc_ref, qsn_ref, qrs_ref,
    cw_ref, cm_ref, rw_ref, rm_ref, gs_ref, sw_ref, sm_ref,
    cres_ref, rres_ref, cn_ref, cmn_ref, rn_ref, rmn_ref, sn_ref, smn_ref, *, n
):
    step = pl.program_id(0)
    share = D // n
    cres_ref[...] = mcol_ref[...] - dot(qst_ref[...], pst_ref[...]) * (1.0 / n)
    rres_ref[...] = mrow_ref[...] - dot(psr_ref[...], qrs_ref[...]) * (1.0 / n)

    @pl.when(step == 0)
    def _():
        place = lax.broadcasted_iota(jnp.int32, (D, 128), 0) == w_ref[0] * share + lax.broadcasted_iota(jnp.int32, (D, 128), 1)
        pick = jnp.where(place, 1.0, 0.0).astype(BF)
        mom = DECAY * cm_ref[...] + tdot(dot(pst_ref[...], pick).astype(BF), qsn_ref[...])[0:share, 0:COLS]
        cmn_ref[...] = mom
        cn_ref[...] = cw_ref[...] - LEARN_RATE * mom
        mom = DECAY * rm_ref[...] + tdot(dot(qrs_ref[...], pick).astype(BF), pc_ref[...])[0:share]
        rmn_ref[...] = mom
        rn_ref[...] = rw_ref[...] - LEARN_RATE * mom
        mom = DECAY * sm_ref[...] + gs_ref[...]
        smn_ref[...] = mom
        sn_ref[...] = sw_ref[...] - LEARN_RATE * mom


def run_apply(w, operands, n):
    share = D // n
    S = jax.ShapeDtypeStruct
    blk = lambda r, cc: pl.BlockSpec((r, cc), lambda i, *_: (i, 0))
    full = lambda r, cc: pl.BlockSpec((r, cc), lambda i, *_: (0, 0))
    cb, rb, sb = full(share, COLS), full(share, 960), full(share, 1093)
    return pl.pallas_call(
        functools.partial(apply_kernel, n=n),
        grid_spec=pltpu.PrefetchScalarGridSpec(
            num_scalar_prefetch=1,
            grid=(8,),
            in_specs=[blk(360, D), blk(120, D), blk(360, 128), blk(120, 128), full(128, D), full(128, 960), full(128, 2944), full(128, D)]
            + [cb, cb, rb, rb, sb, sb, sb],
            out_specs=[blk(360, D), blk(120, D), cb, cb, rb, rb, sb, sb],
        ),
        out_shape=[S((COLS, D), F32), S((960, D), F32)] + [S((share, v), F32) for v in (COLS, COLS, 960, 960, 1093, 1093)],
        compiler_params=pltpu.CompilerParams(vmem_limit_bytes=48 * 1024 * 1024),
        name="apply",
    )(w, *operands)


def position_table():
    quarter = D // 4
    omega = 1.0 / 10000.0 ** (jnp.arange(quarter, dtype=jnp.float32) / quarter)
    place = jnp.arange(GRID, dtype=jnp.float32)[:, None] * omega[None, :]
    return jnp.concatenate([jnp.sin(place), jnp.cos(place)], axis=1)


def time_features(times):
    half = FREQ // 2
    freqs = jnp.exp(-math.log(10000.0) * jnp.arange(half, dtype=jnp.float32) / half)
    angles = 1000.0 * times[:, None] * freqs[None, :]
    return jnp.concatenate([jnp.cos(angles), jnp.sin(angles)], axis=1)


def small_starts():
    counts = [PATCH_IN, 1, FREQ, 1, D, 1, CLASSES, PATCH_IN, 1, 1]
    starts = [0]
    for amount in counts:
        starts.append(starts[-1] + amount)
    return starts


def cut_parts(array, widths, axis):
    pieces = []
    offset = 0
    for width in widths:
        pieces.append(lax.slice_in_dim(array, offset, offset + width, axis=axis))
        offset = offset + width
    return pieces


def ortho_kernel(x_ref, o_ref):
    count = x_ref.shape[0]
    rows = [x_ref[index] for index in range(count)]
    for index in range(count):
        vector = rows[index]
        vector = vector * lax.rsqrt(jnp.sum(vector * vector, axis=-1, keepdims=True) + TINY)
        o_ref[index] = vector
        for later in range(index + 1, count):
            rows[later] = rows[later] - jnp.sum(rows[later] * vector, axis=-1, keepdims=True) * vector


def orthonormal_all(parts):
    stacked = jnp.stack([jnp.pad(part, ((0, 0), (0, D - part.shape[1]))) for part in parts], axis=1)
    stacked = jnp.pad(stacked, ((0, 0), (0, 8 - len(parts)), (0, 0)))
    out = pl.pallas_call(ortho_kernel, out_shape=jax.ShapeDtypeStruct(stacked.shape, F32), name="ortho")(stacked)
    return [out[:, index, : part.shape[1]] for index, part in enumerate(parts)]


def rounded(values):
    return lax.optimization_barrier(values.astype(BF)).astype(F32)


def silu_slope(values):
    gate = jax.nn.sigmoid(values)
    return gate * (1.0 + values * (1.0 - gate))


def shards_general(
    clean_latents,
    noise_draw,
    timesteps,
    labels,
    col_weights,
    col_moments,
    col_errors,
    row_weights,
    row_moments,
    row_errors,
    bias_weights,
    bias_moments,
    small_weights,
    small_moments,
    head_bias,
    head_moments,
    right_factors,
):
    tensor_size = lax.axis_size("tensor")
    data_size = lax.axis_size("dp")
    tensor_rank = lax.axis_index("tensor")
    data_rank = lax.axis_index("dp")
    batch = clean_latents.shape[0]
    half = batch // 2
    share = D // data_size
    mod_width = 8 * D // tensor_size
    qkv_width = 3 * D // tensor_size
    ffn_width = FF // tensor_size
    proj_rows = D // tensor_size
    count_all = data_size * batch * SEQ * PATCH_IN
    col_widths = [mod_width, qkv_width, ffn_width]
    core = lax.rem(tensor_rank, 2)
    base = tensor_rank - core
    pair = [(index, index + 1 - 2 * (index % 2)) for index in range(tensor_size)]

    def swap(values):
        return lax.ppermute(values, "tensor", pair)

    col_low = col_weights[:, 0, :].astype(BF)
    row_low = row_weights[0].astype(BF).T
    packed = jnp.concatenate(
        [
            col_low[:, mod_width : mod_width + qkv_width],
            row_low[:, :proj_rows],
            col_low[:, mod_width + qkv_width :],
            row_low[:, proj_rows:],
        ],
        axis=1,
    )
    wall = lax.all_gather(lax.all_gather(packed, "dp", axis=0, tiled=True), "tensor", axis=0)
    wall = jnp.stack([wall[:, :, 768 * index : 768 * index + 768] for index in range(3)])
    starts = small_starts()
    small_low = small_weights.astype(BF)
    small_exact = rounded(small_weights)
    picked = jnp.concatenate([small_low[: starts[2]], small_low[starts[7] :]], axis=0)
    emb = lax.all_gather(picked.astype(F32), "dp", axis=1, tiled=True)
    emb = jnp.concatenate([emb[:16], emb[17:33], emb[16:17], emb[33:35], jnp.zeros((5, D), F32)], axis=0)
    w_tin = small_exact[starts[2] : starts[3]]
    b_tin = small_exact[starts[3]]
    w_tout = small_exact[starts[4] : starts[5]]
    b_tout = small_exact[starts[5]]
    table = small_exact[starts[6] : starts[7]]
    bias_exact = rounded(bias_weights[0])
    head_exact = rounded(head_bias)
    w_mod = rounded(col_weights[:, 0, :mod_width])
    bias_all = lax.all_gather(bias_exact, "tensor", axis=0)
    times_all = lax.all_gather(timesteps, "dp", axis=0, tiled=True)
    labels_all = lax.all_gather(labels, "dp", axis=0, tiled=True)
    time_feat = time_features(times_all)
    time_hidden = exact_dot(time_feat, w_tin) + b_tin
    time_act = lax.all_gather(jax.nn.silu(time_hidden), "dp", axis=1, tiled=True)
    onehot = (labels_all[:, None] == jnp.arange(CLASSES, dtype=jnp.int32)[None, :]).astype(F32)
    condition = exact_dot(time_act, w_tout) + b_tout + exact_dot(onehot, table)
    cond_act = jax.nn.silu(condition)
    mod_part = exact_dot(cond_act, w_mod)
    mod_own = lax.psum_scatter(mod_part, "dp", scatter_dimension=0, tiled=True) + bias_exact[:mod_width]
    mod_full = lax.all_gather(mod_own, "tensor", axis=1, tiled=True).reshape(batch, 8, D)
    cond_rows = lax.all_to_all(cond_act, "dp", split_axis=0, concat_axis=1, tiled=True)

    def mine(values):
        return lax.dynamic_slice_in_dim(values, core * half, half, 0)

    ball = jnp.concatenate(
        [
            jnp.pad(bias_all[:, mod_width : mod_width + qkv_width], ((0, 0), (0, 768 - qkv_width))),
            bias_all[:, mod_width + qkv_width :],
        ],
        axis=1,
    )[:, None]
    (a, m, dy, dz, o, dq, du, g, dmod, small, dbq, db1, hb) = run_block(
        base.reshape(1),
        mine(timesteps),
        mine(clean_latents).transpose(0, 2, 1),
        mine(noise_draw).transpose(0, 2, 1),
        mine(mod_full),
        wall,
        position_table(),
        emb,
        head_exact[:, None],
        ball,
        count_all,
    )
    rows = half * SEQ

    def flat(values):
        return values.reshape(rows, values.shape[-1])

    def pick(values, which):
        return lax.dynamic_index_in_dim(values, which, 0, keepdims=False)

    def gradients(which):
        return (
            tdot(flat(a), flat(pick(dq, which))[:, :qkv_width]),
            tdot(flat(m), flat(pick(du, which))),
            tdot(flat(pick(o, which))[:, :proj_rows], flat(dy)),
            tdot(flat(pick(g, which)), flat(dz)),
            pick(dbq, which)[0, :qkv_width],
            pick(db1, which)[0],
        )

    other = swap(gradients(1 - core))
    own = gradients(core)
    g_qkv, g_fc1, g_proj, g_fc2, g_bqkv, g_bfc1 = [left + right for left, right in zip(own, other)]
    dmod_own = dmod.reshape(half, 8 * D)
    dmod_other = swap(dmod_own)
    dmod_group = jnp.where(
        core == 0,
        jnp.concatenate([dmod_own, dmod_other], axis=0),
        jnp.concatenate([dmod_other, dmod_own], axis=0),
    )
    d_mod = lax.dynamic_slice_in_dim(dmod_group, tensor_rank * mod_width, mod_width, 1)
    g_bmod = jnp.sum(d_mod, axis=0)
    g_mod = exact_tdot(cond_rows, d_mod)
    d_mod_all = lax.all_gather(d_mod, "dp", axis=0, tiled=True)
    d_cond = lax.psum(exact_ndot(d_mod_all, w_mod), "tensor") * silu_slope(condition)
    g_table = exact_tdot(onehot, d_cond)
    g_btout = jnp.sum(d_cond, axis=0)
    g_tout = exact_tdot(time_act, d_cond)
    d_time = lax.psum_scatter(exact_ndot(d_cond, w_tout), "dp", scatter_dimension=1, tiled=True)
    d_time = d_time * silu_slope(time_hidden)
    g_btin = jnp.sum(d_time, axis=0)
    g_tin = exact_tdot(time_feat, d_time)
    small_own = lax.psum(lax.psum_scatter(small, "dp", scatter_dimension=1, tiled=True), "tensor") * 0.5
    head_sum, loss_value = lax.psum((hb[:, 0] * 0.5, hb[0, 1] * 0.5), ("dp", "tensor"))
    small_step = jnp.concatenate(
        [
            small_own[:16],
            small_own[32:33],
            g_tin,
            g_btin[None],
            g_tout,
            g_btout[None],
            g_table,
            small_own[16:32],
            small_own[33:34],
            small_own[34:35],
        ],
        axis=0,
    )
    bias_sum = lax.psum(jnp.concatenate([g_bmod, g_bqkv, g_bfc1], axis=0), "dp")
    col_cuts = cut_parts(col_errors[0, 0], col_widths, 1)
    row_cuts = cut_parts(row_errors[0, 0], [proj_rows, ffn_width], 0)
    matrices = [
        g_mod + col_cuts[0],
        g_qkv + col_cuts[1],
        g_fc1 + col_cuts[2],
        g_proj + row_cuts[0],
        g_fc2 + row_cuts[1],
    ]
    right_pieces = cut_parts(right_factors[0], col_widths + [D, D], 1)
    left_local = jnp.concatenate([exact_ndot(right_pieces[i], matrices[i]) for i in range(5)], axis=1)
    left_sum = lax.psum(left_local, "dp")
    bases = orthonormal_all(cut_parts(left_sum, [D, D, D, proj_rows, ffn_width], 1))
    right_local = jnp.concatenate([exact_dot(bases[i], matrices[i]) for i in range(5)], axis=1)
    right_sum = lax.psum(right_local, "dp")
    right_split = cut_parts(right_sum, col_widths + [D, D], 1)
    approx = [exact_tdot(bases[i], right_split[i]) for i in range(5)]
    rest = [matrices[i] - approx[i] / data_size for i in range(5)]
    col_residue = jnp.concatenate(rest[:3], axis=1)[None, None]
    row_residue = jnp.concatenate(rest[3:], axis=0)[None, None]

    def own_columns(values):
        return lax.dynamic_slice_in_dim(values, data_rank * share, share, 1)

    col_step = jnp.concatenate(
        [exact_tdot(own_columns(bases[i]), right_split[i]) for i in range(3)], axis=1
    )[:, None, :]
    row_step = jnp.concatenate(
        [exact_tdot(bases[i], own_columns(right_split[i])) for i in (3, 4)], axis=0
    )[None]
    col_momentum = DECAY * col_moments + col_step
    col_new = col_weights - LEARN_RATE * col_momentum
    row_momentum = DECAY * row_moments + row_step
    row_new = row_weights - LEARN_RATE * row_momentum
    small_momentum = DECAY * small_moments + small_step
    small_new = small_weights - LEARN_RATE * small_momentum
    bias_momentum = DECAY * bias_moments + bias_sum[None]
    bias_new = bias_weights - LEARN_RATE * bias_momentum
    head_momentum = DECAY * head_moments + head_sum
    head_new = head_bias - LEARN_RATE * head_momentum
    left_factors = jnp.concatenate(bases, axis=1)[None]
    right_new = right_sum[None]
    return (
        loss_value,
        col_new,
        col_momentum,
        col_residue,
        row_new,
        row_momentum,
        row_residue,
        bias_new,
        bias_momentum,
        small_new,
        small_momentum,
        head_new,
        head_momentum,
        left_factors,
        right_new,
    )


def shards(
    clean_latents,
    noise_draw,
    timesteps,
    labels,
    col_weights,
    col_moments,
    col_errors,
    row_weights,
    row_moments,
    row_errors,
    bias_weights,
    bias_moments,
    small_weights,
    small_moments,
    head_bias,
    head_moments,
    right_factors,
):
    tensor_size = lax.axis_size("tensor")
    data_size = lax.axis_size("dp")
    tensor_rank = lax.axis_index("tensor")
    data_rank = lax.axis_index("dp")
    batch = clean_latents.shape[0]
    half = batch // 2
    share = D // data_size
    mod_width = 8 * D // tensor_size
    qkv_width = 3 * D // tensor_size
    ffn_width = FF // tensor_size
    proj_rows = D // tensor_size
    count_all = data_size * batch * SEQ * PATCH_IN
    col_widths = [mod_width, qkv_width, ffn_width]
    core = lax.rem(tensor_rank, 2)
    base = tensor_rank - core
    col = col_weights[:, 0]
    col_low = col.astype(BF)
    row_low = row_weights[0].T.astype(BF)
    packed = jnp.stack(
        [
            jnp.concatenate([col_low[:, mod_width : mod_width + qkv_width], row_low[:, :proj_rows]], axis=1),
            col_low[:, mod_width + qkv_width :],
            row_low[:, proj_rows:],
        ]
    )
    wmod = col_low[:, :mod_width]
    onehot = (labels[:, None] == jnp.arange(128, dtype=jnp.int32)[None, :]).astype(F32)
    features = jnp.concatenate([time_features(timesteps), onehot], axis=1)
    bias_exact = rounded(bias_weights)
    bias_row = jnp.concatenate(
        [bias_exact[:, mod_width : mod_width + qkv_width], jnp.zeros((1, 192), F32), bias_exact[:, mod_width + qkv_width :]],
        axis=1,
    )
    small_t = small_weights.T
    wall, mod, emb, ball, cs, ct, t1, a1, tf, hot, wto = run_gather(
        packed, features, small_t, wmod, bias_row, bias_exact[:, :mod_width], data_size
    )

    def mine(values):
        return lax.dynamic_slice_in_dim(values, core * half, half, 0)

    a, m, dy, dz, o, dq, du, g, dmod, small, dbq, db1, hb = run_block(
        base.reshape(1),
        mine(timesteps),
        mine(clean_latents.transpose(0, 2, 1)),
        mine(noise_draw.transpose(0, 2, 1)),
        mod,
        wall.reshape(3, tensor_size, D, D),
        position_table(),
        emb,
        rounded(head_bias)[:, None],
        ball,
        count_all,
    )
    rows = half * SEQ

    def flat(values):
        return values.reshape(values.shape[:-3] + (rows, values.shape[-1]))

    acts = [flat(values) for values in (a, m, dy, dz, o, dq, du, g)]
    errors = [col_errors[0, 0].T, row_errors[0, 0]]
    mcol, mrow, left_all, right_sum, pst, psr, pc, qst, qsn, qrs, gb, gh, gsm = run_grad(
        acts + errors + [dmod, small, dbq, db1, hb, right_factors[0], cs, ct, t1, a1, tf, hot, wmod, wto], data_size
    )
    cres, rres, cn, cmn, rn, rmn, sn, smn = run_apply(
        data_rank.reshape(1),
        [mcol, mrow, qst, psr, pst, pc, qsn, qrs, col, col_moments[:, 0], row_weights[0].T, row_moments[0].T]
        + [gsm, small_t, small_moments.T],
        data_size,
    )
    col_new, col_momentum, col_residue = cn[:, None], cmn[:, None], cres.T[None, None]
    row_new, row_momentum, row_residue = rn.T[None], rmn.T[None], rres[None, None]
    small_new, small_momentum = sn.T, smn.T
    bias_sum = gb[0]
    head_sum = gh[:, 0]
    loss_value = gh[0, 1]
    bias_momentum = DECAY * bias_moments + bias_sum[None]
    bias_new = bias_weights - LEARN_RATE * bias_momentum
    head_momentum = DECAY * head_moments + head_sum
    head_new = head_bias - LEARN_RATE * head_momentum
    left_factors = left_all[None]
    right_new = right_sum[None]
    return (
        loss_value,
        col_new,
        col_momentum,
        col_residue,
        row_new,
        row_momentum,
        row_residue,
        bias_new,
        bias_momentum,
        small_new,
        small_momentum,
        head_new,
        head_momentum,
        left_factors,
        right_new,
    )


def solution(mesh):
    fits = mesh.shape["dp"] == 8 and mesh.shape["tensor"] == 4
    placed = (
        P("dp", None, None),
        P("dp", None, None),
        P("dp"),
        P("dp"),
        P("dp", "tensor", None),
        P("dp", "tensor", None),
        P("dp", "tensor", None, None),
        P("tensor", None, "dp"),
        P("tensor", None, "dp"),
        P("dp", "tensor", None, None),
        P("tensor", None),
        P("tensor", None),
        P(None, "dp"),
        P(None, "dp"),
        P(),
        P(),
        P("tensor", None, None),
    )
    return jax.shard_map(
        shards if fits else shards_general,
        mesh=mesh,
        in_specs=placed,
        out_specs=(
            P(),
            P("dp", "tensor", None),
            P("dp", "tensor", None),
            P("dp", "tensor", None, None),
            P("tensor", None, "dp"),
            P("tensor", None, "dp"),
            P("dp", "tensor", None, None),
            P("tensor", None),
            P("tensor", None),
            P(None, "dp"),
            P(None, "dp"),
            P(),
            P(),
            P("tensor", None, None),
            P("tensor", None, None),
        ),
        check_vma=False,
    )
```

time: 472 us -> 318 us (0.67)
  blocking collectives: 114 us -> 0 us
  Pallas kernels: 188 us -> 289 us
  waiting for transfers between devices: 71 us -> 0 us
  local copies, waits for them, and re-layouts: 63.9 us -> 25.1 us
  between operations: 15.6 us -> 1 us
  other arithmetic: 10.6 us -> 2.31 us
    pallas_call x1 -> x2, Pallas kernels: 57 us -> 158 us  [the longest x1 99 us: run_gather(): pl.pallas_call(gather_kernel, out_shape=outs, in_specs=[any_spec] + [vm]...]
    all_gather x3 -> x0, blocking collectives: 71.9 us -> none  [the longest x1 33.7 us: shards(): lax.all_gather(jax.nn.silu(time_hidden), 'dp', axis=1, tiled=True)]
    all_gather x2 -> x0, waiting for transfers between devices: 70.3 us -> none  [the longest x1 70.3 us: shards(): lax.all_gather(lax.all_gather(packed, 'dp', axis=0, tiled=True), 'tensor'...]
    unnamed x3 -> x0, blocking collectives: 42.3 us -> none
    unnamed x95 -> x72, local copies, waits for them, and re-layouts: 45.5 us -> 20.7 us
    slice x19 -> x6, local copies, waits for them, and re-layouts: 6.59 us -> 0.8 us  [the longest x1 0.58 us: shards(): loss_value = gh[0, 1]]
  transfers between devices with their start and end apart: 4 -> 0, of which waited for: 1 -> 0; matrix products, arithmetic and copies ran while one was open for 8% -> 0% of each run, Pallas kernels for 0% -> 0%
where the time goes in v3:
time: 318 us
  Pallas kernels  289 us (91%)
  local copies, waits for them, and re-layouts  25.1 us (8%)
    pallas_call x1, Pallas kernels, run_block(): pl.pallas_call(functools.partial(block_kernel, count_all=count_all), grid...  117 us
    pallas_call x1, Pallas kernels, run_gather(): pl.pallas_call(gather_kernel, out_shape=outs, in_specs=[any_spec] + [vm]...  99 us
    pallas_call x1, Pallas kernels, run_grad(): pl.pallas_call(grad_kernel, out_shape=outs, in_specs=[any_spec] * 10 + [v...  59 us
    unnamed x72, local copies, waits for them, and re-layouts  20.7 us
    pallas_call x1, Pallas kernels, run_apply(): pl.pallas_call(functools.partial(apply_kernel, n=n), grid_spec=pltpu.Pref...  14.3 us

profile of v3, /device:TPU:0, one launch (start us, length us, event | category | flops | bytes accessed | tf_op | source)
XLA Modules:
  0.0 317.9 jit_solution(15073640398993726705)
XLA Ops:
  0.7 1.4 dynamic-slice_bitcast_fusion
  2.1 1.2 dynamic_slice.9.times_ref
  3.4 1.3 copy.44
  5.9 99.0 %gather.1 = (bf16[3,4,8,96,768]{4,3,2,1,0:T(8,128)(2,1)}, f32[4,8,768]{2,1,0:T(8,128)S(1)}, f32[40,768]{1,0:T(8,128)S(1)}, f32[4,1,1536]{2,1,0:T(1,128)S(1)}, f3...) custom-call(bf16[3,96,768]{2,1,0:T(8,128)(2,1)S(1)} %pad_maximum_fus, ...), custom_call_target="tpu_custom_call" | custom-call | tf_op jit(solution)/shard_map/gather/pallas_call | solution.py:550
  104.9 0.7 copy-done.7
  105.6 0.7 copy-done.13
  106.3 0.6 copy-done.14
  106.9 0.6 copy-done.15
  109.4 0.6 copy-done.19
  111.3 0.7 pad_maximum_fusion.1.pe_ref
  112.0 0.7 copy.35.bh_ref
  112.7 117.2 %block.1 = (bf16[4,256,768]{2,1,0:T(8,128)(2,1)}, bf16[4,256,768]{2,1,0:T(8,128)(2,1)}, bf16[4,256,768]{2,1,0:T(8,128)(2,1)}, bf16[4,256,768]{2,1,0:T(8,128)(2,1...) custom-call(s32[1]{0:T(128)} %bitcast.base_ref, ...), custom_call_target="tpu_custom_call" | custom-call | tf_op jit(solution)/shard_map/block/pallas_call | solution.py:225
  229.9 59.0 %grad.1 = (f32[2880,768]{1,0:T(8,128)}, f32[960,768]{1,0:T(8,128)}, f32[8,3264]{1,0:T(8,128)}, f32[8,4416]{1,0:T(8,128)}, bf16[128,768]{1,0:T(8,128)(2,1)}, /*in...) custom-call(bf16[1024,768]{1,0:T(8,128)(2,1)} %bitcast.77, ...), custom_call_target="tpu_custom_call" | custom-call | tf_op jit(solution)/shard_map/grad/pallas_call | solution.py:867
  288.9 3.3 %copy_bitcast_fusion = (f32[96,2880]{1,0:T(8,128)}, f32[96,2880]{1,0:T(8,128)}) fusion(f32[96,1,2880]{2,1,0:T(1,128)} %param.22, f32[96,1,2880]{2,1,0:T(1,128)} %param.21), kind=kLoop, calls=%fused_computation | loop fusion | bytes 4423680
  292.3 1.0 copy-done.8
  293.2 0.9 copy-done.10
  294.2 0.9 copy-done.11
  295.1 0.9 copy-done.12
  296.0 14.3 %apply.1 = (f32[2880,768]{1,0:T(8,128)}, f32[960,768]{1,0:T(8,128)}, f32[96,2880]{1,0:T(8,128)S(1)}, f32[96,2880]{1,0:T(8,128)}, f32[96,960]{1,0:T(8,128)}, /*in...) custom-call(s32[1]{0:T(128)} %bitcast.24.w_ref, f32[2880,768]{1,0:T(8,128)} %get-tuple-element.85.mcol_ref, ...), custom_call_target="tpu_custom_call" | custom-call | tf_op jit(solution)/shard_map/apply/pallas_call | solution.py:909
  310.3 2.2 copy.36
  312.5 2.2 copy.37
  314.7 0.6 multiply_subtract_fusion
  316.6 0.6 copy.47
  317.2 0.7 copy.48
  (82 shorter events, 5.5 us)
Async XLA Ops:
  0.6 4.0 %copy-start.2 = (f32[1,960,96]{1,2,0:T(8,128)S(1)}, f32[1,960,96]{1,2,0:T(8,128)}, u32[]{:S(2)}) copy-start(f32[1,960,96]{1,2,0:T(8,128)} %param.24) | copy-start | bytes 1105924
  4.7 0.7 copy-start.25
  4.7 0.9 copy-start.32
  4.7 1.1 copy-start.29
  4.7 1.1 copy-start.1
  5.0 107.0 %copy-start.30 = (f32[16]{0:T(128)S(1)}, f32[16]{0:T(128)}, u32[]{:S(2)}) copy-start(f32[16]{0:T(128)} %param.31) | copy-start | bytes 196
  5.6 224.3 %copy-start = (bf16[96,1536]{1,0:T(8,128)(2,1)}, bf16[96,1536]{1,0:T(8,128)(2,1)S(1)}, u32[]{:S(2)}) copy-start(bf16[96,1536]{1,0:T(8,128)(2,1)S(1)} %slice.44.wmod_ref) | copy-start | bytes 884740
  104.8 0.7 copy-start.7
  288.9 3.3 %copy-start.3 = (bf16[128,2944]{1,0:T(8,128)(2,1)S(1)}, bf16[128,2944]{1,0:T(8,128)(2,1)}, u32[]{:S(2)}) copy-start(bf16[128,2944]{1,0:T(8,128)(2,1)} %get-tuple-element.91.qsn_ref) | copy-start | bytes 2260996
  288.9 3.3 %copy-start.4 = (bf16[2880,128]{1,0:T(8,128)(2,1)S(1)}, bf16[2880,128]{1,0:T(8,128)(2,1)}, u32[]{:S(2)}) copy-start(bf16[2880,128]{1,0:T(8,128)(2,1)} %get-tuple-element.87.qst_ref) | copy-start | bytes 2211844
  288.9 3.3 %copy-start.5 = (f32[1093,96]{0,1:T(8,128)S(1)}, f32[1093,96]{0,1:T(8,128)}, u32[]{:S(2)}) copy-start(f32[1093,96]{0,1:T(8,128)} %param.30) | copy-start | bytes 1259140
  288.9 3.3 %copy-start.6 = (f32[96,1093]{1,0:T(8,128)S(1)}, f32[96,1093]{1,0:T(8,128)}, u32[]{:S(2)}) copy-start(f32[96,1093]{1,0:T(8,128)} %get-tuple-element.93.gs_ref) | copy-start | bytes 1259140
  288.9 3.3 %copy-start.9 = (bf16[128,960]{1,0:T(8,128)(2,1)S(1)}, bf16[128,960]{1,0:T(8,128)(2,1)}, u32[]{:S(2)}) copy-start(bf16[128,960]{1,0:T(8,128)(2,1)} %get-tuple-element.90.pc_ref) | copy-start | bytes 737284
  292.2 1.0 copy-start.8
  293.2 0.9 copy-start.10
  294.2 0.9 copy-start.11
  295.1 0.9 copy-start.12
  310.3 2.2 copy-start.22
  312.5 2.2 copy-start.26
  312.5 2.2 copy-start.27
  312.5 2.8 copy-start.28
  312.5 3.0 copy-start.31
  312.5 4.1 %copy-start.24 = (f32[8,3264]{1,0:T(8,128)S(1)}, f32[8,3264]{1,0:T(8,128)}, u32[]{:S(2)}) copy-start(f32[8,3264]{1,0:T(8,128)} %get-tuple-element.103) | copy-start | bytes 313348
  312.5 4.7 %copy-start.23 = (f32[8,4416]{1,0:T(8,128)S(1)}, f32[8,4416]{1,0:T(8,128)}, u32[]{:S(2)}) copy-start(f32[8,4416]{1,0:T(8,128)} %get-tuple-element.104) | copy-start | bytes 423940
  (9 other events, 5.6 us)

commit v4 on v3

--- a/solution.py
+++ b/solution.py
@@ -57,180 +57,251 @@
 
 def colsum(v): return jnp.sum(v,axis=0,keepdims=True)
 
-def block_kernel(base_ref,times_ref,clean_ref,noise_ref,mod_ref,wall_ref,pe_ref,emb_ref,bh_ref,ball_ref,
-           a_ref,m_ref,dy_ref,dz_ref,o_ref,dq_ref,du_ref,g_ref,dmod_ref,small_ref,dbq_ref,db1_ref,hb_ref,
-           pe_s,r_s,p_s,gp_s,xh1_s,xh2_s,y_s,z_s,h_s,acc_s,r1_s,r2_s,*,count_all):
-    step=pl.program_id(0)
-    base=base_ref[0]
-    t=times_ref[step]
-    lo=lax.broadcasted_iota(jnp.int32,(1,128),1)<64
-    @pl.when(step==0)
-    def _():
-        small_ref[...]=jnp.zeros_like(small_ref); dbq_ref[...]=jnp.zeros_like(dbq_ref); db1_ref[...]=jnp.zeros_like(db1_ref)
-        hb_ref[...]=jnp.zeros_like(hb_ref)
+UNROLL=dict(af=2,ff=4,fb=4,ab=4)
+
+def block_state():
+    V=pltpu.VMEM
+    return dict(
+        wall=V((3,4,D,D),BF), pe=V((SEQ,D),F32), qkv=V((4,4,SEQ,640),BF), p=V((4,12,SEQ,SEQ),BF),
+        xh1=V((4,SEQ,D),F32), y=V((4,SEQ,D),F32), h=V((4,SEQ,D),F32), r1=V((4,SEQ,1),F32),
+        xh2=V((SEQ,D),F32), z=V((SEQ,D),F32), r2=V((SEQ,1),F32), slope=V((4,SEQ,D),F32),
+        a=V((SEQ,D),BF), m=V((SEQ,D),BF), dz=V((SEQ,D),BF), dy=V((SEQ,D),BF),
+        o=V((4,SEQ,256),BF), g=V((4,SEQ,D),BF), du=V((4,SEQ,D),BF), dq=V((4,SEQ,640),BF),
+        dbq=V((4,1,640),F32), db1=V((4,1,D),F32), out_sem=pltpu.SemaphoreType.DMA((8,)))
+
+class Block:
+    def __init__(self,s,times,clean,noise,mod,pe,emb,bh,ball,outs,dmod,small,hb,base,first,count_all,service):
+        self.s=s; self.times=times; self.clean=clean; self.noise=noise; self.mod_ref=mod; self.pe=pe; self.emb=emb; self.bh=bh; self.ball=ball
+        self.outs=outs; self.dmod=dmod; self.small=small; self.hb=hb; self.base=base; self.first=first; self.count_all=count_all; self.service=service
+        self.lo=lax.broadcasted_iota(jnp.int32,(1,128),1)<64
+        self.zero=jnp.zeros((),BF)
+    def roll(self,v): return pltpu.roll(v.astype(F32),64,1).astype(BF)
+    def out(self,lat,name,index,pair):
+        s=self.s
+        src=s[name].at[pl.ds(self.base,2)] if pair else s[name]
+        dst=self.outs[index].at[:,lat] if pair else self.outs[index].at[lat]
+        return pltpu.make_async_copy(src,dst,s["out_sem"].at[index])
+    def emit(self,lat,name,index,pair=False): self.out(lat,name,index,pair).start()
+    def clear(self,lat,name,index,pair=False):
+        @pl.when(lat>0)
+        def _(): self.out(lat-1,name,index,pair).wait()
+    def last(self):
+        for name,index,pair in (("a",0,False),("m",1,False),("dy",2,False),("dz",3,False),("o",4,True),("dq",5,True),("du",6,True),("g",7,True)):
+            self.out(3,name,index,pair).wait()
+    def start(self):
+        s=self.s
+        self.small[...]=jnp.zeros_like(self.small); self.hb[...]=jnp.zeros_like(self.hb)
+        s["dbq"][...]=jnp.zeros_like(s["dbq"]); s["db1"][...]=jnp.zeros_like(s["db1"])
         for i in range(GRID):
-            pe_s[16*i:16*i+16,0:384]=jnp.broadcast_to(pe_ref[i:i+1,:],(16,384))
-            pe_s[16*i:16*i+16,384:768]=pe_ref[...]
-    clean=clean_ref[0].astype(F32); noise=noise_ref[0].astype(F32)
-    mixed=(t*clean+(1.0-t)*noise).astype(BF)
-    mod=lambda i: mod_ref[0,i:i+1,:]
-    wp=emb_ref[0:16].astype(BF); wh=emb_ref[16:32].astype(BF)
-    h0=tdot(mixed,wp)+emb_ref[32:33]+pe_s[...]
-    h_s[...]=h0
-    xh,r=ln(h0)
-    xh1_s[...]=xh; r1_s[...]=r
-    a_ref[0]=(xh*(1.0+mod(1))+mod(0)).astype(BF)
-    y_s[...]=jnp.zeros_like(y_s)
-    zero=jnp.zeros((),BF)
-    roll=lambda v: pltpu.roll(v.astype(F32),64,1).astype(BF)
-    def softmax_store(s,idx):
-        s=s*SCALE
-        e=jnp.exp(s-jnp.max(s,axis=-1,keepdims=True))
-        p=e/jnp.sum(e,axis=-1,keepdims=True)
-        p_s[idx]=p
-        return p.astype(BF)
-    @pl.loop(0,4)
-    def _(j):
-        own=(j>=base)&(j<base+2)
-        k=j-base
-        r_s[j]=(dot(a_ref[0],wall_ref[0,j])+ball_ref[j,:,0:768]).astype(BF)
-        blk=lambda i: r_s[j,:,128*i:128*(i+1)]
-        b0,b1,b2,b3,b4=[blk(i) for i in range(5)]
-        p0=softmax_store(ndot(jnp.where(lo,b0,zero),roll(b0)),3*j)
-        p1=softmax_store(ndot(jnp.where(lo,zero,b1),roll(b2)),3*j+1)
-        p2=softmax_store(ndot(jnp.where(lo,b3,zero),roll(b3)),3*j+2)
-        o01=jnp.where(lo,dot(p0,b1),dot(p1,b2)).astype(BF)
-        o2=jnp.where(lo,dot(p2,b4),0.0).astype(BF)
-        @pl.when(own)
-        def _():
-            o_ref[k,0,:,0:128]=o01; o_ref[k,0,:,128:256]=o2
-        ro=roll(o01)
-        ob4=jnp.where(lo,zero,ro)
-        ob5=jnp.where(lo,ro,roll(o2))
-        y_s[...]+=ndot(jnp.concatenate([ob4,ob5],axis=1),wall_ref[0,j,:,512:768])
-    y=y_s[...]+emb_ref[33:34]
-    y_s[...]=y
-    h1=h_s[...]+mod(2)*y
-    h_s[...]=h1
-    xh,r=ln(h1)
-    xh2_s[...]=xh; r2_s[...]=r
-    m_ref[0]=(xh*(1.0+mod(4))+mod(3)).astype(BF)
-    z_s[...]=jnp.zeros_like(z_s)
-    @pl.loop(0,4)
-    def _(j):
-        own=(j>=base)&(j<base+2)
-        k=j-base
-        u=dot(m_ref[0],wall_ref[1,j])+ball_ref[j,:,768:1536]
+            s["pe"][16*i:16*i+16,0:384]=jnp.broadcast_to(self.pe[i:i+1,:],(16,384))
+            s["pe"][16*i:16*i+16,384:768]=self.pe[...]
+    def mixed(self,lat):
+        place=self.first+lat
+        t=self.times[place]
+        clean=self.clean[place].astype(F32); noise=self.noise[place].astype(F32)
+        return t,clean,noise,(t*clean+(1.0-t)*noise).astype(BF)
+    def mod(self,lat,i): return self.mod_ref[lat,i:i+1,:]
+    def embed(self,lat):
+        s=self.s
+        mixed=self.mixed(lat)[3]
+        h0=tdot(mixed,self.emb[0:16].astype(BF))+self.emb[32:33]+s["pe"][...]
+        s["h"][lat]=h0
+        xh,r=ln(h0)
+        s["xh1"][lat]=xh; s["r1"][lat]=r
+        self.clear(lat,"a",0)
+        s["a"][...]=(xh*(1.0+self.mod(lat,1))+self.mod(lat,0)).astype(BF)
+        self.emit(lat,"a",0)
+        self.clear(lat,"o",4,True)
+    def softmax(self,v,lat,idx):
+        v=v*SCALE
+        e=jnp.exp(v-jnp.max(v,axis=-1,keepdims=True))
+        p=(e/jnp.sum(e,axis=-1,keepdims=True)).astype(BF)
+        self.s["p"][lat,idx]=p
+        return p
+    def attend(self,lat,j):
+        s=self.s; lo=self.lo; zero=self.zero; wall=s["wall"]
+        full=(dot(s["a"][...],wall[0,j])[:,0:640]+self.ball[j,:,0:640]).astype(BF)
+        s["qkv"][lat,j]=full
+        b0,b1,b2,b3,b4=[full[:,128*i:128*i+128] for i in range(5)]
+        p0=self.softmax(ndot(jnp.where(lo,b0,zero),self.roll(b0)),lat,3*j)
+        p1=self.softmax(ndot(jnp.where(lo,zero,b1),self.roll(b2)),lat,3*j+1)
+        p2=self.softmax(ndot(jnp.where(lo,b3,zero),self.roll(b3)),lat,3*j+2)
+        o0=pltpu.roll(dot(p0,b1),64,1)
+        s["o"][j,:,0:128]=jnp.where(lo,0.0,o0).astype(BF)
+        s["o"][j,:,128:256]=pltpu.roll(jnp.where(lo,dot(p2,b4),dot(p1,b2)),64,1).astype(BF)
+    def project(self,lat):
+        s=self.s
+        self.emit(lat,"o",4,True)
+        for n in range(3):
+            cols=slice(256*n,256*n+256)
+            y=sum(ndot(s["o"][j],s["wall"][0,j,cols,512:768]) for j in range(4))+self.emb[33:34,cols]
+            s["y"][lat,:,cols]=y
+            s["h"][lat,:,cols]+=self.mod(lat,2)[:,cols]*y
+    def attn_fwd(self,lat):
+        self.service(lat,0)
+        self.embed(lat)
+        self.service(lat,1)
+        for j in range(2): self.attend(lat,j)
+        self.service(lat,2)
+        for j in range(2,4): self.attend(lat,j)
+        self.service(lat,3)
+        self.project(lat)
+    def fc_in(self,lat):
+        s=self.s
+        xh,r=ln(s["h"][lat])
+        s["xh2"][...]=xh; s["r2"][...]=r
+        self.clear(lat,"m",1)
+        s["m"][...]=(xh*(1.0+self.mod(lat,4))+self.mod(lat,3)).astype(BF)
+        self.emit(lat,"m",1)
+        self.clear(lat,"g",7,True)
+    def fc_one(self,lat,j):
+        s=self.s
+        u=dot(s["m"][...],s["wall"][1,j])+self.ball[j,:,768:1536]
         uu=u*u
-        th=jnp.tanh(GELU_C*(u+0.044715*(uu*u)))
-        cdf=0.5*(1.0+th)
-        g=(u*cdf).astype(BF)
-        gp_s[j]=cdf+0.5*u*(1.0-th*th)*(GELU_C*(1.0+3.0*0.044715*uu))
-        @pl.when(own)
-        def _(): g_ref[k,0]=g
-        z_s[...]+=ndot(g,wall_ref[2,j])
-    z=z_s[...]+emb_ref[34:35]
-    z_s[...]=z
-    h2=h_s[...]+mod(5)*z
-    xh,r=ln(h2)
-    fi=(xh*(1.0+mod(7))+mod(6)).astype(BF)
-    pred=ndot(wh,fi)+bh_ref[...]
-    diff=pred-(clean-noise)
-    weight=1.0/(1.0-t+0.25)
-    hb_ref[0:1,1:2]+=jnp.sum(colsum(weight*diff*diff),axis=1,keepdims=True)*(1.0/count_all)
-    dpred=2.0*weight*diff*(1.0/count_all)
-    hb_ref[:,0:1]+=jnp.sum(dpred,axis=1,keepdims=True)
-    dpl=dpred.astype(BF)
-    small_ref[16:32]+=dot(dpl,fi)
-    dfi=tdot(dpl,wh)
-    dmod_ref[0,6:7]=colsum(dfi); dmod_ref[0,7:8]=colsum(dfi*xh)
-    dh=ln_back(dfi,xh,r,mod(7))
-    h_s[...]=dh
-    dmod_ref[0,5:6]=colsum(dh*z_s[...])
-    dzf=dh*mod(5)
-    small_ref[34:35]+=colsum(dzf)
-    dz_ref[0]=dzf.astype(BF)
-    acc_s[...]=jnp.zeros_like(acc_s)
-    @pl.loop(0,4)
-    def _(j):
-        own=(j>=base)&(j<base+2)
-        k=j-base
-        du=dot(dz_ref[0],wall_ref[2,j])*gp_s[j]
-        dul=du.astype(BF)
-        @pl.when(own)
-        def _():
-            du_ref[k,0]=dul
-            db1_ref[k]+=colsum(du)
-        acc_s[...]+=ndot(dul,wall_ref[1,j])
-    dm=acc_s[...]
-    xh=xh2_s[...]
-    dmod_ref[0,3:4]=colsum(dm); dmod_ref[0,4:5]=colsum(dm*xh)
-    dh=h_s[...]+ln_back(dm,xh,r2_s[...],mod(4))
-    h_s[...]=dh
-    dmod_ref[0,2:3]=colsum(dh*y_s[...])
-    dyf=dh*mod(2)
-    small_ref[33:34]+=colsum(dyf)
-    dy_ref[0]=dyf.astype(BF)
-    acc_s[...]=jnp.zeros_like(acc_s)
-    @pl.loop(0,4)
-    def _(j):
-        own=(j>=base)&(j<base+2)
-        k=j-base
-        do=dot(dy_ref[0],wall_ref[0,j,:,512:768]).astype(BF)
-        r4=roll(do[:,0:128]); r5=roll(do[:,128:256])
+        th=jnp.tanh(u*(GELU_C+(GELU_C*0.044715)*uu))
+        half=0.5+0.5*th
+        s["g"][j]=(u*half).astype(BF)
+        s["slope"][j]=half*(1.0+(u-u*th)*(GELU_C+(3.0*0.044715*GELU_C)*uu))
+    def fc_fwd(self,lat):
+        s=self.s
+        self.fc_in(lat)
+        u=UNROLL["ff"]
+        @pl.loop(0,4//u)
+        def _(i):
+            for k in range(u): self.fc_one(lat,i*u+k)
+        self.emit(lat,"g",7,True)
+        for n in range(3):
+            cols=slice(256*n,256*n+256)
+            z=sum(ndot(s["g"][j],s["wall"][2,j,cols,:]) for j in range(4))+self.emb[34:35,cols]
+            s["z"][:,cols]=z
+    def head(self,lat):
+        s=self.s; mod=lambda i: self.mod(lat,i)
+        t,clean,noise,_=self.mixed(lat)
+        wh=self.emb[16:32].astype(BF)
+        h2=s["h"][lat]+mod(5)*s["z"][...]
+        xh,r=ln(h2)
+        fi=(xh*(1.0+mod(7))+mod(6)).astype(BF)
+        pred=ndot(wh,fi)+self.bh[...]
+        diff=pred-(clean-noise)
+        weight=1.0/(1.0-t+TIME_OFFSET)
+        self.hb[0:1,1:2]+=jnp.sum(colsum(weight*diff*diff),axis=1,keepdims=True)*(1.0/self.count_all)
+        dpred=2.0*weight*diff*(1.0/self.count_all)
+        self.hb[:,0:1]+=jnp.sum(dpred,axis=1,keepdims=True)
+        dpl=dpred.astype(BF)
+        self.small[16:32]+=dot(dpl,fi)
+        dfi=tdot(dpl,wh)
+        self.dmod[lat,6:7]=colsum(dfi); self.dmod[lat,7:8]=colsum(dfi*xh)
+        dh=ln_back(dfi,xh,r,mod(7))
+        s["h"][lat]=dh
+        self.dmod[lat,5:6]=colsum(dh*s["z"][...])
+        dzf=dh*mod(5)
+        self.small[34:35]+=colsum(dzf)
+        self.clear(lat,"dz",3)
+        s["dz"][...]=dzf.astype(BF)
+        self.emit(lat,"dz",3)
+        self.clear(lat,"du",6,True)
+    def fc_back_one(self,j):
+        s=self.s
+        du=dot(s["dz"][...],s["wall"][2,j])*s["slope"][j]
+        s["du"][j]=du.astype(BF)
+        s["db1"][j]+=colsum(du)
+    def fc_bwd(self,lat):
+        s=self.s; mod=lambda i: self.mod(lat,i)
+        u=UNROLL["fb"]
+        @pl.loop(0,4//u)
+        def _(i):
+            for k in range(u): self.fc_back_one(i*u+k)
+        self.emit(lat,"du",6,True)
+        for n in range(3):
+            cols=slice(256*n,256*n+256)
+            s["z"][:,cols]=sum(ndot(s["du"][j],s["wall"][1,j,cols,:]) for j in range(4))
+        dm=s["z"][...]
+        xh=s["xh2"][...]
+        self.dmod[lat,3:4]=colsum(dm); self.dmod[lat,4:5]=colsum(dm*xh)
+        dh=s["h"][lat]+ln_back(dm,xh,s["r2"][...],mod(4))
+        s["h"][lat]=dh
+        self.dmod[lat,2:3]=colsum(dh*s["y"][lat])
+        dyf=dh*mod(2)
+        self.small[33:34]+=colsum(dyf)
+        self.clear(lat,"dy",2)
+        s["dy"][...]=dyf.astype(BF)
+        self.emit(lat,"dy",2)
+        self.clear(lat,"dq",5,True)
+    def attend_back(self,lat,j):
+        s=self.s; lo=self.lo; zero=self.zero; roll=self.roll
+        do=dot(s["dy"][...],s["wall"][0,j,:,512:768])
+        r4=pltpu.roll(do[:,0:128],64,1).astype(BF); r5=pltpu.roll(do[:,128:256],64,1).astype(BF)
         do0=jnp.where(lo,r4,zero); do1=jnp.where(lo,zero,r5); do2=jnp.where(lo,r5,zero)
-        blk=lambda i: r_s[j,:,128*i:128*(i+1)]
-        b0,b1,b2,b3,b4=[blk(i) for i in range(5)]
-        def head(h,doh,v,):
-            p=p_s[3*j+h]
-            dv=tdot(p.astype(BF),doh)
+        b0,b1,b2,b3,b4=[s["qkv"][lat,j,:,128*i:128*i+128] for i in range(5)]
+        def head(h,doh,v):
+            p=s["p"][lat,3*j+h]
+            dv=tdot(p,doh)
             dp=ndot(doh,v)
-            ds=(p*(dp-jnp.sum(p*dp,axis=-1,keepdims=True))).astype(BF)
+            pf=p.astype(F32)
+            t=pf*dp
+            ds=(t-pf*jnp.sum(t,axis=-1,keepdims=True)).astype(BF)
             return dv,ds
         dv0,ds0=head(0,do0,b1)
         dv1,ds1=head(1,do1,b2)
         dv2,ds2=head(2,do2,b4)
         rb0=roll(b0); rb3=roll(b3)
         n0=jnp.where(lo,dot(ds0,rb0),tdot(ds0,rb0))*SCALE
-        dq1=dot(ds1,roll(b2))*SCALE; dk1=tdot(ds1,roll(b1))*SCALE
-        n1=jnp.where(lo,dv0,dq1); n2=jnp.where(lo,dk1,dv1)
+        n1=jnp.where(lo,dv0,dot(ds1,roll(b2))*SCALE); n2=jnp.where(lo,tdot(ds1,roll(b1))*SCALE,dv1)
         n3=jnp.where(lo,dot(ds2,rb3),tdot(ds2,rb3))*SCALE
         n4=jnp.where(lo,dv2,0.0)
-        dqkv=jnp.concatenate([n0,n1,n2,n3,n4],axis=1)
-        dl=dqkv.astype(BF)
-        @pl.when(own)
-        def _():
-            dq_ref[k,0]=dl
-            dbq_ref[k]+=colsum(dqkv)
-        acc_s[...]+=ndot(dl,wall_ref[0,j,:,0:640])
-    da=acc_s[...]
-    xh=xh1_s[...]
-    dmod_ref[0,0:1]=colsum(da); dmod_ref[0,1:2]=colsum(da*xh)
-    dh=h_s[...]+ln_back(da,xh,r1_s[...],mod(1))
-    small_ref[32:33]+=colsum(dh)
-    small_ref[0:16]+=dot(mixed,dh.astype(BF))
+        for i,v in enumerate((n0,n1,n2,n3,n4)):
+            cols=slice(128*i,128*i+128)
+            s["dq"][j,:,cols]=v.astype(BF)
+            s["dbq"][j,:,cols]+=colsum(v)
+    def attn_bwd(self,lat):
+        s=self.s; mod=lambda i: self.mod(lat,i)
+        u=UNROLL["ab"]
+        @pl.loop(0,4//u)
+        def _(i):
+            for k in range(u): self.attend_back(lat,i*u+k)
+        self.emit(lat,"dq",5,True)
+        for n in range(3):
+            cols=slice(256*n,256*n+256)
+            s["z"][:,cols]=sum(ndot(s["dq"][j],s["wall"][0,j,cols,0:640]) for j in range(4))
+        da=s["z"][...]
+        xh=s["xh1"][lat]
+        self.dmod[lat,0:1]=colsum(da); self.dmod[lat,1:2]=colsum(da*xh)
+        dh=s["h"][lat]+ln_back(da,xh,s["r1"][lat],mod(1))
+        self.small[32:33]+=colsum(dh)
+        self.small[0:16]+=dot(self.mixed(lat)[3],dh.astype(BF))
+
+    def run(self,ready=lambda: None):
+        @pl.loop(0,4)
+        def _(lat): self.attn_fwd(lat)
+        ready()
+        @pl.loop(0,4)
+        def _(lat):
+            for phase in (self.fc_fwd,self.head,self.fc_bwd,self.attn_bwd): phase(lat)
+        self.last()
+
+def block_kernel(times_ref,base_ref,clean_ref,noise_ref,mod_ref,wall_ref,pe_ref,emb_ref,bh_ref,ball_ref,*rest,count_all,names):
+    outs=rest[0:8]; dmod,small,dbq,db1,hb=rest[8:13]
+    s=dict(zip(names,rest[13:13+len(names)])); wsem=rest[-1]
+    cp=pltpu.make_async_copy(wall_ref,s["wall"],wsem); cp.start()
+    base=base_ref[0]
+    b=Block(s,times_ref,clean_ref,noise_ref,mod_ref,pe_ref,emb_ref,bh_ref,ball_ref,outs,dmod,small,hb,base,0,count_all,lambda lat,pos: None)
+    b.start()
+    cp.wait()
+    b.run()
+    for k in range(2):
+        dbq[k]=s["dbq"][base+k]; db1[k]=s["db1"][base+k]
 
 def run_block(base,times,clean,noise,mod,wall,pe,emb,bh,ball,count_all):
     L=clean.shape[0]
-    full=lambda a: pl.BlockSpec(a.shape,lambda i,*_: (0,)*a.ndim,pipeline_mode=pl.Buffered(1))
-    lat=lambda *s: pl.BlockSpec((1,)+s,lambda i,*_:(i,)+(0,)*len(s))
-    pair=lambda w: pl.BlockSpec((2,1,SEQ,w),lambda i,*_:(0,i,0,0))
-    const=lambda *s: pl.BlockSpec(s,lambda i,*_:(0,)*len(s))
     S=jax.ShapeDtypeStruct
     outs=[S((L,SEQ,D),BF)]*4+[S((2,L,SEQ,256),BF),S((2,L,SEQ,640),BF),S((2,L,SEQ,768),BF),S((2,L,SEQ,768),BF),
         S((L,8,D),F32),S((40,D),F32),S((2,1,640),F32),S((2,1,768),F32),S((PATCH_IN,128),F32)]
-    ospecs=[lat(SEQ,D)]*4+[pair(256),pair(640),pair(768),pair(768),lat(8,D),const(40,D),const(2,1,640),const(2,1,768),const(PATCH_IN,128)]
-    V=pltpu.VMEM
-    f=lambda: V((SEQ,D),F32)
-    return pl.pallas_call(functools.partial(block_kernel,count_all=count_all),
-        grid_spec=pltpu.PrefetchScalarGridSpec(num_scalar_prefetch=2,grid=(L,),
-            in_specs=[lat(PATCH_IN,SEQ),lat(PATCH_IN,SEQ),lat(8,D)]+[full(v) for v in (wall,pe,emb,bh,ball)],
-            out_specs=ospecs,
-            scratch_shapes=[f(),V((4,SEQ,768),BF),V((12,SEQ,SEQ),F32),V((4,SEQ,768),F32),f(),f(),f(),f(),f(),f(),V((SEQ,1),F32),V((SEQ,1),F32)]),
-        out_shape=outs,
-        compiler_params=pltpu.CompilerParams(vmem_limit_bytes=60*1024*1024),
-        name="block",
-    )(base,times,clean,noise,mod,wall,pe,emb,bh,ball)
+    st=block_state(); names=tuple(st)
+    vm=pl.BlockSpec(memory_space=pltpu.VMEM); anys=pl.BlockSpec(memory_space=pl.ANY); sm=pl.BlockSpec(memory_space=pltpu.SMEM)
+    return pl.pallas_call(functools.partial(block_kernel,count_all=count_all,names=names),
+        out_shape=outs,in_specs=[sm,sm,vm,vm,vm,anys,vm,vm,vm,vm],out_specs=[anys]*8+[vm]*5,
+        scratch_shapes=list(st.values())+[pltpu.SemaphoreType.DMA(())],
+        compiler_params=pltpu.CompilerParams(vmem_limit_bytes=62*1024*1024),name="block")(times,base,clean,noise,mod,wall,pe,emb,bh,ball)
 
 
 MESH = pl.DeviceIdType.MESH
@@ -341,20 +412,31 @@
     return jnp.concatenate(rows + [jnp.zeros((total - used, rows[0].shape[1]), F32)], axis=0)
 
 
-def gather_kernel(
-    pack_ref, pk_ref, smt_ref, wmod_ref, brow_ref, bmod_ref,
-    wall_ref, mod_ref, emb_ref, ball_ref, cs_ref, ct_ref, t1_ref, a1_ref, tf_ref, hot_ref, wto_ref,
-    pkl, ems, eml, a1s, a1l, css, csl, mps, mpl_, mos, mol, bal,
-    local_sem, wsend, wrecv, send_sem, recv_sem,
+AUX = ("cs", "ct", "t1", "a1", "tf", "hot", "wto", "dmod", "small", "dbq", "db1", "hb")
+
+
+def step_kernel(
+    pack_ref, pk_ref, smt_ref, wmod_ref, brow_ref, bmod_ref, times_ref, clean_ref, noise_ref, pe_ref, bh_ref, *rest, names, count_all
 ):
+    outs, aux_out, rest = rest[:8], rest[8 : 8 + len(AUX)], rest[8 + len(AUX) :]
+    s = dict(zip(names, rest[: len(names)]))
+    aux, rest = dict(zip(AUX, rest[len(names) :])), rest[len(names) + len(AUX) :]
+    mod_ref, emb_ref, ball_ref = rest[:3]
+    pkl, ems, eml, a1s, a1l, css, csl, mps, mpl_, mos, mol, bal, local_sem, wsend, wrecv, send_sem, recv_sem = rest[3:]
+    wall_ref = s["wall"]
+    cs_ref, ct_ref, t1_ref, a1_ref, tf_ref, hot_ref, wto_ref = [aux[name] for name in AUX[:7]]
     net = Peers(send_sem, recv_sem)
     w, t, c, n = net.w, net.t, net.c, net.n
     share = D // n
     half = share // 2
     x, z, y = t // 2, w // 2, lax.rem(w, 2)
     own = []
+
+    def place(q, j, v):
+        return wall_ref.at[q, j, pl.ds(pl.multiple_of(share * v, 32), share)]
+
     for q in range(3):
-        op = pltpu.make_async_copy(pack_ref.at[q], wall_ref.at[q, t, w], local_sem.at[q])
+        op = pltpu.make_async_copy(pack_ref.at[q], place(q, t, w), local_sem.at[q])
         op.start()
         own.append(op)
     net.barrier()
@@ -376,40 +458,38 @@
     zs = [z, z + 1 - 2 * lax.rem(z, 2), lax.rem(z + 2, 4), 3 - z]
     xo = 1 - x
     mine, across = 2 * x + c, 2 * xo + c
-    wy = lambda k: 2 * zs[k] + y
-    wo = lambda k: 2 * zs[k] + (1 - y)
-    to_z = lambda k: (2 * zs[k] + y, t)
+    wys = [2 * zs[k] + y for k in range(4)]
+    wos = [2 * zs[k] + (1 - y) for k in range(4)]
+    to_zs = [(wys[k], t) for k in range(4)]
+    wy, wo, to_z = wys.__getitem__, wos.__getitem__, to_zs.__getitem__
     to_x, to_y, to_core = (w, across), (2 * z + (1 - y), t), (w, net.sib)
     sends = []
 
-    def send(q, j, v, device, src=None):
-        slot = wall_ref.at[q, j, v]
-        op = pltpu.make_async_remote_copy(
-            src_ref=slot if src is None else src, dst_ref=slot, send_sem=wsend.at[len(sends)],
+    def piece_copy(index, q, j, v, device, own_block):
+        slot = place(q, j, v)
+        return pltpu.make_async_remote_copy(
+            src_ref=pack_ref.at[q] if own_block else slot, dst_ref=slot, send_sem=wsend.at[index],
             recv_sem=wrecv.at[q, j, v], device_id=device, device_id_type=MESH,
         )
-        op.start()
-        sends.append(op)
+
+    def send(q, j, v, device, own_block=False):
+        sends.append((len(sends), q, j, v, device, own_block))
+        piece_copy(*sends[-1]).start()
 
     def arrived(q, j, v):
-        slot = wall_ref.at[q, j, v]
-        pltpu.make_async_remote_copy(
-            src_ref=slot, dst_ref=slot, send_sem=wsend.at[0], recv_sem=wrecv.at[q, j, v], device_id=to_core, device_id_type=MESH
-        ).wait_recv()
+        piece_copy(0, q, j, v, to_core, False).wait_recv()
 
     def column(q, k):
         if k == 0:
-            src = pack_ref.at[q]
-            send(q, mine, w, to_z(1), src)
-            send(q, mine, w, to_z(2), src)
+            send(q, mine, w, to_z(1), True)
+            send(q, mine, w, to_z(2), True)
         else:
-            src = None
             arrived(q, mine, wy(k))
             if k == 2:
                 send(q, mine, wy(2), to_z(1))
-        send(q, mine, wy(k), to_x, src)
-        send(q, mine, wy(k), to_y, src)
-        send(q, mine, wy(k), to_core, src)
+        send(q, mine, wy(k), to_x, k == 0)
+        send(q, mine, wy(k), to_y, k == 0)
+        send(q, mine, wy(k), to_core, k == 0)
 
     def by_y(q, k):
         return (q * 4 + k) % 3 == 0
@@ -510,52 +590,105 @@
                 for piece in range(2):
                     mod_ref[lat, 2 * j + piece : 2 * j + piece + 1, :] = mol[j, pl.ds(4 * c + lat, 1), D * piece : D * piece + D]
 
-    ops = None
-    stage(0)
+    column(0, 0)
+    column(0, 1)
     ops = chain0()
-    stage(1)
+    side(0, 0)
+    column(0, 2)
+    side(0, 1)
+    corner(0, 0)
+    column(0, 3)
+    side(0, 2)
+    corner(0, 1)
+    column(1, 0)
+    column(2, 0)
     cs_ops, ops = chain1(ops)
-    stage(2)
+    side(0, 3)
+    corner(0, 2)
+    corner(0, 3)
+    for k in range(1, 4):
+        column(1, k)
     ops = chain2(ops)
+    for k in range(1, 4):
+        column(2, k)
     chain3(cs_ops, ops)
-    for q in range(3):
+
+    def other_core(q):
         for j in (2 * x + 1 - c, 2 * xo + 1 - c):
             for v in range(n):
                 arrived(q, j, v)
-    for op in own:
+
+    other_core(0)
+    own[0].wait()
+    items = []
+    for q in (1, 2):
+        for k in range(4):
+            items.append(functools.partial(side, q, k))
+            items.append(functools.partial(corner, q, k))
+    early = [0, 2, 1, 4, 3, 6, 5, 7]
+    items = [items[i] for i in early] + [items[8 + i] for i in early]
+
+    def service(lat, pos):
+        for index, item in enumerate(items):
+            if index % 4 == pos:
+                pl.when(lat == index // 4)(item)
+
+    def ready():
+        for q in (1, 2):
+            other_core(q)
+            own[q].wait()
+
+    block = Block(
+        s, times_ref, clean_ref, noise_ref, mod_ref, pe_ref, emb_ref, bh_ref, ball_ref, outs,
+        aux["dmod"], aux["small"], aux["hb"], 2 * x, 4 * c, count_all, service,
+    )
+    block.start()
+    block.run(ready)
+    for k in range(2):
+        aux["dbq"][k] = s["dbq"][2 * x + k]
+        aux["db1"][k] = s["db1"][2 * x + k]
+    copies = [pltpu.make_async_copy(aux[name], aux_out[i], local_sem.at[3 + i]) for i, name in enumerate(AUX)]
+    for op in copies:
+        op.start()
+    for record in sends:
+        piece_copy(*record).wait_send()
+    net.finish()
+    for op in copies:
         op.wait()
-    for op in sends:
-        op.wait_send()
-    net.finish()
-
-
-def run_gather(pack, pk, smt, wmod, brow, bmod, n):
+
+
+def run_step(pack, pk, smt, wmod, brow, bmod, times, clean, noise, pe, bh, n, count_all):
     S = jax.ShapeDtypeStruct
     V = pltpu.VMEM
     DMA = pltpu.SemaphoreType.DMA
     share = D // n
     lat = 8 * n
+    half = 4
     any_spec = pl.BlockSpec(memory_space=pl.ANY)
     vm = pl.BlockSpec(memory_space=pltpu.VMEM)
-    outs = [
-        S((3, 4, n, share, D), BF), S((4, 8, D), F32), S((40, D), F32), S((4, 1, QKV0), F32), S((8, D), F32),
-        S((share, lat), F32), S((share, lat), F32), S((D, lat), F32), S((lat, FREQ), F32), S((lat, 128), F32), S((share, D), BF),
+    aux = [
+        ((8, D), F32), ((share, lat), F32), ((share, lat), F32), ((D, lat), F32), ((lat, FREQ), F32), ((lat, 128), F32), ((share, D), BF),
+        ((half, 8, D), F32), ((40, D), F32), ((2, 1, 640), F32), ((2, 1, D), F32), ((PATCH_IN, 128), F32),
     ]
-    scratch = [
+    outs = [S((half, SEQ, D), BF)] * 4 + [S((2, half, SEQ, width), BF) for width in (256, 640, D, D)]
+    outs += [S(*a) for a in aux]
+    state = block_state()
+    scratch = list(state.values()) + [V(*a) for a in aux] + [
+        V((half, 8, D), F32), V((40, D), F32), V((4, 1, QKV0), F32),
         V((n, 8, 384), F32), V((share // 3, 128), BF), V((n, share // 3, 128), BF),
         V((share // 2, 128), F32), V((n, share // 2, 128), F32), V((share // 2, 128), F32), V((n, share // 2, 128), F32),
         V((n, 8, QKV0), F32), V((n, 8, QKV0), F32), V((8, QKV0), F32), V((4, 8, QKV0), F32), V((4, 1, QKV0), F32),
-        DMA((3,)), DMA((120,)), DMA((3, 4, n)), DMA((41,)), DMA((41,)),
+        DMA((3 + len(AUX),)), DMA((120,)), DMA((3, 4, n)), DMA((41,)), DMA((41,)),
     ]
     return pl.pallas_call(
-        gather_kernel,
+        functools.partial(step_kernel, names=tuple(state), count_all=count_all),
         out_shape=outs,
-        in_specs=[any_spec] + [vm] * 5,
-        out_specs=[any_spec] + [vm] * 10,
+        in_specs=[any_spec] + [vm] * 5 + [pl.BlockSpec(memory_space=pltpu.SMEM)] + [vm] * 4,
+        out_specs=[any_spec] * len(outs),
         scratch_shapes=scratch,
-        compiler_params=pltpu.CompilerParams(collective_id=0, has_side_effects=True, vmem_limit_bytes=48 * 1024 * 1024),
-        name="gather",
-    )(pack, pk, smt, wmod, brow, bmod)
+        compiler_params=pltpu.CompilerParams(collective_id=0, has_side_effects=True, vmem_limit_bytes=62 * 1024 * 1024),
+        name="step",
+    )(pack, pk, smt, wmod, brow, bmod, times, clean, noise, pe, bh)
 
 
 def gram_schmidt(block):
@@ -642,7 +775,7 @@
     def _(i):
         sr[after(i, 192), :] = tdot(gv[1 - c, :, chunk(i)], dzv[...])
 
-    sr[0:192, :] = tdot(ov[1 - c], dyv[...])[0:192]
+    sr[0:192, :] = tdot(ov[1 - c], dyv[...])[64:256]
     row_ops.append(net.core_push(sr, rr, 6))
     total = small_ref[...] + smo[...]
     for k in range(n):
@@ -679,7 +812,7 @@
     def _(i):
         mr[after(i, 192), :] += tdot(gv[c, :, chunk(i)], dzv[...]) + rr[after(i, 192), :]
 
-    mr[0:192, :] += tdot(ov[c], dyv[...])[0:192] + rr[0:192, :]
+    mr[0:192, :] += tdot(ov[c], dyv[...])[64:256] + rr[0:192, :]
     out_row = pltpu.make_async_copy(mr, mrow_ref, load_sem.at[1])
     out_row.start()
     right = right_ref[...]
@@ -1094,7 +1227,7 @@
         return (
             tdot(flat(a), flat(pick(dq, which))[:, :qkv_width]),
             tdot(flat(m), flat(pick(du, which))),
-            tdot(flat(pick(o, which))[:, :proj_rows], flat(dy)),
+            tdot(flat(pick(o, which))[:, 64:], flat(dy)),
             tdot(flat(pick(g, which)), flat(dz)),
             pick(dbq, which)[0, :qkv_width],
             pick(db1, which)[0],
@@ -1254,25 +1387,10 @@
         axis=1,
     )
     small_t = small_weights.T
-    wall, mod, emb, ball, cs, ct, t1, a1, tf, hot, wto = run_gather(
-        packed, features, small_t, wmod, bias_row, bias_exact[:, :mod_width], data_size
-    )
-
-    def mine(values):
-        return lax.dynamic_slice_in_dim(values, core * half, half, 0)
-
-    a, m, dy, dz, o, dq, du, g, dmod, small, dbq, db1, hb = run_block(
-        base.reshape(1),
-        mine(timesteps),
-        mine(clean_latents.transpose(0, 2, 1)),
-        mine(noise_draw.transpose(0, 2, 1)),
-        mod,
-        wall.reshape(3, tensor_size, D, D),
-        position_table(),
-        emb,
-        rounded(head_bias)[:, None],
-        ball,
-        count_all,
+    a, m, dy, dz, o, dq, du, g, cs, ct, t1, a1, tf, hot, wto, dmod, small, dbq, db1, hb = run_step(
+        packed, features, small_t, wmod, bias_row, bias_exact[:, :mod_width], timesteps,
+        clean_latents.transpose(0, 2, 1), noise_draw.transpose(0, 2, 1), position_table(), rounded(head_bias)[:, None],
+        data_size, count_all,
     )
     rows = half * SEQ
 

time: 318 us -> 265 us (0.83)
  Pallas kernels: 289 us -> 242 us
  local copies, waits for them, and re-layouts: 25.1 us -> 17.8 us
    pallas_call x2 -> x1, Pallas kernels: 216 us -> 170 us  [run_step(): pl.pallas_call(functools.partial(step_kernel, names=tuple(state), count_a...]
    unnamed x72 -> x50, local copies, waits for them, and re-layouts: 20.7 us -> 14.1 us
where the time goes in v4:
time: 265 us
  Pallas kernels  242 us (91%)
  local copies, waits for them, and re-layouts  17.8 us (7%)
  other arithmetic  3.67 us (1%)
    pallas_call x1, Pallas kernels, run_step(): pl.pallas_call(functools.partial(step_kernel, names=tuple(state), count_a...  170 us
    pallas_call x1, Pallas kernels, run_grad(): pl.pallas_call(grad_kernel, out_shape=outs, in_specs=[any_spec] * 10 + [v...  57.8 us
    pallas_call x1, Pallas kernels, run_apply(): pl.pallas_call(functools.partial(apply_kernel, n=n), grid_spec=pltpu.Pref...  14.3 us
    unnamed x50, local copies, waits for them, and re-layouts  14.1 us

profile of v4, /device:TPU:0, one launch (start us, length us, event | category | flops | bytes accessed | tf_op | source)
XLA Modules:
  0.0 265.0 jit_solution(11215193618696185298)
XLA Ops:
  0.7 1.4 copy.44
  2.1 0.2 slice_bitcast_fusion
  2.4 0.8 pad_maximum_fusion.pack_ref
  3.3 0.7 concatenate.14.brow_ref
  4.0 0.7 slice.44.wmod_ref
  4.8 0.7 pad_maximum_fusion.1.pe_ref
  5.7 0.6 pad_maximum_fusion.2.pk_ref
  6.3 0.6 slice.47.bmod_ref
  7.0 0.7 copy.35.bh_ref
  7.6 170.4 %step.1 = (bf16[4,256,768]{2,1,0:T(8,128)(2,1)}, bf16[4,256,768]{2,1,0:T(8,128)(2,1)}, bf16[4,256,768]{2,1,0:T(8,128)(2,1)}, bf16[4,256,768]{2,1,0:T(8,128)(2,1)...) custom-call(bf16[3,96,768]{2,1,0:T(8,128)(2,1)} %pad_maximum_fusion., ...), custom_call_target="tpu_custom_call" | custom-call | tf_op jit(solution)/shard_map/step/pallas_call | solution.py:683
  178.1 57.8 %grad.1 = (f32[2880,768]{1,0:T(8,128)}, f32[960,768]{1,0:T(8,128)}, f32[8,3264]{1,0:T(8,128)}, f32[8,4416]{1,0:T(8,128)}, bf16[128,768]{1,0:T(8,128)(2,1)}, /*in...) custom-call(bf16[1024,768]{1,0:T(8,128)(2,1)} %bitcast.72, ...), custom_call_target="tpu_custom_call" | custom-call | tf_op jit(solution)/shard_map/grad/pallas_call | solution.py:1000
  235.9 3.3 %copy_bitcast_fusion = (f32[96,2880]{1,0:T(8,128)}, f32[96,2880]{1,0:T(8,128)}) fusion(f32[96,1,2880]{2,1,0:T(1,128)} %param.22, f32[96,1,2880]{2,1,0:T(1,128)} %param.21), kind=kLoop, calls=%fused_computation | loop fusion | bytes 4423680
  239.2 1.0 copy-done.6
  240.2 0.9 copy-done.8
  241.2 0.9 copy-done.9
  242.1 0.9 copy-done.10
  243.0 14.3 %apply.1 = (f32[2880,768]{1,0:T(8,128)}, f32[960,768]{1,0:T(8,128)}, f32[96,2880]{1,0:T(8,128)S(1)}, f32[96,2880]{1,0:T(8,128)}, f32[96,960]{1,0:T(8,128)}, /*in...) custom-call(s32[1]{0:T(128)} %bitcast.22.w_ref, f32[2880,768]{1,0:T(8,128)} %get-tuple-element.77.mcol_ref, ...), custom_call_target="tpu_custom_call" | custom-call | tf_op jit(solution)/shard_map/apply/pallas_call | solution.py:1042
  257.3 2.2 copy.36
  259.5 2.2 copy.37
  261.7 0.6 multiply_subtract_fusion
  262.4 0.5 multiply_subtract_fusion.1
  262.9 0.6 slice.38
  263.5 0.6 copy.47
  264.2 0.7 copy.48
  (57 shorter events, 0.7 us)
Async XLA Ops:
  0.6 1.4 copy-start.1
  2.0 1.2 copy-start.14
  2.1 3.5 %copy-start.18 = (f32[8]{0:T(128)S(1)}, f32[8]{0:T(128)}, u32[]{:S(2)}) copy-start(f32[8]{0:T(128)} %times_ref.1) | copy-start | bytes 100
  2.1 3.6 %copy-start.19 = (s32[8]{0:T(128)S(1)}, s32[8]{0:T(128)}, u32[]{:S(2)}) copy-start(s32[8]{0:T(128)} %param.20) | copy-start | bytes 100
  2.1 4.8 %copy-start.20 = (f32[16]{0:T(128)S(1)}, f32[16]{0:T(128)}, u32[]{:S(2)}) copy-start(f32[16]{0:T(128)} %param.31) | copy-start | bytes 196
  235.8 3.3 %copy-start = (f32[1093,96]{0,1:T(8,128)S(1)}, f32[1093,96]{0,1:T(8,128)}, u32[]{:S(2)}) copy-start(f32[1093,96]{0,1:T(8,128)} %param.29) | copy-start | bytes 1259140
  235.9 3.3 %copy-start.2 = (bf16[128,2944]{1,0:T(8,128)(2,1)S(1)}, bf16[128,2944]{1,0:T(8,128)(2,1)}, u32[]{:S(2)}) copy-start(bf16[128,2944]{1,0:T(8,128)(2,1)} %get-tuple-element.83.qsn_ref) | copy-start | bytes 2260996
  235.9 3.3 %copy-start.3 = (bf16[2880,128]{1,0:T(8,128)(2,1)S(1)}, bf16[2880,128]{1,0:T(8,128)(2,1)}, u32[]{:S(2)}) copy-start(bf16[2880,128]{1,0:T(8,128)(2,1)} %get-tuple-element.79.qst_ref) | copy-start | bytes 2211844
  235.9 3.3 %copy-start.4 = (f32[1093,96]{0,1:T(8,128)S(1)}, f32[1093,96]{0,1:T(8,128)}, u32[]{:S(2)}) copy-start(f32[1093,96]{0,1:T(8,128)} %param.30) | copy-start | bytes 1259140
  235.9 3.3 %copy-start.5 = (f32[96,1093]{1,0:T(8,128)S(1)}, f32[96,1093]{1,0:T(8,128)}, u32[]{:S(2)}) copy-start(f32[96,1093]{1,0:T(8,128)} %get-tuple-element.85.gs_ref) | copy-start | bytes 1259140
  235.9 3.3 %copy-start.7 = (bf16[128,960]{1,0:T(8,128)(2,1)S(1)}, bf16[128,960]{1,0:T(8,128)(2,1)}, u32[]{:S(2)}) copy-start(bf16[128,960]{1,0:T(8,128)(2,1)} %get-tuple-element.82.pc_ref) | copy-start | bytes 737284
  239.2 1.0 copy-start.6
  240.2 0.9 copy-start.8
  241.2 0.9 copy-start.9
  242.1 0.9 copy-start.10
  257.3 2.2 copy-start.11
  259.5 2.2 copy-start.15
  259.5 2.2 copy-start.16
  259.5 2.8 %copy-start.17 = (f32[16,128]{1,0:T(8,128)S(1)}, f32[16,128]{1,0:T(8,128)}, u32[]{:S(2)}) copy-start(f32[16,128]{1,0:T(8,128)} %get-tuple-element.76) | copy-start | bytes 24580
  259.5 3.0 %copy-start.21 = (f32[16]{0:T(128)S(1)}, f32[16]{0:T(128)}, u32[]{:S(2)}) copy-start(f32[16]{0:T(128)} %param.32) | copy-start | bytes 196
  259.5 4.1 %copy-start.13 = (f32[8,3264]{1,0:T(8,128)S(1)}, f32[8,3264]{1,0:T(8,128)}, u32[]{:S(2)}) copy-start(f32[8,3264]{1,0:T(8,128)} %get-tuple-element.95) | copy-start | bytes 313348
  259.5 4.7 %copy-start.12 = (f32[8,4416]{1,0:T(8,128)S(1)}, f32[8,4416]{1,0:T(8,128)}, u32[]{:S(2)}) copy-start(f32[8,4416]{1,0:T(8,128)} %get-tuple-element.96) | copy-start | bytes 423940

commit v5 on v4

--- a/solution.py
+++ b/solution.py
@@ -491,16 +491,16 @@
         send(q, mine, wy(k), to_y, k == 0)
         send(q, mine, wy(k), to_core, k == 0)
 
-    def by_y(q, k):
-        return (q * 4 + k) % 3 == 0
+    def by_y(k):
+        return k % 2 == 1
 
     def side(q, k):
         arrived(q, across, wy(k))
-        if by_y(q, k):
+        if by_y(k):
             send(q, across, wy(k), to_y)
         send(q, across, wy(k), to_core)
         arrived(q, mine, wo(k))
-        if not by_y(q, k):
+        if not by_y(k):
             send(q, mine, wo(k), to_x)
         send(q, mine, wo(k), to_core)
 
@@ -508,19 +508,38 @@
         arrived(q, across, wo(k))
         send(q, across, wo(k), to_core)
 
-    def stage(q):
-        column(q, 0)
-        column(q, 1)
-        side(q, 0)
-        column(q, 2)
-        side(q, 1)
-        corner(q, 0)
-        column(q, 3)
-        side(q, 2)
-        corner(q, 1)
-        side(q, 3)
-        corner(q, 2)
-        corner(q, 3)
+    first_hop = {1: to_x, 2: to_y}
+    last_hop = {1: to_y, 2: to_x}
+
+    def level(q, k):
+        return (mine, wy(k)), ((across, wy(k)) if q == 1 else (mine, wo(k)))
+
+    def begin(q):
+        send(q, mine, w, first_hop[q], True)
+        send(q, mine, w, to_z(1), True)
+        send(q, mine, w, to_z(2), True)
+        send(q, mine, w, last_hop[q], True)
+        send(q, mine, w, to_core, True)
+
+    def second(q):
+        j, v = level(q, 0)[1]
+        arrived(q, j, v)
+        for device in (to_z(1), to_z(2), last_hop[q], to_core):
+            send(q, j, v, device)
+
+    def along(q, k):
+        for j, v in level(q, k):
+            arrived(q, j, v)
+            if k == 2:
+                send(q, j, v, to_z(1))
+            send(q, j, v, last_hop[q])
+            send(q, j, v, to_core)
+
+    def far(q, k):
+        last = (mine, wo(k)) if q == 1 else (across, wy(k))
+        for j, v in (last, (across, wo(k))):
+            arrived(q, j, v)
+            send(q, j, v, to_core)
 
     def chain0():
         wait_all(pk_ops)
@@ -591,26 +610,24 @@
                     mod_ref[lat, 2 * j + piece : 2 * j + piece + 1, :] = mol[j, pl.ds(4 * c + lat, 1), D * piece : D * piece + D]
 
     column(0, 0)
+    ops = chain0()
     column(0, 1)
-    ops = chain0()
     side(0, 0)
     column(0, 2)
+    cs_ops, ops = chain1(ops)
     side(0, 1)
     corner(0, 0)
     column(0, 3)
     side(0, 2)
+    begin(1)
+    begin(2)
     corner(0, 1)
-    column(1, 0)
-    column(2, 0)
-    cs_ops, ops = chain1(ops)
     side(0, 3)
+    ops = chain2(ops)
     corner(0, 2)
     corner(0, 3)
-    for k in range(1, 4):
-        column(1, k)
-    ops = chain2(ops)
-    for k in range(1, 4):
-        column(2, k)
+    second(1)
+    second(2)
     chain3(cs_ops, ops)
 
     def other_core(q):
@@ -620,20 +637,25 @@
 
     other_core(0)
     own[0].wait()
-    items = []
-    for q in (1, 2):
-        for k in range(4):
-            items.append(functools.partial(side, q, k))
-            items.append(functools.partial(corner, q, k))
-    early = [0, 2, 1, 4, 3, 6, 5, 7]
-    items = [items[i] for i in early] + [items[8 + i] for i in early]
+    slots = {
+        0: [functools.partial(along, 1, 1)],
+        1: [functools.partial(along, 2, 1)],
+        4: [functools.partial(along, 1, 2)],
+        6: [functools.partial(along, 2, 2)],
+        11: [functools.partial(along, 1, 3)],
+        13: [functools.partial(along, 2, 3)],
+    }
+    rest = [functools.partial(far, q, k) for k in range(4) for q in (1, 2)]
 
     def service(lat, pos):
-        for index, item in enumerate(items):
+        for index, todo in slots.items():
             if index % 4 == pos:
-                pl.when(lat == index // 4)(item)
+                for item in todo:
+                    pl.when(lat == index // 4)(item)
 
     def ready():
+        for item in rest:
+            item()
         for q in (1, 2):
             other_core(q)
             own[q].wait()
@@ -705,12 +727,21 @@
 def grad_kernel(
     a_ref, m_ref, dy_ref, dz_ref, o_ref, dq_ref, du_ref, g_ref, cerr_ref, rerr_ref,
     dmod_ref, small_ref, dbq_ref, db1_ref, hb_ref, right_ref, cs_ref, ct_ref, t1_ref, a1_ref, tf_ref, hot_ref, wmod_ref, wto_ref,
-    mcol_ref, mrow_ref, left_ref, rightn_ref, pst_ref, psr_ref, pc_ref, qst_ref, qsn_ref, qrs_ref, gb_ref, gh_ref, gsm_ref,
+    mcol_ref, mrow_ref, left_out, rightn_out, pst_out, psr_out, pc_out, qst_out, qsn_out, qrs_out, gb_out, gh_out, gsm_out,
     mc, mr, sc, sr, rc, rr, av, mv, dyv, dzv, ov, qv, uv, gv,
+    left_ref, rightn_ref, pst_ref, psr_ref, pc_ref, qst_ref, qsn_ref, qrs_ref, gb_ref, gh_ref, gsm_ref,
     dmo, smo, dbo, dbo1, hbo, dm8, dma, dsc, dss, dts, dtl, tks, tkl, px, pland, py, qx, qland, qy,
-    load_sem, send_sem, recv_sem,
+    load_sem, out_sem, send_sem, recv_sem,
 ):
     net = Peers(send_sem, recv_sem)
+    outs = []
+
+    def emit(*pairs):
+        for src, dst in pairs:
+            op = pltpu.make_async_copy(src, dst, out_sem.at[len(outs)])
+            op.start()
+            outs.append(op)
+
     w, t, c = net.w, net.t, net.c
     n = net.n
     share = D // n
@@ -725,12 +756,6 @@
     load("a", a_ref, av, 1)
     load("u", du_ref, uv, 0)
     load("m", m_ref, mv, 2)
-    load("g", g_ref, gv, 3)
-    load("dz", dz_ref, dzv, 4)
-    load("o", o_ref, ov, 5)
-    load("dy", dy_ref, dyv, 6)
-    load("ce", cerr_ref, mc, 7)
-    load("re", rerr_ref, mr, 8)
     net.barrier()
     side = [
         net.core_push(dmod_ref, dmo, 0),
@@ -746,20 +771,6 @@
     def after(i, first):
         return pl.ds(pl.multiple_of(first + 256 * i, 64), 256)
 
-    for name in ("q", "a"):
-        loads[name].wait()
-    col_ops, row_ops = [], []
-    sc[0:256] = tdot(qv[1 - c, :, 0:256], av[...])
-    sc[256:576] = tdot(qv[1 - c, :, 256:640], av[...])[0:320]
-    col_ops.append(net.core_push(sc.at[0:576], rc.at[0:576], 3))
-    for name in ("u", "m"):
-        loads[name].wait()
-
-    @pl.loop(0, 3)
-    def _(i):
-        sc[after(i, 576), :] = tdot(uv[1 - c, :, chunk(i)], mv[...])
-
-    col_ops.append(net.core_push(sc.at[576:1344], rc.at[576:1344], 4))
     wait_all(side)
     for lat in range(4):
         for piece in range(2):
@@ -768,20 +779,40 @@
             dm8[pl.ds(4 * (1 - c) + lat, 1), span] = dmo[lat, pl.ds(2 * t + piece, 1), :]
     dma[w] = dm8[...]
     dm_ops = net.dp_push(lambda peer: dm8, dma.at[w], 16)
-    for name in ("g", "dz", "o", "dy"):
-        loads[name].wait()
-
-    @pl.loop(0, 3)
-    def _(i):
-        sr[after(i, 192), :] = tdot(gv[1 - c, :, chunk(i)], dzv[...])
-
-    sr[0:192, :] = tdot(ov[1 - c], dyv[...])[64:256]
-    row_ops.append(net.core_push(sr, rr, 6))
     total = small_ref[...] + smo[...]
     for k in range(n):
         tks[k, :, 0:share] = total[:, share * k : share * k + share]
     tkl[w] = tks[w]
     tok_ops = net.dp_push(lambda peer: tks.at[peer], tkl.at[w], 24)
+    load("g", g_ref, gv, 3)
+    load("dz", dz_ref, dzv, 4)
+    load("o", o_ref, ov, 5)
+    load("dy", dy_ref, dyv, 6)
+    for name in ("q", "a"):
+        loads[name].wait()
+    col_ops, row_ops = [], []
+    sc[0:256] = tdot(qv[1 - c, :, 0:256], av[...])
+    sc[256:576] = tdot(qv[1 - c, :, 256:640], av[...])[0:320]
+    col_ops.append(net.core_push(sc.at[0:576], rc.at[0:576], 3))
+    load("ce", cerr_ref, mc, 7)
+    for name in ("u", "m"):
+        loads[name].wait()
+
+    @pl.loop(0, 3)
+    def _(i):
+        sc[after(i, 576), :] = tdot(uv[1 - c, :, chunk(i)], mv[...])
+
+    col_ops.append(net.core_push(sc.at[576:1344], rc.at[576:1344], 4))
+    for name in ("g", "dz", "o", "dy"):
+        loads[name].wait()
+
+    @pl.loop(0, 3)
+    def _(i):
+        sr[after(i, 192), :] = tdot(gv[1 - c, :, chunk(i)], dzv[...])
+
+    sr[0:192, :] = tdot(ov[1 - c], dyv[...])[64:256]
+    row_ops.append(net.core_push(sr, rr, 6))
+    load("re", rerr_ref, mr, 8)
     loads["ce"].wait()
     dms = split3(dm8[...])
     cs = split3(cs_ref[...])
@@ -799,22 +830,22 @@
 
     out_col = pltpu.make_async_copy(mc, mcol_ref, load_sem.at[0])
     out_col.start()
+    loads["re"].wait()
+    wait_all(row_ops)
+
+    @pl.loop(0, 3)
+    def _(i):
+        mr[after(i, 192), :] += tdot(gv[c, :, chunk(i)], dzv[...]) + rr[after(i, 192), :]
+
+    mr[0:192, :] += tdot(ov[c], dyv[...])[64:256] + rr[0:192, :]
+    out_row = pltpu.make_async_copy(mr, mrow_ref, load_sem.at[1])
+    out_row.start()
     wait_all(dm_ops)
     dmx = dma[...].reshape(8 * n, QKV0)
     part = sum(ndot(wmod_ref[...], piece) for piece in split3(dmx))
     dss[...] = part
     dsc[t] = part
     ds_ops = net.tensor_push(dss, dsc.at[t], 32)
-    loads["re"].wait()
-    wait_all(row_ops)
-
-    @pl.loop(0, 3)
-    def _(i):
-        mr[after(i, 192), :] += tdot(gv[c, :, chunk(i)], dzv[...]) + rr[after(i, 192), :]
-
-    mr[0:192, :] += tdot(ov[c], dyv[...])[64:256] + rr[0:192, :]
-    out_row = pltpu.make_async_copy(mr, mrow_ref, load_sem.at[1])
-    out_row.start()
     right = right_ref[...]
 
     def left_part(first, last):
@@ -863,15 +894,13 @@
         return net.dp_push(lambda peer: v.at[own], v.at[own], base)
 
     ops = scatter(px, pland, P_COUNT // n, 40)
+    ops = collect(pland, py, P_COUNT // n, 48, ops)
     wait_all(ds_ops)
     dcond = (dsc[0] + dsc[1] + dsc[2] + dsc[3]) * silu_slope_k(ct_ref[...])
-    dts[...] = sum(tdot(wto_ref[...], piece) for piece in split3(dcond)).reshape(n, share, 8 * n)
+    dtime = sum(tdot(wto_ref[...], piece) for piece in split3(dcond)).reshape(n, 2, share // 2, 8 * n)
+    dts[...] = jnp.concatenate([dtime[:, 0], dtime[:, 1]], axis=2)
     dtl[w] = dts[w]
     dt_ops = net.dp_push(lambda peer: dts.at[peer], dtl.at[w], 56)
-    gsm_ref[:, 274:1042] = hndot(dcond, a1_ref[...])
-    gsm_ref[:, 1042:1043] = jnp.sum(dcond, axis=1, keepdims=True)
-    gsm_ref[:, 1043:1075] = hdot(dcond, hot_ref[...])[:, 0:CLASSES]
-    ops = collect(pland, py, P_COUNT // n, 48, ops)
     wait_all(tok_ops)
     tok = sum(tkl[k] for k in range(1, n)) + tkl[0]
     tok = jnp.concatenate([tok, jnp.zeros((88, 128), F32)], axis=0).T[0:share]
@@ -890,7 +919,9 @@
         left_ref[:, offset : offset + width] = block[:, 0:width]
         offset += width
     gb_ref[...] = jnp.concatenate([py[26 + i // 8, i % 8 : i % 8 + 1, :] for i in range(23)], axis=1)[:, 0:COLS]
-    gh_ref[...] = jnp.concatenate([py[29], py[30]], axis=0)
+    head = jnp.concatenate([py[29], py[30], jnp.zeros((112, 128), F32)], axis=0).T
+    gh_ref[...] = head[0:8]
+    emit((left_ref, left_out), (gb_ref, gb_out), (gh_ref, gh_out))
 
     col_side = fill(halves(bases[0]) + halves(bases[1]) + halves(bases[2]), 128).T.astype(BF)
 
@@ -923,8 +954,12 @@
     for i in range(35, Q_COUNT):
         qx[i] = jnp.zeros((8, 128), F32)
     ops = scatter(qx, qland, Q_COUNT // n, 64)
+    gsm_ref[:, 274:1042] = hndot(dcond, a1_ref[...])
+    gsm_ref[:, 1042:1043] = jnp.sum(dcond, axis=1, keepdims=True)
+    gsm_ref[:, 1043:1075] = hdot(dcond, hot_ref[...])[:, 0:CLASSES]
     wait_all(dt_ops)
-    dtime = (sum(dtl[k] for k in range(1, n)) + dtl[0]) * silu_slope_k(t1_ref[...])
+    dtime = sum(dtl[k] for k in range(1, n)) + dtl[0]
+    dtime = jnp.concatenate([dtime[:, 0:64], dtime[:, 64:128]], axis=0) * silu_slope_k(t1_ref[...])
     gsm_ref[:, 17:273] = hdot(dtime, tf_ref[...])
     gsm_ref[:, 273:274] = jnp.sum(dtime, axis=1, keepdims=True)
 
@@ -949,6 +984,7 @@
     pc_ref[...] = row_stack.astype(BF)
     row_stack = jnp.concatenate([row_stack, jnp.zeros((128, 64), F32)], axis=1)
     psr_ref[...] = row_stack.T[0:960].astype(BF)
+    emit((pst_ref, pst_out), (pc_ref, pc_out), (psr_ref, psr_out), (gsm_ref, gsm_out))
     ops = collect(qland, qy, Q_COUNT // n, 72, ops)
     wait_all(ops)
     qkv = jnp.concatenate([qy[12 + i] for i in range(5)], axis=1)[:, 0:576]
@@ -967,7 +1003,10 @@
     rightn_ref[:, 0:COLS] = qc[:, 0:COLS]
     rightn_ref[:, COLS : COLS + D] = qr[0]
     rightn_ref[:, COLS + D : COLS + 2 * D] = qr[1]
+    emit((qst_ref, qst_out), (qsn_ref, qsn_out), (qrs_ref, qrs_out), (rightn_ref, rightn_out))
     net.finish()
+    for op in outs:
+        op.wait()
     out_col.wait()
     out_row.wait()
 
@@ -983,25 +1022,26 @@
     outs = [
         S((COLS, D), F32), S((960, D), F32), S((8, 3264), F32), S((8, 4416), F32),
         S((128, D), BF), S((960, 128), BF), S((128, 960), BF), S((COLS, 128), BF), S((128, 2944), BF), S((128, D), BF),
-        S((1, COLS), F32), S((16, 128), F32), S((share, 1093), F32),
+        S((1, COLS), F32), S((8, 128), F32), S((share, 1093), F32),
     ]
     scratch = [
         V((COLS, D), F32), V((960, D), F32), V((1344, D), F32), V((960, D), F32), V((1344, D), F32), V((960, D), F32),
         V((rows, D), BF), V((rows, D), BF), V((rows, D), BF), V((rows, D), BF),
         V((2, rows, 256), BF), V((2, rows, 640), BF), V((2, rows, D), BF), V((2, rows, D), BF),
+        *[V(o.shape, o.dtype) for o in outs[2:]],
         V((4, 8, D), F32), V((40, D), F32), V((1, 640), F32), V((1, D), F32), V((16, 128), F32),
         V((8, QKV0), F32), V((n, 8, QKV0), F32),
-        V((4, share, lat), F32), V((share, lat), F32), V((n, share, lat), F32), V((n, share, lat), F32),
+        V((4, share, lat), F32), V((share, lat), F32), V((n, share // 2, 128), F32), V((n, share // 2, 128), F32),
         V((n, 40, 128), F32), V((n, 40, 128), F32),
         V((P_COUNT, 8, 128), F32), V((n, P_COUNT // n, 8, 128), F32), V((P_COUNT, 8, 128), F32),
         V((Q_COUNT, 8, 128), F32), V((n, Q_COUNT // n, 8, 128), F32), V((Q_COUNT, 8, 128), F32),
-        pltpu.SemaphoreType.DMA((10,)), pltpu.SemaphoreType.DMA((80,)), pltpu.SemaphoreType.DMA((80,)),
+        pltpu.SemaphoreType.DMA((10,)), pltpu.SemaphoreType.DMA((11,)), pltpu.SemaphoreType.DMA((80,)), pltpu.SemaphoreType.DMA((80,)),
     ]
     return pl.pallas_call(
         grad_kernel,
         out_shape=outs,
         in_specs=[any_spec] * 10 + [vm] * 14,
-        out_specs=[any_spec] * 2 + [vm] * 11,
+        out_specs=[any_spec] * 13,
         scratch_shapes=scratch,
         compiler_params=pltpu.CompilerParams(collective_id=1, has_side_effects=True, vmem_limit_bytes=60 * 1024 * 1024),
         name="grad",
@@ -1009,28 +1049,40 @@
 
 
 def apply_kernel(
-    w_ref, mcol_ref, mrow_ref, qst_ref, psr_ref, pst_ref, pc_ref, qsn_ref, qrs_ref,
-    cw_ref, cm_ref, rw_ref, rm_ref, gs_ref, sw_ref, sm_ref,
-    cres_ref, rres_ref, cn_ref, cmn_ref, rn_ref, rmn_ref, sn_ref, smn_ref, *, n
+    w_ref, mcol_ref, mrow_ref, qst_ref, psr_ref, pst_ref, pc_ref, qsn_ref, qrs_ref, left_ref, right_ref, gs_ref, gb_ref, gh_ref,
+    cw_ref, cm_ref, rw_ref, rm_ref, sw_ref, sm_ref, bw_ref, bm_ref, hw_ref, hm_ref,
+    cres_ref, rres_ref, cn_ref, cmn_ref, rn_ref, rmn_ref, sn_ref, smn_ref, bn_ref, bmn_ref, hn_ref, hmn_ref,
+    left_out, right_out, loss_ref, hat_s, *, n
 ):
     step = pl.program_id(0)
     share = D // n
-    cres_ref[...] = mcol_ref[...] - dot(qst_ref[...], pst_ref[...]) * (1.0 / n)
-    rres_ref[...] = mrow_ref[...] - dot(psr_ref[...], qrs_ref[...]) * (1.0 / n)
+    per = share // 8
+
+    def update(weight, moment, grad):
+        moment = DECAY * moment + grad
+        return weight - LEARN_RATE * moment, moment
 
     @pl.when(step == 0)
     def _():
         place = lax.broadcasted_iota(jnp.int32, (D, 128), 0) == w_ref[0] * share + lax.broadcasted_iota(jnp.int32, (D, 128), 1)
         pick = jnp.where(place, 1.0, 0.0).astype(BF)
-        mom = DECAY * cm_ref[...] + tdot(dot(pst_ref[...], pick).astype(BF), qsn_ref[...])[0:share, 0:COLS]
-        cmn_ref[...] = mom
-        cn_ref[...] = cw_ref[...] - LEARN_RATE * mom
-        mom = DECAY * rm_ref[...] + tdot(dot(qrs_ref[...], pick).astype(BF), pc_ref[...])[0:share]
-        rmn_ref[...] = mom
-        rn_ref[...] = rw_ref[...] - LEARN_RATE * mom
-        mom = DECAY * sm_ref[...] + gs_ref[...]
-        smn_ref[...] = mom
-        sn_ref[...] = sw_ref[...] - LEARN_RATE * mom
+        hat_s[...] = tdot(dot(pst_ref[...], pick).astype(BF), qsn_ref[...])[0:share, 0:COLS]
+        rows = tdot(dot(qrs_ref[...], pick).astype(BF), pc_ref[...])[0:share]
+        rn_ref[...], rmn_ref[...] = update(rw_ref[...], rm_ref[...], rows)
+
+    @pl.when(step == 1)
+    def _():
+        sn_ref[...], smn_ref[...] = update(sw_ref[...], sm_ref[...], gs_ref[...])
+        bn_ref[...], bmn_ref[...] = update(bw_ref[...], bm_ref[...], gb_ref[...])
+        hn_ref[...], hmn_ref[...] = update(hw_ref[...], hm_ref[...], gh_ref[0:1, 0:PATCH_IN])
+        loss_ref[...] = gh_ref[1:2, 0:1]
+        left_out[...] = left_ref[...]
+        right_out[...] = right_ref[...]
+
+    cres_ref[...] = mcol_ref[...] - dot(qst_ref[...], pst_ref[...]) * (1.0 / n)
+    rres_ref[...] = mrow_ref[...] - dot(psr_ref[...], qrs_ref[...]) * (1.0 / n)
+    for r in range(per):
+        cn_ref[r], cmn_ref[r] = update(cw_ref[r], cm_ref[r], hat_s[pl.ds(per * step + r, 1), :])
 
 
 def run_apply(w, operands, n):
@@ -1038,17 +1090,22 @@
     S = jax.ShapeDtypeStruct
     blk = lambda r, cc: pl.BlockSpec((r, cc), lambda i, *_: (i, 0))
     full = lambda r, cc: pl.BlockSpec((r, cc), lambda i, *_: (0, 0))
-    cb, rb, sb = full(share, COLS), full(share, 960), full(share, 1093)
+    cb = pl.BlockSpec((share // 8, 1, COLS), lambda i, *_: (i, 0, 0))
+    rb, sb, bb, hb = full(share, 960), full(share, 1093), full(1, COLS), full(1, PATCH_IN)
+    left, right = full(8, 3264), full(8, 4416)
     return pl.pallas_call(
         functools.partial(apply_kernel, n=n),
         grid_spec=pltpu.PrefetchScalarGridSpec(
             num_scalar_prefetch=1,
             grid=(8,),
             in_specs=[blk(360, D), blk(120, D), blk(360, 128), blk(120, 128), full(128, D), full(128, 960), full(128, 2944), full(128, D)]
-            + [cb, cb, rb, rb, sb, sb, sb],
-            out_specs=[blk(360, D), blk(120, D), cb, cb, rb, rb, sb, sb],
+            + [left, right, sb, bb, full(8, 128), cb, cb, rb, rb, sb, sb, bb, bb, hb, hb],
+            out_specs=[blk(360, D), blk(120, D), cb, cb, rb, rb, sb, sb, bb, bb, hb, hb, left, right, full(1, 1)],
+            scratch_shapes=[pltpu.VMEM((share, COLS), F32)],
         ),
-        out_shape=[S((COLS, D), F32), S((960, D), F32)] + [S((share, v), F32) for v in (COLS, COLS, 960, 960, 1093, 1093)],
+        out_shape=[S((COLS, D), F32), S((960, D), F32)]
+        + [S(v, F32) for v in [(share, 1, COLS)] * 2 + [(share, 960)] * 2 + [(share, 1093)] * 2 + [(1, COLS)] * 2 + [(1, PATCH_IN)] * 2]
+        + [S(v, F32) for v in ((8, 3264), (8, 4416), (1, 1))],
         compiler_params=pltpu.CompilerParams(vmem_limit_bytes=48 * 1024 * 1024),
         name="apply",
     )(w, *operands)
@@ -1402,24 +1459,19 @@
     mcol, mrow, left_all, right_sum, pst, psr, pc, qst, qsn, qrs, gb, gh, gsm = run_grad(
         acts + errors + [dmod, small, dbq, db1, hb, right_factors[0], cs, ct, t1, a1, tf, hot, wmod, wto], data_size
     )
-    cres, rres, cn, cmn, rn, rmn, sn, smn = run_apply(
+    cres, rres, col_new, col_momentum, rn, rmn, sn, smn, bias_new, bias_momentum, hn, hmn, left_all, right_sum, loss = run_apply(
         data_rank.reshape(1),
-        [mcol, mrow, qst, psr, pst, pc, qsn, qrs, col, col_moments[:, 0], row_weights[0].T, row_moments[0].T]
-        + [gsm, small_t, small_moments.T],
+        [mcol, mrow, qst, psr, pst, pc, qsn, qrs, left_all, right_sum, gsm, gb, gh]
+        + [col_weights, col_moments, row_weights[0].T, row_moments[0].T, small_t, small_moments.T]
+        + [bias_weights, bias_moments, head_bias[None], head_moments[None]],
         data_size,
     )
-    col_new, col_momentum, col_residue = cn[:, None], cmn[:, None], cres.T[None, None]
-    row_new, row_momentum, row_residue = rn.T[None], rmn.T[None], rres[None, None]
+    loss_value = loss[0, 0]
+    col_residue, row_residue = cres.T[None, None], rres[None, None]
+    row_new, row_momentum = rn.T[None], rmn.T[None]
     small_new, small_momentum = sn.T, smn.T
-    bias_sum = gb[0]
-    head_sum = gh[:, 0]
-    loss_value = gh[0, 1]
-    bias_momentum = DECAY * bias_moments + bias_sum[None]
-    bias_new = bias_weights - LEARN_RATE * bias_momentum
-    head_momentum = DECAY * head_moments + head_sum
-    head_new = head_bias - LEARN_RATE * head_momentum
-    left_factors = left_all[None]
-    right_new = right_sum[None]
+    head_new, head_momentum = hn[0], hmn[0]
+    left_factors, right_new = left_all[None], right_sum[None]
     return (
         loss_value,
         col_new,

time: 265 us -> 236 us (0.89)
  Pallas kernels: 242 us -> 216 us
  local copies, waits for them, and re-layouts: 17.8 us -> 14.5 us
    pallas_call x1, Pallas kernels: 170 us -> 146 us  [run_step(): pl.pallas_call(functools.partial(step_kernel, names=tuple(state), count_a...]
    unnamed x50 -> x45, local copies, waits for them, and re-layouts: 14.1 us -> 11.6 us
where the time goes in v5:
time: 236 us; the launch traced here: 235 us
  Pallas kernels  216 us (92%)
  local copies, waits for them, and re-layouts  14.5 us (6%)
  other arithmetic  3.52 us (1%)
    pallas_call x1, Pallas kernels, run_step(): pl.pallas_call(functools.partial(step_kernel, names=tuple(state), count_a...  146 us
    pallas_call x1, Pallas kernels, run_grad(): pl.pallas_call(grad_kernel, out_shape=outs, in_specs=[any_spec] * 10 + [v...  55.1 us
    pallas_call x1, Pallas kernels, run_apply(): pl.pallas_call(functools.partial(apply_kernel, n=n), grid_spec=pltpu.Pref...  14.1 us
    unnamed x45, local copies, waits for them, and re-layouts  11.6 us

profile of v5, /device:TPU:0, one launch (start us, length us, event | category | flops | bytes accessed | tf_op | source)
XLA Modules:
  0.0 234.9 jit_solution(5853729779872354807)
XLA Ops:
  0.7 1.3 copy.37
  2.0 1.0 bitcast_convert_fusion.1
  3.1 0.2 slice_bitcast_fusion
  3.3 0.8 pad_maximum_fusion.pack_ref
  4.3 0.7 concatenate.14.brow_ref
  4.9 0.7 slice.36.wmod_ref
  5.8 0.7 pad_maximum_fusion.1.pe_ref
  6.7 0.6 pad_maximum_fusion.2.pk_ref
  7.3 0.6 slice.39.bmod_ref
  7.9 0.7 copy.33.bh_ref
  8.6 146.5 %step.1 = (bf16[4,256,768]{2,1,0:T(8,128)(2,1)}, bf16[4,256,768]{2,1,0:T(8,128)(2,1)}, bf16[4,256,768]{2,1,0:T(8,128)(2,1)}, bf16[4,256,768]{2,1,0:T(8,128)(2,1)...) custom-call(bf16[3,96,768]{2,1,0:T(8,128)(2,1)} %pad_maximum_fusion., ...), custom_call_target="tpu_custom_call" | custom-call | tf_op jit(solution)/shard_map/step/pallas_call | solution.py:705
  155.2 55.1 %grad.1 = (f32[2880,768]{1,0:T(8,128)}, f32[960,768]{1,0:T(8,128)}, f32[8,3264]{1,0:T(8,128)}, f32[8,4416]{1,0:T(8,128)}, bf16[128,768]{1,0:T(8,128)(2,1)}, /*in...) custom-call(bf16[1024,768]{1,0:T(8,128)(2,1)} %bitcast.71, ...), custom_call_target="tpu_custom_call" | custom-call | tf_op jit(solution)/shard_map/grad/pallas_call | solution.py:1040
  210.4 1.1 copy-done.3
  211.5 1.1 copy-done.4
  212.6 1.0 copy-done.6
  213.6 0.9 copy-done.8
  214.6 0.9 copy-done.9
  215.5 0.9 copy-done.10
  216.5 0.9 copy-done.11
  217.4 0.9 copy-done.12
  218.3 0.9 copy-done.13
  219.2 0.7 copy-done.16
  219.9 0.7 copy-done.17
  220.6 14.1 %apply.1 = (f32[2880,768]{1,0:T(8,128)}, f32[960,768]{1,0:T(8,128)}, f32[96,1,2880]{2,1,0:T(1,128)}, f32[96,1,2880]{2,1,0:T(1,128)}, f32[96,960]{1,0:T(8,128)}, ...) custom-call(s32[1]{0:T(128)} %bitcast.w_ref, ...), custom_call_target="tpu_custom_call" | custom-call | tf_op jit(solution)/shard_map/apply/pallas_call | solution.py:1096
  (48 shorter events, 0.6 us)
Async XLA Ops:
  0.6 3.5 %copy-start.14 = (f32[1,2880]{1,0:T(1,128)S(1)}, f32[1,2880]{1,0:T(1,128)}, u32[]{:S(2)}) copy-start(f32[1,2880]{1,0:T(1,128)} %bw_ref.1) | copy-start | bytes 34564
  0.7 5.8 %copy-start.20 = (f32[8]{0:T(128)S(1)}, f32[8]{0:T(128)}, u32[]{:S(2)}) copy-start(f32[8]{0:T(128)} %times_ref.1) | copy-start | bytes 100
  0.7 5.9 %copy-start.21 = (s32[8]{0:T(128)S(1)}, s32[8]{0:T(128)}, u32[]{:S(2)}) copy-start(s32[8]{0:T(128)} %param.20) | copy-start | bytes 100
  0.7 7.2 %copy-start.18 = (f32[16]{0:T(128)S(1)}, f32[16]{0:T(128)}, u32[]{:S(2)}) copy-start(f32[16]{0:T(128)} %param.31) | copy-start | bytes 196
  155.1 55.2 %copy-start = (f32[96,1,2880]{2,1,0:T(1,128)S(1)}, f32[96,1,2880]{2,1,0:T(1,128)}, u32[]{:S(2)}) copy-start(f32[96,1,2880]{2,1,0:T(1,128)} %cw_ref.1) | copy-start | bytes 3317764
  155.1 55.2 %copy-start.1 = (f32[1093,96]{0,1:T(8,128)S(1)}, f32[1093,96]{0,1:T(8,128)}, u32[]{:S(2)}) copy-start(f32[1093,96]{0,1:T(8,128)} %param.29) | copy-start | bytes 1259140
  155.1 55.2 %copy-start.2 = (f32[1,960,96]{1,2,0:T(8,128)S(1)}, f32[1,960,96]{1,2,0:T(8,128)}, u32[]{:S(2)}) copy-start(f32[1,960,96]{1,2,0:T(8,128)} %param.24) | copy-start | bytes 1105924
  155.1 55.2 %copy-start.5 = (f32[1093,96]{0,1:T(8,128)S(1)}, f32[1093,96]{0,1:T(8,128)}, u32[]{:S(2)}) copy-start(f32[1093,96]{0,1:T(8,128)} %param.30) | copy-start | bytes 1259140
  155.1 55.2 %copy-start.7 = (f32[1,960,96]{1,2,0:T(8,128)S(1)}, f32[1,960,96]{1,2,0:T(8,128)}, u32[]{:S(2)}) copy-start(f32[1,960,96]{1,2,0:T(8,128)} %param.25) | copy-start | bytes 1105924
  155.1 55.2 %copy-start.15 = (f32[1,2880]{1,0:T(1,128)S(1)}, f32[1,2880]{1,0:T(1,128)}, u32[]{:S(2)}) copy-start(f32[1,2880]{1,0:T(1,128)} %bm_ref.1) | copy-start | bytes 34564
  155.1 55.2 %copy-start.19 = (f32[16]{0:T(128)S(1)}, f32[16]{0:T(128)}, u32[]{:S(2)}) copy-start(f32[16]{0:T(128)} %param.32) | copy-start | bytes 196
  210.4 1.1 copy-start.3
  211.5 1.1 copy-start.4
  212.6 1.0 copy-start.6
  213.6 0.9 copy-start.8
  214.6 0.9 copy-start.9
  215.5 0.9 copy-start.10
  216.4 0.9 copy-start.11
  217.4 0.9 copy-start.12
  218.3 0.9 copy-start.13
  219.2 0.7 copy-start.16
  219.9 0.7 copy-start.17
